TPU v7x, 128 devices: a whole 4x4x4 slice. The times are simulated.
128 devices in a mesh: attn: 8 (over x, core), ep: 16 (over y, z).
Axes of the slice: x: 4, y: 4, z: 4, core: 2. Of those that a mesh axis runs over, the one named last changes fastest.
Arguments:
- residual: bfloat16 [2, 128, 6144], P(None, ('attn', 'ep')), may hold values from -6 to 6
- query: bfloat16 [2, 128, 6144], P(None, ('attn', 'ep')), may hold values from -6 to 6
- new_key: bfloat16 [2, 128, 1024], P(None, ('attn', 'ep')), may hold values from -6 to 6
- new_value: bfloat16 [2, 128, 1024], P(None, ('attn', 'ep')), may hold values from -6 to 6
- key_cache: bfloat16 [2, 128, 512, 1024], P(None, ('attn', 'ep')), may hold values from -6 to 6
- value_cache: bfloat16 [2, 128, 512, 1024], P(None, ('attn', 'ep')), may hold values from -6 to 6
- lengths: int32 [2, 128], P(None, ('attn', 'ep')), may hold values from 2 to 512, as said below
- expert_ids: int32 [2, 128, 2], P(None, ('attn', 'ep')), may hold values from 0 to 7, all different within a row; in each aligned block of 16 rows (0 to 15, 16 to 31, ..., all dimensions but the last counted through in order) at most 6 rows name the same one
- norm_gain: float32 [6144], replicated, may hold values from 0.5 to 2
- router: bfloat16 [6144, 8], replicated, may hold values from -0.078125 to 0.078125
- w_gate: bfloat16 [16, 6144, 4096], P('ep', None, 'attn'), may hold values from -0.078125 to 0.078125
- w_up: bfloat16 [16, 6144, 4096], P('ep', None, 'attn'), may hold values from -0.078125 to 0.078125
- w_down: bfloat16 [16, 4096, 6144], P('ep', 'attn'), may hold values from -0.0625 to 0.0625
Outputs:
- mixed: bfloat16 [2, 128, 6144], P(None, ('attn', 'ep'))
Inputs may be any that keep to these rules, and one draw needn't show every extreme that they name: `expert_ids`: the two ids of a row differ. In each micro-batch, each aligned block of 16 rows (the rows of one index of attn) names one expert at most 6 times, and some block reaches 6. `lengths`: in each micro-batch some row has all 512 positions valid.
All inputs are finite; a program needn't handle non-finite values.
Results may differ from a plain program's by a relative error of at most 0.019.
Values may be sent and summed in bfloat16 or wider, within the bound.
No kernel may reach another device: no remote copies, remote signals or barrier semaphores. Data moves between devices by JAX's collectives and lax.ppermute only.
A program may use at most 128 MiB of HBM per device.

v0:
```python
import jax
import jax.numpy as jnp
from jax import lax
from jax.sharding import PartitionSpec as P

KVH = 8
CAP = 6


epsilon = 1e-05


def attend(query, new_key, new_value, key_cache, value_cache, lengths, kv_heads):
    row_total, features = query.shape
    context = key_cache.shape[1]
    head_size = new_key.shape[1] // kv_heads
    group_size = features // (kv_heads * head_size)
    score_scale = head_size ** (-0.5)
    queries = query.reshape(row_total, kv_heads, group_size, head_size)
    key_heads = key_cache.reshape(row_total, context, kv_heads, head_size)
    value_heads = value_cache.reshape(row_total, context, kv_heads, head_size)
    fresh_key = new_key.reshape(row_total, kv_heads, head_size)
    fresh_value = new_value.reshape(row_total, kv_heads, head_size)
    scores = (
        jnp.einsum("rkgd,rtkd->rkgt", queries, key_heads, preferred_element_type=jnp.float32)
        * score_scale
    )
    own_score = (
        jnp.einsum("rkgd,rkd->rkg", queries, fresh_key, preferred_element_type=jnp.float32)
        * score_scale
    )
    in_range = jnp.arange(context, dtype=jnp.int32)[None, :] < lengths[:, None]
    scores = jnp.where(in_range[:, None, None, :], scores, -jnp.inf)
    row_peak = jnp.maximum(jnp.max(scores, axis=-1), own_score)
    exp_terms = jnp.exp(scores - row_peak[..., None])
    own_exp = jnp.exp(own_score - row_peak)
    denominator = jnp.sum(exp_terms, axis=-1) + own_exp
    weights = (exp_terms / denominator[..., None]).astype(jnp.bfloat16)
    own_weight = (own_exp / denominator).astype(jnp.bfloat16)
    mixture = jnp.einsum(
        "rkgt,rtkd->rkgd", weights, value_heads, preferred_element_type=jnp.float32
    )
    mixture = (
        mixture
        + own_weight.astype(jnp.float32)[..., None] * fresh_value.astype(jnp.float32)[:, :, None, :]
    )
    return mixture.reshape(row_total, features).astype(jnp.bfloat16)


def normalize(hidden, norm_gain):
    values = hidden.astype(jnp.float32)
    mean_square = jnp.mean(values * values, axis=-1, keepdims=True)
    return (values * lax.rsqrt(mean_square + epsilon) * norm_gain).astype(jnp.bfloat16)


def slot_table(ids, expert, capacity):
    leading = ids.shape[:-2]
    row_total = ids.shape[-2]
    flat_ids = ids.reshape(leading + (row_total * 2,))
    matches = (flat_ids == expert).astype(jnp.int32)
    position = jnp.cumsum(matches, axis=-1) - matches
    slot_ids = jnp.arange(capacity, dtype=jnp.int32)
    selected = (matches[..., None, :] == 1) & (position[..., None, :] == slot_ids[:, None])
    route_row = jnp.arange(row_total * 2, dtype=jnp.int32) // 2
    partner = flat_ids.reshape(leading + (row_total, 2))[..., ::-1].reshape(
        leading + (row_total * 2,)
    )
    row_of = jnp.sum(jnp.where(selected, route_row, 0), axis=-1)
    other_of = (jnp.sum(jnp.where(selected, partner[..., None, :] + 1, 0), axis=-1) - 1).astype(
        jnp.int32
    )
    return (row_of, other_of)


def route_gate(rows, router, expert, other):
    logits = jnp.dot(rows, router, preferred_element_type=jnp.float32)
    columns = jnp.arange(router.shape[1], dtype=jnp.int32)[None, :]
    own_logit = jnp.sum(jnp.where(columns == expert, logits, 0.0), axis=1)
    other_logit = jnp.sum(jnp.where(columns == other[:, None], logits, 0.0), axis=1)
    larger = jnp.maximum(own_logit, other_logit)
    own_exp = jnp.exp(own_logit - larger)
    other_exp = jnp.exp(other_logit - larger)
    return jnp.where(other >= 0, own_exp / (own_exp + other_exp), 0.0)


def experts(normed, expert_ids, router, w_gate, w_up, w_down):
    batches, rows_here, features = normed.shape
    expert = lax.axis_index("ep") // 2
    groups = lax.axis_size("attn")
    per_group = rows_here * lax.axis_size("ep")
    batch_index = jnp.arange(batches, dtype=jnp.int32)[None, :]
    every_x, every_ids = (
        lax.all_gather(normed, ("attn", "ep"), axis=1, tiled=True),
        lax.all_gather(expert_ids, ("attn", "ep"), axis=1, tiled=True),
    )
    row_of, other_of = slot_table(every_ids.reshape(batches, groups, per_group, 2), expert, CAP)
    offsets = jnp.arange(groups, dtype=jnp.int32)[:, None] * per_group
    flat_row = (row_of + offsets).reshape(batches, groups * CAP).T
    slot_x = every_x[batch_index, flat_row]
    slot_meta = jnp.stack([flat_row, other_of.reshape(batches, groups * CAP).T], axis=-1)
    slot_count = slot_x.shape[0]
    gate_weights = route_gate(
        slot_x.reshape(slot_count * batches, features),
        router,
        expert,
        slot_meta[..., 1].reshape(-1),
    ).reshape(slot_count, batches)
    batch_column = jnp.arange(batches, dtype=jnp.int32)[None, :]
    portion_rows = slot_x.shape[0]
    flat_portion = slot_x.reshape(portion_rows * batches, features)
    gate_proj = jnp.dot(flat_portion, w_gate[0], preferred_element_type=jnp.float32)
    up_proj = jnp.dot(flat_portion, w_up[0], preferred_element_type=jnp.float32)
    activation = (jax.nn.silu(gate_proj) * up_proj).astype(jnp.bfloat16)
    outputs = (
        jnp.dot(activation, w_down[0], preferred_element_type=jnp.float32).reshape(
            portion_rows, batches, features
        )
        * gate_weights[..., None]
    )
    total_rows = per_group * groups
    targets = slot_meta[..., 0] * batches + batch_column
    summand = jax.ops.segment_sum(
        outputs.reshape(slot_count * batches, features),
        targets.reshape(-1),
        num_segments=total_rows * batches,
    ).reshape(total_rows, batches, features)
    return lax.psum_scatter(summand, ("attn", "ep"), scatter_dimension=0, tiled=True)


def shards(
    residual,
    query,
    new_key,
    new_value,
    key_cache,
    value_cache,
    lengths,
    expert_ids,
    norm_gain,
    router,
    w_gate,
    w_up,
    w_down,
):
    rows_here = residual.shape[1]
    features = residual.shape[2]

    def run_layer(first_batch, end_batch):
        batches = end_batch - first_batch

        def flatten_rows(array):
            return array[first_batch:end_batch].reshape((batches * rows_here,) + array.shape[2:])

        attended = attend(
            flatten_rows(query),
            flatten_rows(new_key),
            flatten_rows(new_value),
            flatten_rows(key_cache),
            flatten_rows(value_cache),
            flatten_rows(lengths),
            KVH,
        )
        stream = (flatten_rows(residual).astype(jnp.float32) + attended.astype(jnp.float32)).astype(
            jnp.bfloat16
        )
        normed = normalize(stream, norm_gain).reshape(batches, rows_here, features)
        expert_sum = experts(
            normed, expert_ids[first_batch:end_batch], router, w_gate, w_up, w_down
        )
        mixture = stream.reshape(batches, rows_here, features).astype(jnp.float32) + jnp.swapaxes(
            expert_sum, 0, 1
        )
        return mixture.astype(jnp.bfloat16)

    return jnp.concatenate([run_layer(0, 1), run_layer(1, 2)], axis=0)


def solution(mesh):
    in_specs = (
        P(None, ("attn", "ep"), None),
        P(None, ("attn", "ep"), None),
        P(None, ("attn", "ep"), None),
        P(None, ("attn", "ep"), None),
        P(None, ("attn", "ep"), None, None),
        P(None, ("attn", "ep"), None, None),
        P(None, ("attn", "ep")),
        P(None, ("attn", "ep"), None),
        P(),
        P(),
        P("ep", None, "attn"),
        P("ep", None, "attn"),
        P("ep", "attn", None),
    )
    out_specs = P(None, ("attn", "ep"), None)
    return jax.shard_map(shards, mesh=mesh, in_specs=in_specs, out_specs=out_specs, check_vma=False)
```

profile of v0, /device:TPU:6, one launch (start us, length us, event | category | flops | bytes accessed | tf_op | source)
XLA Modules:
  0.0 355.4 jit_solution(10907975355495747483)
XLA Ops:
  6.5 1.3 fusion.88
  7.9 0.6 iota_compare_fusion.4
  8.5 0.8 slice_convert_fusion
  9.3 1.0 slice_reduce_fusion.1
  10.3 1.7 fusion.85
  12.0 0.5 copy.90
  12.6 0.1 fusion.69
  12.7 0.3 fusion.89
  13.0 0.2 fusion.37
  13.2 2.7 fusion.86
  15.9 1.5 copy.91
  17.4 0.4 fusion.31
  17.9 0.7 iota_compare_fusion.5
  18.6 0.1 fusion.71
  18.7 0.5 copy.87
  19.3 0.3 fusion.90
  19.6 0.2 fusion.36
  19.8 0.5 copy.88
  20.4 0.4 fusion.29
  20.9 0.8 fusion.65
  23.1 0.6 multiply_convert_fusion
  23.8 0.7 all-gather.5.cloned.1.call-update
  24.8 46.3 %all_gather.12 = s32[1,128,2]{2,0,1:T(1,128)S(1)} all-gather(s32[1,1,2]{2,0,1:T(1,128)S(1)} %get-tuple-element.37), channel_id=1, replica_groups=mesh['attn'=8,'ep'=16] {'attn','ep'}, dimensions={1}, use_global_device_ids=true | all-gather | bytes 1032 | tf_op jit(solution)/shard_map/all_gather | solution.py:94
  71.1 0.2 copy.59
  71.4 45.2 %all_gather.14 = s32[1,128,2]{2,0,1:T(1,128)S(1)} all-gather(s32[1,1,2]{2,0,1:T(1,128)S(1)} %get-tuple-element.38), channel_id=1, replica_groups=mesh['attn'=8,'ep'=16] {'attn','ep'}, dimensions={1}, use_global_device_ids=true | all-gather | bytes 1032 | tf_op jit(solution)/shard_map/all_gather | solution.py:94
  116.6 0.2 copy.71
  116.9 0.4 fusion.48
  117.3 0.1 reshape.787
  117.5 0.2 reduce_window_sum.18
  117.7 0.2 reduce_window_sum.17
  117.9 0.5 select_reduce_fusion.2
  119.4 2.5 reshape.832
  121.9 2.7 gather_fusion.1
  124.6 0.3 fusion.91
  124.9 4.0 %fusion.6 = f32[48,512]{1,0:T(8,128)S(1)} fusion(bf16[48,6144]{1,0:T(8,128)(2,1)S(1)} %gather_fusion.1, bf16[1,6144,512]{2,1,0:T(8,128)(2,1)} %param.23), kind=kOutput, calls=%fused_computation.12 | convolution fusion | flops 301989888 | bytes 6979584 | tf_op jit(solution)/shard_map/dot_general | solution.py:111
  128.8 24.2 %all-gather.5.cloned.1.call-done = bf16[786432]{0:T(1024)(128)(2,1)} async-done(((bf16[6144]{0:T(1024)(128)(2,1)}), bf16[786432]{0:T(1024)(128)(2,1)}) %all-gather.5.cloned.1.call-update) | async-done | bytes 1572880 | tf_op jit(solution)/shard_map/all_gather | solution.py:93
  153.0 2.5 reshape.831
  155.5 2.7 gather_fusion
  158.3 4.2 %fusion.8 = f32[48,512]{1,0:T(8,128)S(1)} fusion(bf16[48,6144]{1,0:T(8,128)(2,1)S(1)} %gather_fusion, bf16[1,6144,512]{2,1,0:T(8,128)(2,1)} %param.23), kind=kOutput, calls=%fused_computation.14 | convolution fusion | flops 301989888 | bytes 6979584 | tf_op jit(solution)/shard_map/dot_general | solution.py:111
  162.4 0.3 select_reduce_fusion.7
  162.7 8.0 %convolution_multiply_fusion = f32[48,6144]{1,0:T(8,128)} fusion(bf16[1,512,6144]{2,1,0:T(8,128)(2,1)} %param.25, f32[48]{0:T(128)S(1)} %compare_select_fusion.2, bf16[48,6144]{1,0:T(8,128)(2,1)S(1)} %gather_fusion.1, bf16[1,6144,512]{2,1,0:T(8,128)(2,1)} %param.24, f32[48,512]{1,0:T(8,128)S(1)} %fusion.6), kind=kOutput, calls=%fused_computation.4 | convolution fusion | flops 604422144 | bytes 14450880 | tf_op jit(solution)/shard_map/dot_general | solution.py:115
  170.7 3.7 %scatter_custom_fusion.1 = f32[128,6144]{1,0:T(8,128)S(1)} fusion(s32[48]{0:T(128)S(1)} %get-tuple-element.40, f32[48,6144]{1,0:T(8,128)} %convolution_multiply_fusion, f32[]{:T(128)} %constant.61.clone.1), kind=kCustom, calls=%fused_computation.16 | custom fusion | flops 294912 | bytes 3146240 | tf_op jit(solution)/shard_map/scatter-add | solution.py:122
  174.4 4.9 %copy.74 = f32[128,1,6144]{2,1,0:T(1,128)} copy(f32[128,1,6144]{2,0,1:T(8,128)S(1)} %bitcast.126) | data formatting | bytes 6291456 | tf_op jit(solution)/shard_map/reshape | solution.py:126
  179.3 7.1 %convolution_multiply_fusion.1 = f32[48,6144]{1,0:T(8,128)S(1)} fusion(bf16[1,512,6144]{2,1,0:T(8,128)(2,1)} %param.25, f32[48]{0:T(128)S(1)} %compare_select_fusion.3, bf16[48,6144]{1,0:T(8,128)(2,1)} %copy-done.1, bf16[1,6144,512]{2,1,0:T(8,128)(2,1)} %param.24, f32[48,512]{1,0:T(8,128)S(1)} %fusion.8), kind=kOutput, calls=%fused_computation.5 | convolution fusion | flops 604422144 | bytes 14450880 | tf_op jit(solution)/shard_map/dot_general | solution.py:115
  186.5 3.7 %scatter_custom_fusion = f32[128,6144]{1,0:T(8,128)} fusion(s32[48]{0:T(128)S(1)} %get-tuple-element.39, f32[48,6144]{1,0:T(8,128)S(1)} %convolution_multiply_fusion.1, f32[]{:T(128)} %constant.61.clone.1), kind=kCustom, calls=%fused_computation.18 | custom fusion | flops 294912 | bytes 3145732 | tf_op jit(solution)/shard_map/scatter-add | solution.py:122
  190.3 156.8 %all-reduce.7.cloned.1.call-done = (f32[128,1,6144]{2,1,0:T(1,128)}, f32[128,1,6144]{2,0,1:T(8,128)}) async-done(((f32[128,1,6144]{2,1,0:T(1,128)}, f32[128,1,6144]{2,0,1:T(8,128)}), (f32[128,1,6144]{2,1,0:T(1,128)}, f32[128,1,6144]{2,0,1:T(8,128)})) %all-reduce.7.cloned.1.call-update) | async-done | bytes 6291472
  347.1 1.0 fusion.58
  348.2 0.6 copy.75
  (70 shorter events, 2.0 us)
Async XLA Ops:
  6.5 118.1 %copy-start = (bf16[6144,8]{0,1:T(8,128)(2,1)S(1)}, bf16[6144,8]{0,1:T(8,128)(2,1)}, u32[]{:S(2)}) copy-start(bf16[6144,8]{0,1:T(8,128)(2,1)} %param.22) | copy-start | bytes 294916
  6.5 112.8 %all-gather.7.cloned.1.call-start = ((), (), s32[]{:S(2)}) async-start(), calls=%async_computation.1 | async-start | bytes 1585152 | tf_op jit(solution)/shard_map/all_gather | solution.py:93
  10.3 2.3 copy-start.5
  18.7 2.1 copy-start.2
  18.7 4.4 %copy-start.3 = (f32[6144]{0:T(1024)S(1)}, f32[6144]{0:T(1024)}, u32[]{:S(2)}) copy-start(f32[6144]{0:T(1024)} %param.21) | copy-start | bytes 73732
  19.3 5.5 %copy-start.4 = (s32[2,1,2]{2,1,0:T(1,128)S(1)}, s32[2,1,2]{2,1,0:T(1,128)}, u32[]{:S(2)}) copy-start(s32[2,1,2]{2,1,0:T(1,128)} %param.20) | copy-start | bytes 52
  23.8 129.3 %all-gather.5.cloned.1.call-start = ((), (), s32[]{:S(2)}) async-start(), calls=%async_computation | async-start | bytes 1585152 | tf_op jit(solution)/shard_map/all_gather | solution.py:93
  24.5 322.6 %all-reduce.7.cloned.1.call-start = ((), (), s32[]{:S(2)}) async-start(), calls=%async_computation.2 | async-start | bytes 12582912
  158.3 4.2 %copy-start.1 = (bf16[48,6144]{1,0:T(8,128)(2,1)}, bf16[48,6144]{1,0:T(8,128)(2,1)S(1)}, u32[]{:S(2)}) copy-start(bf16[48,6144]{1,0:T(8,128)(2,1)S(1)} %gather_fusion) | copy-start | bytes 1769476
Sparse Core Ops, SparseCore 0:
  23.9 64.6 all-gather.6
  91.4 61.5 all-gather.4
  190.4 156.7 all-reduce.6
where the time goes:
time: 358 us; the launch traced here: 355 us
  waiting for transfers between devices  182 us (51%)
  blocking collectives  91.5 us (26%)
  local copies, waits for them, and re-layouts  27.8 us (8%)
  matrix products  25.5 us (7%)
  between operations  15 us (4%)
  other arithmetic  13.8 us (4%)
    unnamed x4, waiting for transfers between devices  158 us
    all_gather x2, blocking collectives, experts(): lax.all_gather(expert_ids, ('attn', 'ep'), axis=1, tiled=True)  91.5 us
    all_gather x2, waiting for transfers between devices, experts(): lax.all_gather(normed, ('attn', 'ep'), axis=1, tiled=True)  24.2 us
    dot_general x2, matrix products, experts(): jnp.dot(activation, w_down[0], preferred_element_type=jnp.float32)  15.1 us
    dot_general x2, matrix products, experts(): jnp.dot(flat_portion, w_gate[0], preferred_element_type=jnp.float32)  8.14 us
    scatter-add x2, other arithmetic, experts(): jax.ops.segment_sum(outputs.reshape(slot_count * batches, features), targ...  7.41 us
  transfers between devices with their start and end apart: 3, of which 2 were waited for; matrix products, arithmetic and copies ran while one was open for 4% of the time, Pallas kernels for 0%

commit v1 on v0

v1 whole, which is shorter than its diff:
```python
import functools

import jax
import jax.numpy as jnp
from jax import lax
from jax.experimental import pallas as pl
from jax.experimental.pallas import tpu as pltpu
from jax.sharding import Mesh, PartitionSpec as P

KV_HEADS = 8
HEAD = 128
CAP = 6
CORES = 2
LANES = 128
PARTS = 4
EPSILON = 1e-05

VMEM = pl.BlockSpec(memory_space=pltpu.VMEM)
SMEM = pl.BlockSpec(memory_space=pltpu.SMEM)
ANY = pl.BlockSpec(memory_space=pl.ANY)


def iota(shape, dim):
    return lax.broadcasted_iota(jnp.int32, shape, dim)


def attention_kernel(
    lengths, ids, query, residual, new_key, new_value, keys, values, gain, router,
    send, stream_out, gates_out,
    key_buf, value_buf, spread, rows, packed, sems,
):
    batches, features = query.shape
    context = keys.shape[1]
    heads = features // HEAD
    group = heads // KV_HEADS
    peers = send.shape[0] // CORES
    half = features // CORES
    piece = half // PARTS
    copies = []
    for row in range(batches):
        copies.append(
            (
                pltpu.make_async_copy(keys.at[row], key_buf.at[row], sems.at[2 * row]),
                pltpu.make_async_copy(values.at[row], value_buf.at[row], sems.at[2 * row + 1]),
            )
        )
    for pair in copies:
        for copy in pair:
            copy.start()
    rows[...] = jnp.zeros_like(rows)
    query_wide = query[...].astype(jnp.float32)
    key_wide = new_key[...].astype(jnp.float32)
    value_wide = new_value[...].astype(jnp.float32)
    spread[...] = jnp.zeros_like(spread)
    for row in range(batches):
        for head in range(heads):
            block, place = head // group, head % group
            spread[row, pl.ds(8 * block + place, 1), pl.ds(HEAD * block, HEAD)] = query_wide[
                row : row + 1, HEAD * head : HEAD * (head + 1)
            ]
    for row in range(batches):
        queries = spread[row]
        own = jnp.sum(queries * key_wide[row : row + 1], axis=1, keepdims=True) * HEAD**-0.5
        copies[row][0].wait()
        scores = (
            lax.dot_general(
                queries.astype(jnp.bfloat16),
                key_buf[row],
                (((1,), (1,)), ((), ())),
                preferred_element_type=jnp.float32,
            )
            * HEAD**-0.5
        )
        scores = jnp.where(iota(scores.shape, 1) < lengths[row], scores, -jnp.inf)
        peak = jnp.maximum(jnp.max(scores, axis=1, keepdims=True), own)
        terms = jnp.exp(scores - peak)
        own_term = jnp.exp(own - peak)
        total = jnp.sum(terms, axis=1, keepdims=True) + own_term
        weights = (terms / total).astype(jnp.bfloat16)
        own_weight = (own_term / total).astype(jnp.bfloat16).astype(jnp.float32)
        copies[row][1].wait()
        mixture = jnp.dot(weights, value_buf[row], preferred_element_type=jnp.float32)
        mixture = mixture + own_weight * value_wide[row : row + 1]
        for head in range(heads):
            block, place = head // group, head % group
            rows[row : row + 1, HEAD * head : HEAD * (head + 1)] = mixture[
                8 * block + place : 8 * block + place + 1, HEAD * block : HEAD * (block + 1)
            ]
    attended = rows[0:batches].astype(jnp.bfloat16).astype(jnp.float32)
    stream = (residual[...].astype(jnp.float32) + attended).astype(jnp.bfloat16)
    stream = stream.astype(jnp.float32)
    mean_square = jnp.sum(stream * stream, axis=1, keepdims=True) * (1.0 / features)
    normed = (stream * lax.rsqrt(mean_square + EPSILON) * gain[...]).astype(jnp.bfloat16)
    normed = normed.astype(jnp.float32)
    rows[0:batches] = normed
    logits = lax.dot_general(
        rows[...].astype(jnp.bfloat16),
        router[...],
        (((1,), (1,)), ((), ())),
        preferred_element_type=jnp.float32,
    )
    for core in range(CORES):
        for row in range(batches):
            for part in range(PARTS):
                start = core * half + part * piece
                place = row * PARTS + part
                packed[0, pl.ds(place, 1), 0:piece] = normed[row : row + 1, start : start + piece]
                packed[1, pl.ds(place, 1), 0:piece] = stream[row : row + 1, start : start + piece]
            lane = iota((PARTS, LANES), 1)
            names = jnp.where(lane == 0, ids[row, 0], jnp.where(lane == 1, ids[row, 1], 0))
            packed[0, pl.ds(row * PARTS, PARTS), piece : piece + LANES] = names.astype(jnp.float32)
        chunk = packed[0].astype(jnp.bfloat16)
        for peer in range(peers):
            send[core * peers + peer] = chunk
        stream_out[core] = packed[1, :, 0:piece].astype(jnp.bfloat16)
    for row in range(batches):
        lane = iota((1, logits.shape[1]), 1)
        own = logits[row : row + 1]
        first = jnp.sum(jnp.where(lane == ids[row, 0], own, 0.0), axis=1, keepdims=True)
        second = jnp.sum(jnp.where(lane == ids[row, 1], own, 0.0), axis=1, keepdims=True)
        larger = jnp.maximum(first, second)
        first, second = jnp.exp(first - larger), jnp.exp(second - larger)
        total = first + second
        expert = iota((PARTS, LANES), 1) // 2
        gates_out[pl.ds(row * PARTS, PARTS), :] = jnp.where(
            expert == ids[row, 0],
            first / total,
            jnp.where(expert == ids[row, 1], second / total, 0.0),
        )


def select_kernel(expert, received, chosen_out, places_out):
    count, width = received.shape
    piece = width - LANES
    slots = CORES * 2 * CAP
    here = expert[0].astype(jnp.float32)
    names = received[:, piece:].astype(jnp.float32)
    lane = iota(names.shape, 1)
    match = jnp.where((names == here) & (lane < 2), 1.0, 0.0)
    match = jnp.sum(match, axis=1, keepdims=True)
    a, b = iota((count, count), 0), iota((count, count), 1)
    span = 8 * (count // (8 * CORES))
    earlier = (a // span == b // span) & (a % 8 == b % 8) & (b < a)
    rank = jnp.dot(
        jnp.where(earlier, 1.0, 0.0).astype(jnp.bfloat16),
        jnp.broadcast_to(match, (count, LANES)).astype(jnp.bfloat16),
        preferred_element_type=jnp.float32,
    )
    r, col = iota((count, LANES), 0), iota((count, LANES), 1)
    part, batch, core = r % PARTS, (r % 8) // PARTS, r // span
    target = part * slots + core * (2 * CAP) + batch * CAP + rank.astype(jnp.int32)
    places = jnp.where((col == target) & (match > 0.5), 1.0, 0.0).astype(jnp.bfloat16)
    places_out[...] = places
    chosen = lax.dot_general(
        places,
        received[:, 0:piece],
        (((0,), (0,)), ((), ())),
        preferred_element_type=jnp.float32,
    ).astype(jnp.bfloat16).astype(jnp.float32)
    for part in range(PARTS):
        chosen_out[:, part * piece : (part + 1) * piece] = chosen[
            part * slots : (part + 1) * slots
        ].astype(jnp.bfloat16)


def expert_kernel(
    core, mine, other, w_gate, w_up, w_down, mine_out, other_out,
    gate_buf, up_buf, down_buf, sems,
):
    features, hidden = w_gate.shape
    half = features // CORES
    steps = 4
    width = half // steps
    c = core[0]
    up_copies, down_copies = [], []
    for h in range(CORES):
        base = jnp.where(c == h, 0, half)
        for s in range(steps):
            at = pl.ds(pl.multiple_of(base + s * width, width), width)
            index = 2 * (h * steps + s)
            pair = (
                pltpu.make_async_copy(w_gate.at[at], gate_buf.at[h, s], sems.at[index]),
                pltpu.make_async_copy(w_up.at[at], up_buf.at[h, s], sems.at[index + 1]),
            )
            for copy in pair:
                copy.start()
            up_copies.append(pair)
    for h in range(CORES):
        base = jnp.where(c == h, half, 0)
        for s in range(steps):
            at = pl.ds(pl.multiple_of(base + s * width, width), width)
            copy = pltpu.make_async_copy(
                w_down.at[:, at], down_buf.at[h, s], sems.at[4 * steps + h * steps + s]
            )
            copy.start()
            down_copies.append(copy)
    gate = jnp.zeros((mine.shape[0], hidden), jnp.float32)
    up = jnp.zeros((mine.shape[0], hidden), jnp.float32)
    for h, rows in enumerate((mine, other)):
        for s in range(steps):
            x = rows[:, s * width : (s + 1) * width]
            for copy in up_copies[h * steps + s]:
                copy.wait()
            gate += jnp.dot(x, gate_buf[h, s], preferred_element_type=jnp.float32)
            up += jnp.dot(x, up_buf[h, s], preferred_element_type=jnp.float32)
    act = (gate * (1.0 / (1.0 + jnp.exp(-gate))) * up).astype(jnp.bfloat16)
    for h, out in enumerate((other_out, mine_out)):
        for s in range(steps):
            down_copies[h * steps + s].wait()
            out[:, s * width : (s + 1) * width] = jnp.dot(
                act, down_buf[h, s], preferred_element_type=jnp.float32
            ).astype(jnp.bfloat16)


def spread_kernel(places, own, first, second, third, send):
    slots, width = own.shape
    piece = width // PARTS
    total = own[...].astype(jnp.float32) + first[...].astype(jnp.float32)
    total = total + second[...].astype(jnp.float32) + third[...].astype(jnp.float32)
    stacked = jnp.concatenate(
        [total[:, part * piece : (part + 1) * piece] for part in range(PARTS)]
        + [jnp.zeros((LANES - PARTS * slots, piece), jnp.float32)],
        axis=0,
    ).astype(jnp.bfloat16)
    send[...] = jnp.dot(places[...], stacked, preferred_element_type=jnp.float32).astype(
        jnp.bfloat16
    )


def combine_kernel(received, stream, gates, out, rows):
    peers = received.shape[0] // CORES
    piece = received.shape[2]
    half = piece * PARTS
    batches = out.shape[0]
    gate = gates[...]
    for core in range(CORES):
        total = jnp.zeros(received.shape[1:], jnp.float32)
        for peer in range(peers):
            total += received[core * peers + peer].astype(jnp.float32) * gate[:, peer : peer + 1]
        total += stream[core].astype(jnp.float32)
        for row in range(batches):
            for part in range(PARTS):
                start = core * half + part * piece
                place = row * PARTS + part
                rows[row : row + 1, start : start + piece] = total[place : place + 1]
    out[...] = rows[0:batches].astype(jnp.bfloat16)


def shards(
    residual, query, new_key, new_value, key_cache, value_cache, lengths, expert_ids,
    norm_gain, router, w_gate, w_up, w_down,
):
    batches, _, features = residual.shape
    context = key_cache.shape[2]
    kv_width = key_cache.shape[3]
    xs = lax.axis_size("x")
    peers = lax.axis_size("ep")
    half = features // CORES
    piece = half // PARTS
    slots = CORES * batches * CAP
    expert = lax.axis_index("ep") // 2
    core = lax.axis_index("core")
    f32, bf16 = jnp.float32, jnp.bfloat16
    big = pltpu.CompilerParams(vmem_limit_bytes=48 * 2**20)

    with jax.named_scope("attention"):
        send, stream, gates = pl.pallas_call(
            attention_kernel,
            out_shape=(
                jax.ShapeDtypeStruct((CORES * peers, 8, piece + LANES), bf16),
                jax.ShapeDtypeStruct((CORES, 8, piece), bf16),
                jax.ShapeDtypeStruct((8, LANES), f32),
            ),
            in_specs=[SMEM, SMEM, VMEM, VMEM, VMEM, VMEM, ANY, ANY, VMEM, VMEM],
            out_specs=(VMEM, VMEM, VMEM),
            scratch_shapes=[
                pltpu.VMEM((batches, context, kv_width), bf16),
                pltpu.VMEM((batches, context, kv_width), bf16),
                pltpu.VMEM((batches, 8 * KV_HEADS, kv_width), f32),
                pltpu.VMEM((8, features), f32),
                pltpu.VMEM((2, 8, piece + LANES), f32),
                pltpu.SemaphoreType.DMA((2 * batches,)),
            ],
            compiler_params=big,
            name="attention",
        )(
            lengths.reshape(batches),
            expert_ids.reshape(batches, 2),
            query.reshape(batches, features),
            residual.reshape(batches, features),
            new_key.reshape(batches, kv_width),
            new_value.reshape(batches, kv_width),
            key_cache.reshape(batches, context, kv_width),
            value_cache.reshape(batches, context, kv_width),
            norm_gain.reshape(1, features),
            router.T,
        )
    with jax.named_scope("rows_to_experts"):
        received = lax.all_to_all(send, ("core", "ep"), 0, 0, tiled=True)
    with jax.named_scope("select"):
        chosen, places = pl.pallas_call(
            select_kernel,
            out_shape=(
                jax.ShapeDtypeStruct((slots, half), bf16),
                jax.ShapeDtypeStruct((CORES * peers * 8, LANES), bf16),
            ),
            in_specs=[SMEM, VMEM],
            out_specs=(VMEM, VMEM),
            compiler_params=big,
            name="select",
        )(expert.reshape(1), received.reshape(CORES * peers * 8, piece + LANES))

    def along(array, step):
        return lax.ppermute(array, "x", [(i, (i + step) % xs) for i in range(xs)])

    def swap(array):
        return lax.ppermute(array, "core", [(0, 1), (1, 0)])

    with jax.named_scope("rows_along_x"):
        parts = [chosen] + [along(chosen, step) for step in range(1, xs)]
        mine = jnp.concatenate(parts, axis=0)
    with jax.named_scope("rows_between_cores"):
        other = swap(mine)
    with jax.named_scope("experts"):
        mine_sum, other_sum = pl.pallas_call(
            expert_kernel,
            out_shape=(jax.ShapeDtypeStruct(mine.shape, bf16),) * 2,
            in_specs=[SMEM, VMEM, VMEM, ANY, ANY, ANY],
            out_specs=(VMEM, VMEM),
            scratch_shapes=[
                pltpu.VMEM((2, 4, half // 4, w_gate.shape[2]), bf16),
                pltpu.VMEM((2, 4, half // 4, w_gate.shape[2]), bf16),
                pltpu.VMEM((2, 4, w_down.shape[1], half // 4), bf16),
                pltpu.SemaphoreType.DMA((24,)),
            ],
            compiler_params=big,
            name="experts",
        )(core.reshape(1), mine, other, w_gate[0], w_up[0], w_down[0])
    with jax.named_scope("sums_between_cores"):
        arrived = swap(other_sum)
        total = (mine_sum.astype(f32) + arrived.astype(f32)).astype(bf16)
    with jax.named_scope("sums_along_x"):
        total = total.reshape(xs, slots, half)
        backs = [along(total[step], xs - step) for step in range(1, xs)]
    with jax.named_scope("spread"):
        send = pl.pallas_call(
            spread_kernel,
            out_shape=jax.ShapeDtypeStruct((CORES * peers * 8, piece), bf16),
            in_specs=[VMEM] * (2 + len(backs)),
            out_specs=VMEM,
            compiler_params=big,
            name="spread",
        )(places, total[0], *backs)
    with jax.named_scope("sums_to_rows"):
        received = lax.all_to_all(
            send.reshape(CORES * peers, 8, piece), ("core", "ep"), 0, 0, tiled=True
        )
    with jax.named_scope("combine"):
        out = pl.pallas_call(
            combine_kernel,
            out_shape=jax.ShapeDtypeStruct((batches, features), bf16),
            in_specs=[VMEM, VMEM, VMEM],
            out_specs=VMEM,
            scratch_shapes=[pltpu.VMEM((8, features), f32)],
            compiler_params=big,
            name="combine",
        )(received, stream, gates)
    return out.reshape(batches, 1, features)


def solution(mesh):
    attn, ep = mesh.shape["attn"], mesh.shape["ep"]
    fine = Mesh(mesh.devices.reshape(attn // CORES, CORES, ep), ("x", "core", "ep"))
    rows = ("x", "core", "ep")
    in_specs = (
        P(None, rows, None),
        P(None, rows, None),
        P(None, rows, None),
        P(None, rows, None),
        P(None, rows, None, None),
        P(None, rows, None, None),
        P(None, rows),
        P(None, rows, None),
        P(),
        P(),
        P("ep", None, ("x", "core")),
        P("ep", None, ("x", "core")),
        P("ep", ("x", "core"), None),
    )
    return jax.shard_map(
        shards, mesh=fine, in_specs=in_specs, out_specs=P(None, rows, None), check_vma=False
    )
```

time: 358 us -> 85.4 us (0.24)
  waiting for transfers between devices: 182 us -> 30.3 us
  blocking collectives: 91.5 us -> 14.4 us
  matrix products: 25.5 us -> 0 us
  local copies, waits for them, and re-layouts: 27.8 us -> 9.08 us
  starting transfers between devices: 0.08 us -> 16.4 us
  between operations: 15 us -> 0.14 us
  other arithmetic: 13.8 us -> 0.14 us
  Pallas kernels: 0 us -> 13.1 us
    unnamed x4 -> x0, waiting for transfers between devices: 158 us -> none
    all_gather x2 -> x0, blocking collectives: 91.5 us -> none  [experts(): lax.all_gather(expert_ids, ('attn', 'ep'), axis=1, tiled=True)]
    dot_general x12 -> x0, matrix products: 25.5 us -> none  [the longest x2 15.1 us: experts(): jnp.dot(activation, w_down[0], preferred_element_type=jnp.float32)]
    all_gather x2 -> x0, waiting for transfers between devices: 24.2 us -> none  [experts(): lax.all_gather(normed, ('attn', 'ep'), axis=1, tiled=True)]
    ppermute x0 -> x8, waiting for transfers between devices: none -> 19.1 us  [the longest x6 15.2 us: along(): return lax.ppermute(array, 'x', [(i, (i + step) % xs) for i in range(xs)])]
    all_to_all x0 -> x1, blocking collectives: none -> 14.4 us  [shards(): lax.all_to_all(send.reshape(CORES * peers, 8, piece), ('core', 'ep'), 0,...]
    pallas_call x0 -> x5, Pallas kernels: none -> 13.1 us  [the longest x1 7.53 us: shards(): pl.pallas_call(expert_kernel, out_shape=(jax.ShapeDtypeStruct(mine.shape,...]
    all_to_all x0 -> x1, waiting for transfers between devices: none -> 11.3 us  [shards(): received = lax.all_to_all(send, ('core', 'ep'), 0, 0, tiled=True)]
  transfers between devices with their start and end apart: 3 -> 9, of which waited for: 2 -> 7; matrix products, arithmetic and copies ran while one was open for 4% -> 0% of each run, Pallas kernels for 0% -> 0%
where the time goes in v1:
time: 85.4 us; the launch traced here: 83.7 us
  waiting for transfers between devices  30.3 us (35%)
  starting transfers between devices  16.4 us (19%)
  blocking collectives  14.4 us (17%)
  Pallas kernels  13.1 us (15%)
  local copies, waits for them, and re-layouts  9.08 us (11%)
    ppermute x6, waiting for transfers between devices, along(): return lax.ppermute(array, 'x', [(i, (i + step) % xs) for i in range(xs)])  15.2 us
    all_to_all x1, blocking collectives, shards(): lax.all_to_all(send.reshape(CORES * peers, 8, piece), ('core', 'ep'), 0,...  14.4 us
    all_to_all x1, waiting for transfers between devices, shards(): received = lax.all_to_all(send, ('core', 'ep'), 0, 0, tiled=True)  11.3 us
    unnamed x23, local copies, waits for them, and re-layouts  9.02 us
    all_to_all x1, starting transfers between devices, shards(): received = lax.all_to_all(send, ('core', 'ep'), 0, 0, tiled=True)  8.35 us
    ppermute x6, starting transfers between devices, along(): return lax.ppermute(array, 'x', [(i, (i + step) % xs) for i in range(xs)])  7.79 us
    pallas_call x1, Pallas kernels, shards(): pl.pallas_call(expert_kernel, out_shape=(jax.ShapeDtypeStruct(mine.shape,...  7.53 us
    pallas_call x1, Pallas kernels, shards(): pl.pallas_call(attention_kernel, out_shape=(jax.ShapeDtypeStruct((CORES *...  4.01 us
  transfers between devices with their start and end apart: 9, of which 7 were waited for; matrix products, arithmetic and copies ran while one was open for 0% of the time, Pallas kernels for 0%

profile of v1, /device:TPU:6, one launch (start us, length us, event | category | flops | bytes accessed | tf_op | source)
XLA Modules:
  0.0 83.7 jit_solution(2191453030585700008)
XLA Ops:
  0.0 0.0 copy-start
  0.0 1.6 %copy-done = bf16[2,1,512,1024]{3,2,1,0:T(8,128)(2,1)S(1)} copy-done((bf16[2,1,512,1024]{3,2,1,0:T(8,128)(2,1)S(1)}, bf16[2,1,512,1024]{3,2,1,0:T(8,128)(2,1)}, u32[]{:S(2)}) %copy-start) | copy-done | bytes 2097176
  1.6 0.0 copy-start.1
  1.6 1.6 %copy-done.1 = bf16[2,1,512,1024]{3,2,1,0:T(8,128)(2,1)S(1)} copy-done((bf16[2,1,512,1024]{3,2,1,0:T(8,128)(2,1)S(1)}, bf16[2,1,512,1024]{3,2,1,0:T(8,128)(2,1)}, u32[]{:S(2)}) %copy-start.1) | copy-done | bytes 2097176
  3.2 0.0 copy-start.2
  3.2 0.9 %copy-done.2 = bf16[6144,8]{0,1:T(8,128)(2,1)S(1)} copy-done((bf16[6144,8]{0,1:T(8,128)(2,1)S(1)}, bf16[6144,8]{0,1:T(8,128)(2,1)}, u32[]{:S(2)}) %copy-start.2) | copy-done | bytes 98328
  4.1 0.0 copy-start.3
  4.1 0.7 copy-done.3
  4.8 0.0 copy-start.4
  4.8 0.7 copy-done.4
  5.6 0.0 copy-start.5
  5.6 0.7 copy-done.5
  6.3 0.0 copy-start.6
  6.3 0.7 copy-done.6
  7.0 0.0 copy-start.7
  7.0 0.7 copy-done.7
  7.7 0.0 copy-start.8
  7.7 0.7 copy-done.8
  8.3 0.0 copy-start.9
  8.3 0.7 copy-done.9
  9.0 4.0 %attention.1 = (bf16[32,8,896]{2,1,0:T(8,128)(2,1)}, bf16[2,8,768]{2,1,0:T(8,128)(2,1)S(1)}, f32[8,128]{1,0:T(8,128)S(1)}) custom-call(s32[2]{0:T(128)S(1)} %bitcast.29, s32[2,2]{1,0:T(2,128)S(1)} %bitcast.28, bf16[2,6144]{1,0:T(2,128)(2,1)S(1)} %bitcast.23, bf16[2,6144]{1,0:T(2,128)(2,1)S(1)} %bitcast.24, bf16[2,1024]{1,0:T(2,128)(2,1)S(1)} %bitcast.26, ...), custom_call_target="tpu_custom_call" | custom-call | tf_op jit(solution)/shard_map/attention/attention/pallas_call | solution.py:267
  13.0 8.3 %all-to-all-start = ((bf16[32,8,896]{2,1,0:T(8,128)(2,1)}), bf16[32,8,896]{2,1,0:T(8,128)(2,1)S(1)}, u32[]{:S(2)}, u32[]{:S(2)}) async-start(bf16[32,8,896]{2,1,0:T(8,128)(2,1)} %get-tuple-element.12), calls=%async_computation | async-start | bytes 917504 | tf_op jit(solution)/shard_map/rows_to_experts/all_to_all | solution.py:299
  21.4 11.3 %all-to-all-done = bf16[32,8,896]{2,1,0:T(8,128)(2,1)S(1)} async-done(((bf16[32,8,896]{2,1,0:T(8,128)(2,1)}), bf16[32,8,896]{2,1,0:T(8,128)(2,1)S(1)}, u32[]{:S(2)}, u32[]{:S(2)}) %all-to-all-start) | async-done | bytes 458784 | tf_op jit(solution)/shard_map/rows_to_experts/all_to_all | solution.py:299
  32.7 0.5 select.5
  33.2 0.9 %collective-permute-start.2 = (bf16[24,3072]{1,0:T(8,128)(2,1)S(1)}, bf16[24,3072]{1,0:T(8,128)(2,1)S(1)}, u32[]{:S(2)}, u32[]{:S(2)}) collective-permute-start(bf16[24,3072]{1,0:T(8,128)(2,1)S(1)} %get-tuple-element.14), channel_id=1, source_target_pairs={{0,96},{32,0},{64,32},{96,64},{1,97},{33,1},{65,33},{97,65},{2,98}... | collective-permute-start | bytes 442376 | tf_op jit(solution)/shard_map/rows_along_x/ppermute | solution.py:314
  34.1 1.1 %collective-permute-start.1 = (bf16[24,3072]{1,0:T(8,128)(2,1)S(1)}, bf16[24,3072]{1,0:T(8,128)(2,1)S(1)}, u32[]{:S(2)}, u32[]{:S(2)}) collective-permute-start(bf16[24,3072]{1,0:T(8,128)(2,1)S(1)} %get-tuple-element.14), channel_id=1, source_target_pairs={{0,64},{32,96},{64,0},{96,32},{1,65},{33,97},{65,1},{97,33},{2,66}... | collective-permute-start | bytes 442376 | tf_op jit(solution)/shard_map/rows_along_x/ppermute | solution.py:314
  35.2 2.1 %collective-permute-start = (bf16[24,3072]{1,0:T(8,128)(2,1)S(1)}, bf16[24,3072]{1,0:T(8,128)(2,1)S(1)}, u32[]{:S(2)}, u32[]{:S(2)}) collective-permute-start(bf16[24,3072]{1,0:T(8,128)(2,1)S(1)} %get-tuple-element.14), channel_id=1, source_target_pairs={{0,32},{32,64},{64,96},{96,0},{1,33},{33,65},{65,97},{97,1},{2,34}... | collective-permute-start | bytes 442376 | tf_op jit(solution)/shard_map/rows_along_x/ppermute | solution.py:314
  37.3 6.2 %collective-permute-done = bf16[24,3072]{1,0:T(8,128)(2,1)S(1)} collective-permute-done((bf16[24,3072]{1,0:T(8,128)(2,1)S(1)}, bf16[24,3072]{1,0:T(8,128)(2,1)S(1)}, u32[]{:S(2)}, u32[]{:S(2)}) %collective-permute-start) | collective-permute-done | bytes 147488 | tf_op jit(solution)/shard_map/rows_along_x/ppermute | solution.py:314
  43.5 0.0 collective-permute-done.1
  43.5 0.0 collective-permute-done.2
  43.6 0.1 collective-permute-start.3
  43.7 2.0 %collective-permute-done.3.other = bf16[96,3072]{1,0:T(8,128)(2,1)S(1)} collective-permute-done((bf16[96,3072]{1,0:T(8,128)(2,1)S(1)}, bf16[96,3072]{1,0:T(8,128)(2,1)S(1)}, u32[]{:S(2)}, u32[]{:S(2)}) %collective-permute-start.3) | collective-permute-done | bytes 589856 | tf_op jit(solution)/shard_map/rows_between_cores/ppermute | solution.py:317
  45.7 7.5 %experts.1 = (bf16[96,3072]{1,0:T(8,128)(2,1)S(1)}, bf16[96,3072]{1,0:T(8,128)(2,1)S(1)}) custom-call(s32[1]{0:T(128)} %bitcast.12.core, bf16[96,3072]{1,0:T(8,128)(2,1)S(1)} %constant_dynamic-update-slice_fusion.mine, bf16[96,3072]{1,0:T(8,128)(2,1)S(1)} %collective-permute-done.3.other, bf16[6144,512]{1,0:T(8,128)(2,1)} %bitcast.30, ...), custom_call_target="tpu_custom_call" | custom-call | tf_op jit(solution)/shard_map/experts/experts/pallas_call | solution.py:325
  53.2 0.2 collective-permute-start.4
  53.4 1.9 %collective-permute-done.4 = bf16[96,3072]{1,0:T(8,128)(2,1)S(1)} collective-permute-done((bf16[96,3072]{1,0:T(8,128)(2,1)S(1)}, bf16[96,3072]{1,0:T(8,128)(2,1)S(1)}, u32[]{:S(2)}, u32[]{:S(2)}) %collective-permute-start.4) | collective-permute-done | bytes 589856 | tf_op jit(solution)/shard_map/sums_between_cores/ppermute | solution.py:317
  55.3 0.1 add_convert_fusion
  55.5 2.7 %collective-permute-start.7 = (bf16[24,3072]{1,0:T(8,128)(2,1)S(1)}, bf16[24,3072]{1,0:T(8,128)(2,1)S(1)}, u32[]{:S(2)}, u32[]{:S(2)}) collective-permute-start(bf16[24,3072]{1,0:T(8,128)(2,1)S(1)} %get-tuple-element.19), channel_id=1, source_target_pairs={{0,32},{32,64},{64,96},{96,0},{1,33},{33,65},{65,97},{97,1},{2,34}... | collective-permute-start | bytes 442376 | tf_op jit(solution)/shard_map/sums_along_x/ppermute | solution.py:314
  58.2 0.2 collective-permute-start.6
  58.4 0.8 collective-permute-start.5
  59.2 5.7 %collective-permute-done.7.third = bf16[24,3072]{1,0:T(8,128)(2,1)S(1)} collective-permute-done((bf16[24,3072]{1,0:T(8,128)(2,1)S(1)}, bf16[24,3072]{1,0:T(8,128)(2,1)S(1)}, u32[]{:S(2)}, u32[]{:S(2)}) %collective-permute-start.7) | collective-permute-done | bytes 147488 | tf_op jit(solution)/shard_map/sums_along_x/ppermute | solution.py:314
  64.8 1.6 %collective-permute-done.6.second = bf16[24,3072]{1,0:T(8,128)(2,1)S(1)} collective-permute-done((bf16[24,3072]{1,0:T(8,128)(2,1)S(1)}, bf16[24,3072]{1,0:T(8,128)(2,1)S(1)}, u32[]{:S(2)}, u32[]{:S(2)}) %collective-permute-start.6) | collective-permute-done | bytes 147488 | tf_op jit(solution)/shard_map/sums_along_x/ppermute | solution.py:314
  66.5 1.7 %collective-permute-done.5.first = bf16[24,3072]{1,0:T(8,128)(2,1)S(1)} collective-permute-done((bf16[24,3072]{1,0:T(8,128)(2,1)S(1)}, bf16[24,3072]{1,0:T(8,128)(2,1)S(1)}, u32[]{:S(2)}, u32[]{:S(2)}) %collective-permute-start.5) | collective-permute-done | bytes 147488 | tf_op jit(solution)/shard_map/sums_along_x/ppermute | solution.py:314
  68.2 0.3 spread.1
  68.5 14.4 %all_to_all.10.received = bf16[32,8,768]{2,1,0:T(8,128)(2,1)S(1)} all-to-all(bf16[32,8,768]{2,1,0:T(8,128)(2,1)S(1)} %bitcast.21), channel_id=1, replica_groups=mesh['x'=4,'core'=2,'ep'=16] {'core','ep'}, dimensions={0} | all-to-all | bytes 786432 | tf_op jit(solution)/shard_map/sums_to_rows/all_to_all | solution.py:355
  82.9 0.8 combine.1
  (5 shorter events, 0.1 us)
Async XLA Ops:
  0.0 1.6 %copy-start = (bf16[2,1,512,1024]{3,2,1,0:T(8,128)(2,1)S(1)}, bf16[2,1,512,1024]{3,2,1,0:T(8,128)(2,1)}, u32[]{:S(2)}) copy-start(bf16[2,1,512,1024]{3,2,1,0:T(8,128)(2,1)} %param.17) | copy-start | bytes 6291460
  1.6 1.6 %copy-start.1 = (bf16[2,1,512,1024]{3,2,1,0:T(8,128)(2,1)S(1)}, bf16[2,1,512,1024]{3,2,1,0:T(8,128)(2,1)}, u32[]{:S(2)}) copy-start(bf16[2,1,512,1024]{3,2,1,0:T(8,128)(2,1)} %param.18) | copy-start | bytes 6291460
  3.2 0.9 %copy-start.2 = (bf16[6144,8]{0,1:T(8,128)(2,1)S(1)}, bf16[6144,8]{0,1:T(8,128)(2,1)}, u32[]{:S(2)}) copy-start(bf16[6144,8]{0,1:T(8,128)(2,1)} %param.22) | copy-start | bytes 294916
  4.1 0.7 copy-start.3
  4.8 0.7 copy-start.4
  5.6 0.7 copy-start.5
  6.3 0.7 copy-start.6
  7.0 0.7 copy-start.7
  7.7 0.7 copy-start.8
  8.3 0.7 copy-start.9
  13.0 19.6 %all-to-all-start = ((bf16[32,8,896]{2,1,0:T(8,128)(2,1)}), bf16[32,8,896]{2,1,0:T(8,128)(2,1)S(1)}, u32[]{:S(2)}, u32[]{:S(2)}) async-start(bf16[32,8,896]{2,1,0:T(8,128)(2,1)} %get-tuple-element.12), calls=%async_computation | async-start | bytes 917504 | tf_op jit(solution)/shard_map/rows_to_experts/all_to_all | solution.py:299
  33.2 10.3 %collective-permute-start.2 = (bf16[24,3072]{1,0:T(8,128)(2,1)S(1)}, bf16[24,3072]{1,0:T(8,128)(2,1)S(1)}, u32[]{:S(2)}, u32[]{:S(2)}) collective-permute-start(bf16[24,3072]{1,0:T(8,128)(2,1)S(1)} %get-tuple-element.14), channel_id=1, source_target_pairs={{0,96},{32,0},{64,32},{96,64},{1,97},{33,1},{65,33},{97,65},{2,98}... | collective-permute-start | bytes 442376 | tf_op jit(solution)/shard_map/rows_along_x/ppermute | solution.py:314
  34.1 9.4 %collective-permute-start.1 = (bf16[24,3072]{1,0:T(8,128)(2,1)S(1)}, bf16[24,3072]{1,0:T(8,128)(2,1)S(1)}, u32[]{:S(2)}, u32[]{:S(2)}) collective-permute-start(bf16[24,3072]{1,0:T(8,128)(2,1)S(1)} %get-tuple-element.14), channel_id=1, source_target_pairs={{0,64},{32,96},{64,0},{96,32},{1,65},{33,97},{65,1},{97,33},{2,66}... | collective-permute-start | bytes 442376 | tf_op jit(solution)/shard_map/rows_along_x/ppermute | solution.py:314
  35.2 8.3 %collective-permute-start = (bf16[24,3072]{1,0:T(8,128)(2,1)S(1)}, bf16[24,3072]{1,0:T(8,128)(2,1)S(1)}, u32[]{:S(2)}, u32[]{:S(2)}) collective-permute-start(bf16[24,3072]{1,0:T(8,128)(2,1)S(1)} %get-tuple-element.14), channel_id=1, source_target_pairs={{0,32},{32,64},{64,96},{96,0},{1,33},{33,65},{65,97},{97,1},{2,34}... | collective-permute-start | bytes 442376 | tf_op jit(solution)/shard_map/rows_along_x/ppermute | solution.py:314
  43.6 2.1 %collective-permute-start.3 = (bf16[96,3072]{1,0:T(8,128)(2,1)S(1)}, bf16[96,3072]{1,0:T(8,128)(2,1)S(1)}, u32[]{:S(2)}, u32[]{:S(2)}) collective-permute-start(bf16[96,3072]{1,0:T(8,128)(2,1)S(1)} %constant_dynamic-update-slice_fusion.mine), channel_id=1, source_target_pairs={{0,16},{16,0},{1,17},{17,1},{2,18},{18,2},{3,19},{19,3},{4,20},{20... | collective-permute-start | bytes 1769480 | tf_op jit(solution)/shard_map/rows_between_cores/ppermute | solution.py:317
  53.2 2.1 %collective-permute-start.4 = (bf16[96,3072]{1,0:T(8,128)(2,1)S(1)}, bf16[96,3072]{1,0:T(8,128)(2,1)S(1)}, u32[]{:S(2)}, u32[]{:S(2)}) collective-permute-start(bf16[96,3072]{1,0:T(8,128)(2,1)S(1)} %get-tuple-element.16), channel_id=1, source_target_pairs={{0,16},{16,0},{1,17},{17,1},{2,18},{18,2},{3,19},{19,3},{4,20},{20... | collective-permute-start | bytes 1769480 | tf_op jit(solution)/shard_map/sums_between_cores/ppermute | solution.py:317
  55.5 9.3 %collective-permute-start.7 = (bf16[24,3072]{1,0:T(8,128)(2,1)S(1)}, bf16[24,3072]{1,0:T(8,128)(2,1)S(1)}, u32[]{:S(2)}, u32[]{:S(2)}) collective-permute-start(bf16[24,3072]{1,0:T(8,128)(2,1)S(1)} %get-tuple-element.19), channel_id=1, source_target_pairs={{0,32},{32,64},{64,96},{96,0},{1,33},{33,65},{65,97},{97,1},{2,34}... | collective-permute-start | bytes 442376 | tf_op jit(solution)/shard_map/sums_along_x/ppermute | solution.py:314
  58.2 8.2 %collective-permute-start.6 = (bf16[24,3072]{1,0:T(8,128)(2,1)S(1)}, bf16[24,3072]{1,0:T(8,128)(2,1)S(1)}, u32[]{:S(2)}, u32[]{:S(2)}) collective-permute-start(bf16[24,3072]{1,0:T(8,128)(2,1)S(1)} %get-tuple-element.20), channel_id=1, source_target_pairs={{0,64},{32,96},{64,0},{96,32},{1,65},{33,97},{65,1},{97,33},{2,66}... | collective-permute-start | bytes 442376 | tf_op jit(solution)/shard_map/sums_along_x/ppermute | solution.py:314
  58.4 9.8 %collective-permute-start.5 = (bf16[24,3072]{1,0:T(8,128)(2,1)S(1)}, bf16[24,3072]{1,0:T(8,128)(2,1)S(1)}, u32[]{:S(2)}, u32[]{:S(2)}) collective-permute-start(bf16[24,3072]{1,0:T(8,128)(2,1)S(1)} %get-tuple-element.21), channel_id=1, source_target_pairs={{0,96},{32,0},{64,32},{96,64},{1,97},{33,1},{65,33},{97,65},{2,98}... | collective-permute-start | bytes 442376 | tf_op jit(solution)/shard_map/sums_along_x/ppermute | solution.py:314

commit v2 on v1

--- a/solution.py
+++ b/solution.py
@@ -25,12 +25,12 @@
 
 
 def attention_kernel(
-    lengths, ids, query, residual, new_key, new_value, keys, values, gain, router,
-    send, stream_out, gates_out,
-    key_buf, value_buf, spread, rows, packed, sems,
+    expert, core, lengths_at, ids_at, query_at, residual_at, new_key_at, new_value_at, keys, values, gain_at,
+    router_at, send, stream_out, gates_out,
+    lengths, ids, query, residual, new_key, new_value, gain, router,
+    key_buf, value_buf, spread, rows, packed, sems, small_sems,
 ):
     batches, features = query.shape
-    context = keys.shape[1]
     heads = features // HEAD
     group = heads // KV_HEADS
     peers = send.shape[0] // CORES
@@ -44,14 +44,37 @@
                 pltpu.make_async_copy(values.at[row], value_buf.at[row], sems.at[2 * row + 1]),
             )
         )
-    for pair in copies:
+    small = [
+        pltpu.make_async_copy(source, target, small_sems.at[index])
+        for index, (source, target) in enumerate(
+            (
+                (query_at, query),
+                (new_key_at, new_key),
+                (new_value_at, new_value),
+                (residual_at, residual),
+                (gain_at, gain),
+                (router_at, router),
+                (lengths_at, lengths),
+                (ids_at, ids),
+            )
+        )
+    ]
+    for copy in small[:3]:
+        copy.start()
+    for copy in copies[0]:
+        copy.start()
+    for copy in small[3:]:
+        copy.start()
+    for pair in copies[1:]:
         for copy in pair:
             copy.start()
     rows[...] = jnp.zeros_like(rows)
+    spread[...] = jnp.zeros_like(spread)
+    for copy in small:
+        copy.wait()
     query_wide = query[...].astype(jnp.float32)
     key_wide = new_key[...].astype(jnp.float32)
     value_wide = new_value[...].astype(jnp.float32)
-    spread[...] = jnp.zeros_like(spread)
     for row in range(batches):
         for head in range(heads):
             block, place = head // group, head % group
@@ -99,10 +122,10 @@
         (((1,), (1,)), ((), ())),
         preferred_element_type=jnp.float32,
     )
-    for core in range(CORES):
+    for side in range(CORES):
         for row in range(batches):
             for part in range(PARTS):
-                start = core * half + part * piece
+                start = side * half + part * piece
                 place = row * PARTS + part
                 packed[0, pl.ds(place, 1), 0:piece] = normed[row : row + 1, start : start + piece]
                 packed[1, pl.ds(place, 1), 0:piece] = stream[row : row + 1, start : start + piece]
@@ -111,8 +134,8 @@
             packed[0, pl.ds(row * PARTS, PARTS), piece : piece + LANES] = names.astype(jnp.float32)
         chunk = packed[0].astype(jnp.bfloat16)
         for peer in range(peers):
-            send[core * peers + peer] = chunk
-        stream_out[core] = packed[1, :, 0:piece].astype(jnp.bfloat16)
+            send[side * peers + peer] = chunk
+        stream_out[side] = packed[1, :, 0:piece].astype(jnp.bfloat16)
     for row in range(batches):
         lane = iota((1, logits.shape[1]), 1)
         own = logits[row : row + 1]
@@ -163,53 +186,51 @@
         ].astype(jnp.bfloat16)
 
 
-def expert_kernel(
-    core, mine, other, w_gate, w_up, w_down, mine_out, other_out,
-    gate_buf, up_buf, down_buf, sems,
-):
-    features, hidden = w_gate.shape
-    half = features // CORES
-    steps = 4
-    width = half // steps
-    c = core[0]
-    up_copies, down_copies = [], []
-    for h in range(CORES):
-        base = jnp.where(c == h, 0, half)
-        for s in range(steps):
-            at = pl.ds(pl.multiple_of(base + s * width, width), width)
-            index = 2 * (h * steps + s)
-            pair = (
-                pltpu.make_async_copy(w_gate.at[at], gate_buf.at[h, s], sems.at[index]),
-                pltpu.make_async_copy(w_up.at[at], up_buf.at[h, s], sems.at[index + 1]),
+def fetch_kernel(after, gate_at, up_at, down_at, gate, up, down, ready, sems):
+    pieces = 4
+    copies = []
+    for source, target in ((gate_at, gate), (up_at, up), (down_at, down)):
+        rows = source.shape[0] // pieces
+        for piece in range(pieces):
+            at = pl.ds(piece * rows, rows)
+            copies.append(
+                pltpu.make_async_copy(source.at[at], target.at[at], sems.at[len(copies)])
             )
-            for copy in pair:
-                copy.start()
-            up_copies.append(pair)
-    for h in range(CORES):
-        base = jnp.where(c == h, half, 0)
-        for s in range(steps):
-            at = pl.ds(pl.multiple_of(base + s * width, width), width)
-            copy = pltpu.make_async_copy(
-                w_down.at[:, at], down_buf.at[h, s], sems.at[4 * steps + h * steps + s]
-            )
-            copy.start()
-            down_copies.append(copy)
-    gate = jnp.zeros((mine.shape[0], hidden), jnp.float32)
-    up = jnp.zeros((mine.shape[0], hidden), jnp.float32)
-    for h, rows in enumerate((mine, other)):
-        for s in range(steps):
-            x = rows[:, s * width : (s + 1) * width]
-            for copy in up_copies[h * steps + s]:
-                copy.wait()
-            gate += jnp.dot(x, gate_buf[h, s], preferred_element_type=jnp.float32)
-            up += jnp.dot(x, up_buf[h, s], preferred_element_type=jnp.float32)
-    act = (gate * (1.0 / (1.0 + jnp.exp(-gate))) * up).astype(jnp.bfloat16)
-    for h, out in enumerate((other_out, mine_out)):
-        for s in range(steps):
-            down_copies[h * steps + s].wait()
-            out[:, s * width : (s + 1) * width] = jnp.dot(
-                act, down_buf[h, s], preferred_element_type=jnp.float32
-            ).astype(jnp.bfloat16)
+    for copy in copies:
+        copy.start()
+    ready[...] = jnp.zeros_like(ready)
+    for copy in copies:
+        copy.wait()
+
+
+def join_kernel(ready, *refs):
+    parts, out = refs[:-1], refs[-1]
+    count = parts[0].shape[0]
+    for index, part in enumerate(parts):
+        out[index * count : (index + 1) * count, :] = part[...]
+
+
+def near_kernel(core, rows, w_gate, w_up, gate_out, up_out):
+    half = rows.shape[1]
+    at = pl.ds(pl.multiple_of(core[0] * half, half), half)
+    gate_out[...] = jnp.dot(rows[...], w_gate[at], preferred_element_type=jnp.float32)
+    up_out[...] = jnp.dot(rows[...], w_up[at], preferred_element_type=jnp.float32)
+
+
+def far_kernel(core, rows, gate, up, w_gate, w_up, w_down, act_out, out):
+    half = rows.shape[1]
+    at = pl.ds(pl.multiple_of((1 - core[0]) * half, half), half)
+    total = gate[...] + jnp.dot(rows[...], w_gate[at], preferred_element_type=jnp.float32)
+    other = up[...] + jnp.dot(rows[...], w_up[at], preferred_element_type=jnp.float32)
+    act = (total * (1.0 / (1.0 + jnp.exp(-total))) * other).astype(jnp.bfloat16)
+    act_out[...] = act
+    out[...] = jnp.dot(act, w_down[:, at], preferred_element_type=jnp.float32).astype(out.dtype)
+
+
+def down_kernel(core, act, w_down, out):
+    half = out.shape[1]
+    at = pl.ds(pl.multiple_of(core[0] * half, half), half)
+    out[...] = jnp.dot(act[...], w_down[:, at], preferred_element_type=jnp.float32)
 
 
 def spread_kernel(places, own, first, second, third, send):
@@ -258,10 +279,20 @@
     half = features // CORES
     piece = half // PARTS
     slots = CORES * batches * CAP
-    expert = lax.axis_index("ep") // 2
-    core = lax.axis_index("core")
+    expert = (lax.axis_index("ep") // 2).reshape(1)
+    core = lax.axis_index("core").reshape(1)
     f32, bf16 = jnp.float32, jnp.bfloat16
-    big = pltpu.CompilerParams(vmem_limit_bytes=48 * 2**20)
+    hidden = w_gate.shape[2]
+    params = pltpu.CompilerParams(vmem_limit_bytes=16 * 2**20)
+
+    def in_hbm(array):
+        return pltpu.with_memory_space_constraint(array, pltpu.HBM)
+
+    def in_vmem(array):
+        return pltpu.with_memory_space_constraint(array, pltpu.VMEM)
+
+    def cost(flops, moved):
+        return pl.CostEstimate(flops=flops, bytes_accessed=moved, transcendentals=0)
 
     with jax.named_scope("attention"):
         send, stream, gates = pl.pallas_call(
@@ -271,29 +302,40 @@
                 jax.ShapeDtypeStruct((CORES, 8, piece), bf16),
                 jax.ShapeDtypeStruct((8, LANES), f32),
             ),
-            in_specs=[SMEM, SMEM, VMEM, VMEM, VMEM, VMEM, ANY, ANY, VMEM, VMEM],
+            in_specs=[SMEM, SMEM] + [ANY] * 10,
             out_specs=(VMEM, VMEM, VMEM),
             scratch_shapes=[
+                pltpu.SMEM((batches,), jnp.int32),
+                pltpu.SMEM((batches, 2), jnp.int32),
+                pltpu.VMEM((batches, features), bf16),
+                pltpu.VMEM((batches, features), bf16),
+                pltpu.VMEM((batches, kv_width), bf16),
+                pltpu.VMEM((batches, kv_width), bf16),
+                pltpu.VMEM((1, features), f32),
+                pltpu.VMEM(router.shape[::-1], bf16),
                 pltpu.VMEM((batches, context, kv_width), bf16),
                 pltpu.VMEM((batches, context, kv_width), bf16),
                 pltpu.VMEM((batches, 8 * KV_HEADS, kv_width), f32),
                 pltpu.VMEM((8, features), f32),
                 pltpu.VMEM((2, 8, piece + LANES), f32),
                 pltpu.SemaphoreType.DMA((2 * batches,)),
+                pltpu.SemaphoreType.DMA((8,)),
             ],
-            compiler_params=big,
+            compiler_params=params,
             name="attention",
         )(
-            lengths.reshape(batches),
-            expert_ids.reshape(batches, 2),
-            query.reshape(batches, features),
-            residual.reshape(batches, features),
-            new_key.reshape(batches, kv_width),
-            new_value.reshape(batches, kv_width),
-            key_cache.reshape(batches, context, kv_width),
-            value_cache.reshape(batches, context, kv_width),
-            norm_gain.reshape(1, features),
-            router.T,
+            expert,
+            core,
+            in_hbm(lengths.reshape(batches)),
+            in_hbm(expert_ids.reshape(batches, 2)),
+            in_hbm(query.reshape(batches, features)),
+            in_hbm(residual.reshape(batches, features)),
+            in_hbm(new_key.reshape(batches, kv_width)),
+            in_hbm(new_value.reshape(batches, kv_width)),
+            in_hbm(key_cache.reshape(batches, context, kv_width)),
+            in_hbm(value_cache.reshape(batches, context, kv_width)),
+            in_hbm(norm_gain.reshape(1, features)),
+            in_hbm(router.T),
         )
     with jax.named_scope("rows_to_experts"):
         received = lax.all_to_all(send, ("core", "ep"), 0, 0, tiled=True)
@@ -306,9 +348,9 @@
             ),
             in_specs=[SMEM, VMEM],
             out_specs=(VMEM, VMEM),
-            compiler_params=big,
+            compiler_params=params,
             name="select",
-        )(expert.reshape(1), received.reshape(CORES * peers * 8, piece + LANES))
+        )(expert, received.reshape(CORES * peers * 8, piece + LANES))
 
     def along(array, step):
         return lax.ppermute(array, "x", [(i, (i + step) % xs) for i in range(xs)])
@@ -318,27 +360,68 @@
 
     with jax.named_scope("rows_along_x"):
         parts = [chosen] + [along(chosen, step) for step in range(1, xs)]
-        mine = jnp.concatenate(parts, axis=0)
+    with jax.named_scope("weights"):
+        gate_here, up_here, down_here, ready = pl.pallas_call(
+            fetch_kernel,
+            out_shape=tuple(pltpu.VMEM(w.shape[1:], bf16) for w in (w_gate, w_up, w_down))
+            + (jax.ShapeDtypeStruct((8, LANES), f32),),
+            in_specs=[VMEM] + [ANY] * 3,
+            out_specs=(VMEM,) * 4,
+            scratch_shapes=[pltpu.SemaphoreType.DMA((12,))],
+            compiler_params=pltpu.CompilerParams(vmem_limit_bytes=2**20),
+            cost_estimate=cost(0, 6 * w_gate.size),
+            name="weights",
+        )(places, in_hbm(w_gate[0]), in_hbm(w_up[0]), in_hbm(w_down[0]))
+    with jax.named_scope("join"):
+        mine = pl.pallas_call(
+            join_kernel,
+            out_shape=jax.ShapeDtypeStruct((xs * slots, half), bf16),
+            in_specs=[VMEM] * (xs + 1),
+            out_specs=VMEM,
+            compiler_params=params,
+            name="join",
+        )(ready, *parts)
     with jax.named_scope("rows_between_cores"):
         other = swap(mine)
-    with jax.named_scope("experts"):
-        mine_sum, other_sum = pl.pallas_call(
-            expert_kernel,
-            out_shape=(jax.ShapeDtypeStruct(mine.shape, bf16),) * 2,
-            in_specs=[SMEM, VMEM, VMEM, ANY, ANY, ANY],
+    with jax.named_scope("near_half"):
+        gate, up = pl.pallas_call(
+            near_kernel,
+            out_shape=(jax.ShapeDtypeStruct((mine.shape[0], hidden), f32),) * 2,
+            in_specs=[SMEM, VMEM, VMEM, VMEM],
             out_specs=(VMEM, VMEM),
-            scratch_shapes=[
-                pltpu.VMEM((2, 4, half // 4, w_gate.shape[2]), bf16),
-                pltpu.VMEM((2, 4, half // 4, w_gate.shape[2]), bf16),
-                pltpu.VMEM((2, 4, w_down.shape[1], half // 4), bf16),
-                pltpu.SemaphoreType.DMA((24,)),
-            ],
-            compiler_params=big,
-            name="experts",
-        )(core.reshape(1), mine, other, w_gate[0], w_up[0], w_down[0])
+            compiler_params=params,
+            cost_estimate=cost(2 * mine.size * 2 * hidden, 2 * w_gate.size),
+            name="near_half",
+        )(core, mine, in_vmem(gate_here), in_vmem(up_here))
+    with jax.named_scope("far_half"):
+        act, other_sum = pl.pallas_call(
+            far_kernel,
+            out_shape=(
+                jax.ShapeDtypeStruct((mine.shape[0], hidden), bf16),
+                jax.ShapeDtypeStruct(mine.shape, bf16),
+            ),
+            in_specs=[SMEM] + [VMEM] * 6,
+            out_specs=(VMEM, VMEM),
+            compiler_params=params,
+            cost_estimate=cost(2 * mine.size * 3 * hidden, 3 * w_gate.size),
+            name="far_half",
+        )(
+            core, other, gate, up,
+            in_vmem(gate_here), in_vmem(up_here), in_vmem(down_here),
+        )
     with jax.named_scope("sums_between_cores"):
         arrived = swap(other_sum)
-        total = (mine_sum.astype(f32) + arrived.astype(f32)).astype(bf16)
+    with jax.named_scope("down"):
+        mine_sum = pl.pallas_call(
+            down_kernel,
+            out_shape=jax.ShapeDtypeStruct(mine.shape, f32),
+            in_specs=[SMEM] + [VMEM] * 2,
+            out_specs=VMEM,
+            compiler_params=params,
+            cost_estimate=cost(2 * mine.size * hidden, w_gate.size),
+            name="down",
+        )(core, act, in_vmem(down_here))
+        total = (mine_sum + arrived.astype(f32)).astype(bf16)
     with jax.named_scope("sums_along_x"):
         total = total.reshape(xs, slots, half)
         backs = [along(total[step], xs - step) for step in range(1, xs)]
@@ -348,7 +431,7 @@
             out_shape=jax.ShapeDtypeStruct((CORES * peers * 8, piece), bf16),
             in_specs=[VMEM] * (2 + len(backs)),
             out_specs=VMEM,
-            compiler_params=big,
+            compiler_params=params,
             name="spread",
         )(places, total[0], *backs)
     with jax.named_scope("sums_to_rows"):
@@ -362,7 +445,7 @@
             in_specs=[VMEM, VMEM, VMEM],
             out_specs=VMEM,
             scratch_shapes=[pltpu.VMEM((8, features), f32)],
-            compiler_params=big,
+            compiler_params=params,
             name="combine",
         )(received, stream, gates)
     return out.reshape(batches, 1, features)

time: 85.4 us -> 70.2 us (0.82)
  waiting for transfers between devices: 30.3 us -> 10.8 us
  blocking collectives: 14.4 us -> 33.8 us
  local copies, waits for them, and re-layouts: 9.08 us -> 0.04 us
  starting transfers between devices: 16.4 us -> 8.02 us
  Pallas kernels: 13.1 us -> 16 us
    all_to_all x0 -> x1, blocking collectives: none -> 19.4 us  [shards(): received = lax.all_to_all(send, ('core', 'ep'), 0, 0, tiled=True)]
    all_to_all x1 -> x0, waiting for transfers between devices: 11.3 us -> none  [shards(): received = lax.all_to_all(send, ('core', 'ep'), 0, 0, tiled=True)]
    unnamed x23 -> x0, local copies, waits for them, and re-layouts: 9.02 us -> none
    all_to_all x1 -> x0, starting transfers between devices: 8.35 us -> none  [shards(): received = lax.all_to_all(send, ('core', 'ep'), 0, 0, tiled=True)]
    ppermute x6, waiting for transfers between devices: 15.2 us -> 8.74 us  [along(): return lax.ppermute(array, 'x', [(i, (i + step) % xs) for i in range(xs)])]
    pallas_call x1 -> x5, Pallas kernels: 7.53 us -> 10.1 us  [the longest x1 6.52 us: shards(): pl.pallas_call(fetch_kernel, out_shape=tuple((pltpu.VMEM(w.shape[1:], bf1...]
    ppermute x2, waiting for transfers between devices: 3.85 us -> 2.09 us  [swap(): return lax.ppermute(array, 'core', [(0, 1), (1, 0)])]
  transfers between devices with their start and end apart: 9 -> 8, of which waited for: 7 -> 5; matrix products, arithmetic and copies ran while one was open for 0% -> 0% of each run, Pallas kernels for 0% -> 12%
where the time goes in v2:
time: 70.2 us; the launch traced here: 69 us
  blocking collectives  33.8 us (48%)
  Pallas kernels  16 us (23%)
  waiting for transfers between devices  10.8 us (15%)
  starting transfers between devices  8.02 us (11%)
    all_to_all x1, blocking collectives, shards(): received = lax.all_to_all(send, ('core', 'ep'), 0, 0, tiled=True)  19.4 us
    all_to_all x1, blocking collectives, shards(): lax.all_to_all(send.reshape(CORES * peers, 8, piece), ('core', 'ep'), 0,...  14.4 us
    ppermute x6, waiting for transfers between devices, along(): return lax.ppermute(array, 'x', [(i, (i + step) % xs) for i in range(xs)])  8.74 us
    ppermute x6, starting transfers between devices, along(): return lax.ppermute(array, 'x', [(i, (i + step) % xs) for i in range(xs)])  7.72 us
    pallas_call x1, Pallas kernels, shards(): pl.pallas_call(fetch_kernel, out_shape=tuple((pltpu.VMEM(w.shape[1:], bf1...  6.52 us
    pallas_call x1, Pallas kernels, shards(): pl.pallas_call(attention_kernel, out_shape=(jax.ShapeDtypeStruct((CORES *...  4.32 us
    ppermute x2, waiting for transfers between devices, swap(): return lax.ppermute(array, 'core', [(0, 1), (1, 0)])  2.09 us
    pallas_call x1, Pallas kernels, shards(): pl.pallas_call(far_kernel, out_shape=(jax.ShapeDtypeStruct((mine.shape[0]...  1.73 us
  transfers between devices with their start and end apart: 8, of which 5 were waited for; matrix products, arithmetic and copies ran while one was open for 0% of the time, Pallas kernels for 12%

profile of v2, /device:TPU:6, one launch (start us, length us, event | category | flops | bytes accessed | tf_op | source)
XLA Modules:
  0.0 69.0 jit_solution(1454484526369430563)
XLA Ops:
  0.0 4.3 %attention.1 = (bf16[32,8,896]{2,1,0:T(8,128)(2,1)S(1)}, bf16[2,8,768]{2,1,0:T(8,128)(2,1)S(1)}, f32[8,128]{1,0:T(8,128)S(1)}) custom-call(s32[1]{0:T(128)} %bitcast.expert, s32[1]{0:T(128)} %bitcast.1.core, s32[2]{0:T(128)} %bitcast.32, s32[2,2]{1,0:T(2,128)} %bitcast.31, bf16[2,6144]{1,0:T(2,128)(2,1)} %bitcast.26, bf16[2,6144]{1,0:T(2,128)(2,1)} %bitcast.27, ...), custom_call_target="tpu_custom_call" | custom-call | tf_op jit(solution)/shard_map/attention/attention/pallas_call | solution.py:298
  4.3 19.4 %all_to_all.10 = bf16[32,8,896]{2,1,0:T(8,128)(2,1)S(1)} all-to-all(bf16[32,8,896]{2,1,0:T(8,128)(2,1)S(1)} %get-tuple-element.18), channel_id=1, replica_groups=mesh['x'=4,'core'=2,'ep'=16] {'core','ep'}, dimensions={0} | all-to-all | bytes 917504 | tf_op jit(solution)/shard_map/rows_to_experts/all_to_all | solution.py:341
  23.8 0.5 select.5
  24.3 0.9 %collective-permute-start.2 = (bf16[24,3072]{1,0:T(8,128)(2,1)S(1)}, bf16[24,3072]{1,0:T(8,128)(2,1)S(1)}, u32[]{:S(2)}, u32[]{:S(2)}) collective-permute-start(bf16[24,3072]{1,0:T(8,128)(2,1)S(1)} %get-tuple-element.21.refs_0_), channel_id=1, source_target_pairs={{0,96},{32,0},{64,32},{96,64},{1,97},{33,1},{65,33},{97,65},{2,98}... | collective-permute-start | bytes 442376 | tf_op jit(solution)/shard_map/rows_along_x/ppermute | solution.py:356
  25.2 1.1 %collective-permute-start.1 = (bf16[24,3072]{1,0:T(8,128)(2,1)S(1)}, bf16[24,3072]{1,0:T(8,128)(2,1)S(1)}, u32[]{:S(2)}, u32[]{:S(2)}) collective-permute-start(bf16[24,3072]{1,0:T(8,128)(2,1)S(1)} %get-tuple-element.21.refs_0_), channel_id=1, source_target_pairs={{0,64},{32,96},{64,0},{96,32},{1,65},{33,97},{65,1},{97,33},{2,66}... | collective-permute-start | bytes 442376 | tf_op jit(solution)/shard_map/rows_along_x/ppermute | solution.py:356
  26.3 2.1 %collective-permute-start = (bf16[24,3072]{1,0:T(8,128)(2,1)S(1)}, bf16[24,3072]{1,0:T(8,128)(2,1)S(1)}, u32[]{:S(2)}, u32[]{:S(2)}) collective-permute-start(bf16[24,3072]{1,0:T(8,128)(2,1)S(1)} %get-tuple-element.21.refs_0_), channel_id=1, source_target_pairs={{0,32},{32,64},{64,96},{96,0},{1,33},{33,65},{65,97},{97,1},{2,34}... | collective-permute-start | bytes 442376 | tf_op jit(solution)/shard_map/rows_along_x/ppermute | solution.py:356
  28.4 6.5 %weights.1 = (bf16[6144,512]{1,0:T(8,128)(2,1)S(1)}, bf16[6144,512]{1,0:T(8,128)(2,1)S(1)}, bf16[512,6144]{1,0:T(8,128)(2,1)S(1)}, f32[8,128]{1,0:T(8,128)S(1)}) custom-call(bf16[256,128]{1,0:T(8,128)(2,1)S(1)} %get-tuple-element.19.after.places, bf16[6144,512]{1,0:T(8,128)(2,1)} %bitcast.20, bf16[6144,512]{1,0:T(8,128)(2,1)} %bitcast.21, ...), custom_call_target="tpu_custom_call" | custom-call | bytes 18874368 | tf_op jit(solution)/shard_map/weights/weights/pallas_call | solution.py:364
  34.9 0.0 collective-permute-done.2.refs_3_
  35.0 0.0 collective-permute-done.1.refs_2_
  35.0 0.0 collective-permute-done.refs_1_
  35.0 0.1 collective-permute-start.3
  35.1 1.1 %near_half.1 = (f32[96,512]{1,0:T(8,128)S(1)}, f32[96,512]{1,0:T(8,128)S(1)}) custom-call(s32[1]{0:T(128)} %bitcast.1.core, bf16[96,3072]{1,0:T(8,128)(2,1)S(1)} %join.1.rows, bf16[6144,512]{1,0:T(8,128)(2,1)S(1)} %get-tuple-element.22.w_gate, bf16[6144,512]{1,0:T(8,128)(2,1)S(1)} %get-tuple-element.23.w_up), custom_call_target="tpu_custom_call" | custom-call | flops 603979776 | bytes 6291456 | tf_op jit(solution)/shard_map/near_half/near_half/pallas_call | solution.py:387
  36.2 0.9 %collective-permute-done.3.rows = bf16[96,3072]{1,0:T(8,128)(2,1)S(1)} collective-permute-done((bf16[96,3072]{1,0:T(8,128)(2,1)S(1)}, bf16[96,3072]{1,0:T(8,128)(2,1)S(1)}, u32[]{:S(2)}, u32[]{:S(2)}) %collective-permute-start.3) | collective-permute-done | bytes 589856 | tf_op jit(solution)/shard_map/rows_between_cores/ppermute | solution.py:359
  37.1 1.7 %far_half.1 = (bf16[96,512]{1,0:T(8,128)(2,1)S(1)}, bf16[96,3072]{1,0:T(8,128)(2,1)S(1)}) custom-call(s32[1]{0:T(128)} %bitcast.1.core, bf16[96,3072]{1,0:T(8,128)(2,1)S(1)} %collective-permute-done.3.rows, f32[96,512]{1,0:T(8,128)S(1)} %get-tuple-element.24.gate, f32[96,512]{1,0:T(8,128)S(1)} %get-tuple-element.25.up, ...), custom_call_target="tpu_custom_call" | custom-call | flops 905969664 | bytes 9437184 | tf_op jit(solution)/shard_map/far_half/far_half/pallas_call | solution.py:397
  38.8 0.2 collective-permute-start.4
  39.1 0.6 down.1
  39.7 1.2 %collective-permute-done.4 = bf16[96,3072]{1,0:T(8,128)(2,1)S(1)} collective-permute-done((bf16[96,3072]{1,0:T(8,128)(2,1)S(1)}, bf16[96,3072]{1,0:T(8,128)(2,1)S(1)}, u32[]{:S(2)}, u32[]{:S(2)}) %collective-permute-start.4) | collective-permute-done | bytes 589856 | tf_op jit(solution)/shard_map/sums_between_cores/ppermute | solution.py:359
  40.9 0.1 add_convert_fusion
  41.1 2.4 %collective-permute-start.7 = (bf16[24,3072]{1,0:T(8,128)(2,1)S(1)}, bf16[24,3072]{1,0:T(8,128)(2,1)S(1)}, u32[]{:S(2)}, u32[]{:S(2)}) collective-permute-start(bf16[24,3072]{1,0:T(8,128)(2,1)S(1)} %get-tuple-element.31), channel_id=1, source_target_pairs={{0,32},{32,64},{64,96},{96,0},{1,33},{33,65},{65,97},{97,1},{2,34}... | collective-permute-start | bytes 442376 | tf_op jit(solution)/shard_map/sums_along_x/ppermute | solution.py:356
  43.5 0.2 collective-permute-start.6
  43.7 1.1 %collective-permute-start.5 = (bf16[24,3072]{1,0:T(8,128)(2,1)S(1)}, bf16[24,3072]{1,0:T(8,128)(2,1)S(1)}, u32[]{:S(2)}, u32[]{:S(2)}) collective-permute-start(bf16[24,3072]{1,0:T(8,128)(2,1)S(1)} %get-tuple-element.33), channel_id=1, source_target_pairs={{0,96},{32,0},{64,32},{96,64},{1,97},{33,1},{65,33},{97,65},{2,98}... | collective-permute-start | bytes 442376 | tf_op jit(solution)/shard_map/sums_along_x/ppermute | solution.py:356
  44.7 5.4 %collective-permute-done.7.third = bf16[24,3072]{1,0:T(8,128)(2,1)S(1)} collective-permute-done((bf16[24,3072]{1,0:T(8,128)(2,1)S(1)}, bf16[24,3072]{1,0:T(8,128)(2,1)S(1)}, u32[]{:S(2)}, u32[]{:S(2)}) %collective-permute-start.7) | collective-permute-done | bytes 147488 | tf_op jit(solution)/shard_map/sums_along_x/ppermute | solution.py:356
  50.1 1.6 %collective-permute-done.6.second = bf16[24,3072]{1,0:T(8,128)(2,1)S(1)} collective-permute-done((bf16[24,3072]{1,0:T(8,128)(2,1)S(1)}, bf16[24,3072]{1,0:T(8,128)(2,1)S(1)}, u32[]{:S(2)}, u32[]{:S(2)}) %collective-permute-start.6) | collective-permute-done | bytes 147488 | tf_op jit(solution)/shard_map/sums_along_x/ppermute | solution.py:356
  51.7 1.8 %collective-permute-done.5.first = bf16[24,3072]{1,0:T(8,128)(2,1)S(1)} collective-permute-done((bf16[24,3072]{1,0:T(8,128)(2,1)S(1)}, bf16[24,3072]{1,0:T(8,128)(2,1)S(1)}, u32[]{:S(2)}, u32[]{:S(2)}) %collective-permute-start.5) | collective-permute-done | bytes 147488 | tf_op jit(solution)/shard_map/sums_along_x/ppermute | solution.py:356
  53.5 0.3 spread.1
  53.8 14.4 %all_to_all.11.received = bf16[32,8,768]{2,1,0:T(8,128)(2,1)S(1)} all-to-all(bf16[32,8,768]{2,1,0:T(8,128)(2,1)S(1)} %bitcast.19), channel_id=1, replica_groups=mesh['x'=4,'core'=2,'ep'=16] {'core','ep'}, dimensions={0} | all-to-all | bytes 786432 | tf_op jit(solution)/shard_map/sums_to_rows/all_to_all | solution.py:438
  68.2 0.8 %combine.1 = bf16[2,6144]{1,0:T(2,128)(2,1)} custom-call(bf16[32,8,768]{2,1,0:T(8,128)(2,1)S(1)} %all_to_all.11.received, bf16[2,8,768]{2,1,0:T(8,128)(2,1)S(1)} %get-tuple-element.29.stream, f32[8,128]{1,0:T(8,128)S(1)} %get-tuple-element.30.gates), custom_call_target="tpu_custom_call" | custom-call | tf_op jit(solution)/shard_map/combine/combine/pallas_call | solution.py:442
  (2 shorter events, 0.1 us)
Async XLA Ops:
  24.3 10.6 %collective-permute-start.2 = (bf16[24,3072]{1,0:T(8,128)(2,1)S(1)}, bf16[24,3072]{1,0:T(8,128)(2,1)S(1)}, u32[]{:S(2)}, u32[]{:S(2)}) collective-permute-start(bf16[24,3072]{1,0:T(8,128)(2,1)S(1)} %get-tuple-element.21.refs_0_), channel_id=1, source_target_pairs={{0,96},{32,0},{64,32},{96,64},{1,97},{33,1},{65,33},{97,65},{2,98}... | collective-permute-start | bytes 442376 | tf_op jit(solution)/shard_map/rows_along_x/ppermute | solution.py:356
  25.2 9.8 %collective-permute-start.1 = (bf16[24,3072]{1,0:T(8,128)(2,1)S(1)}, bf16[24,3072]{1,0:T(8,128)(2,1)S(1)}, u32[]{:S(2)}, u32[]{:S(2)}) collective-permute-start(bf16[24,3072]{1,0:T(8,128)(2,1)S(1)} %get-tuple-element.21.refs_0_), channel_id=1, source_target_pairs={{0,64},{32,96},{64,0},{96,32},{1,65},{33,97},{65,1},{97,33},{2,66}... | collective-permute-start | bytes 442376 | tf_op jit(solution)/shard_map/rows_along_x/ppermute | solution.py:356
  26.3 8.7 %collective-permute-start = (bf16[24,3072]{1,0:T(8,128)(2,1)S(1)}, bf16[24,3072]{1,0:T(8,128)(2,1)S(1)}, u32[]{:S(2)}, u32[]{:S(2)}) collective-permute-start(bf16[24,3072]{1,0:T(8,128)(2,1)S(1)} %get-tuple-element.21.refs_0_), channel_id=1, source_target_pairs={{0,32},{32,64},{64,96},{96,0},{1,33},{33,65},{65,97},{97,1},{2,34}... | collective-permute-start | bytes 442376 | tf_op jit(solution)/shard_map/rows_along_x/ppermute | solution.py:356
  35.0 2.1 %collective-permute-start.3 = (bf16[96,3072]{1,0:T(8,128)(2,1)S(1)}, bf16[96,3072]{1,0:T(8,128)(2,1)S(1)}, u32[]{:S(2)}, u32[]{:S(2)}) collective-permute-start(bf16[96,3072]{1,0:T(8,128)(2,1)S(1)} %join.1.rows), channel_id=1, source_target_pairs={{0,16},{16,0},{1,17},{17,1},{2,18},{18,2},{3,19},{19,3},{4,20},{20... | collective-permute-start | bytes 1769480 | tf_op jit(solution)/shard_map/rows_between_cores/ppermute | solution.py:359
  38.8 2.1 %collective-permute-start.4 = (bf16[96,3072]{1,0:T(8,128)(2,1)S(1)}, bf16[96,3072]{1,0:T(8,128)(2,1)S(1)}, u32[]{:S(2)}, u32[]{:S(2)}) collective-permute-start(bf16[96,3072]{1,0:T(8,128)(2,1)S(1)} %get-tuple-element.28), channel_id=1, source_target_pairs={{0,16},{16,0},{1,17},{17,1},{2,18},{18,2},{3,19},{19,3},{4,20},{20... | collective-permute-start | bytes 1769480 | tf_op jit(solution)/shard_map/sums_between_cores/ppermute | solution.py:359
  41.1 9.0 %collective-permute-start.7 = (bf16[24,3072]{1,0:T(8,128)(2,1)S(1)}, bf16[24,3072]{1,0:T(8,128)(2,1)S(1)}, u32[]{:S(2)}, u32[]{:S(2)}) collective-permute-start(bf16[24,3072]{1,0:T(8,128)(2,1)S(1)} %get-tuple-element.31), channel_id=1, source_target_pairs={{0,32},{32,64},{64,96},{96,0},{1,33},{33,65},{65,97},{97,1},{2,34}... | collective-permute-start | bytes 442376 | tf_op jit(solution)/shard_map/sums_along_x/ppermute | solution.py:356
  43.5 8.2 %collective-permute-start.6 = (bf16[24,3072]{1,0:T(8,128)(2,1)S(1)}, bf16[24,3072]{1,0:T(8,128)(2,1)S(1)}, u32[]{:S(2)}, u32[]{:S(2)}) collective-permute-start(bf16[24,3072]{1,0:T(8,128)(2,1)S(1)} %get-tuple-element.32), channel_id=1, source_target_pairs={{0,64},{32,96},{64,0},{96,32},{1,65},{33,97},{65,1},{97,33},{2,66}... | collective-permute-start | bytes 442376 | tf_op jit(solution)/shard_map/sums_along_x/ppermute | solution.py:356
  43.7 9.8 %collective-permute-start.5 = (bf16[24,3072]{1,0:T(8,128)(2,1)S(1)}, bf16[24,3072]{1,0:T(8,128)(2,1)S(1)}, u32[]{:S(2)}, u32[]{:S(2)}) collective-permute-start(bf16[24,3072]{1,0:T(8,128)(2,1)S(1)} %get-tuple-element.33), channel_id=1, source_target_pairs={{0,96},{32,0},{64,32},{96,64},{1,97},{33,1},{65,33},{97,65},{2,98}... | collective-permute-start | bytes 442376 | tf_op jit(solution)/shard_map/sums_along_x/ppermute | solution.py:356

commit v3 on v2

--- a/solution.py
+++ b/solution.py
@@ -12,7 +12,7 @@
 CAP = 6
 CORES = 2
 LANES = 128
-PARTS = 4
+PARTS = 8
 EPSILON = 1e-05
 
 VMEM = pl.BlockSpec(memory_space=pltpu.VMEM)
@@ -25,7 +25,7 @@
 
 
 def attention_kernel(
-    expert, core, lengths_at, ids_at, query_at, residual_at, new_key_at, new_value_at, keys, values, gain_at,
+    expert, lengths_at, ids_at, query_at, residual_at, new_key_at, new_value_at, keys, values, gain_at,
     router_at, send, stream_out, gates_out,
     lengths, ids, query, residual, new_key, new_value, gain, router,
     key_buf, value_buf, spread, rows, packed, sems, small_sems,
@@ -33,9 +33,8 @@
     batches, features = query.shape
     heads = features // HEAD
     group = heads // KV_HEADS
-    peers = send.shape[0] // CORES
-    half = features // CORES
-    piece = half // PARTS
+    peers = send.shape[0]
+    piece = features // PARTS
     copies = []
     for row in range(batches):
         copies.append(
@@ -122,20 +121,18 @@
         (((1,), (1,)), ((), ())),
         preferred_element_type=jnp.float32,
     )
-    for side in range(CORES):
-        for row in range(batches):
-            for part in range(PARTS):
-                start = side * half + part * piece
-                place = row * PARTS + part
-                packed[0, pl.ds(place, 1), 0:piece] = normed[row : row + 1, start : start + piece]
-                packed[1, pl.ds(place, 1), 0:piece] = stream[row : row + 1, start : start + piece]
-            lane = iota((PARTS, LANES), 1)
-            names = jnp.where(lane == 0, ids[row, 0], jnp.where(lane == 1, ids[row, 1], 0))
-            packed[0, pl.ds(row * PARTS, PARTS), piece : piece + LANES] = names.astype(jnp.float32)
-        chunk = packed[0].astype(jnp.bfloat16)
-        for peer in range(peers):
-            send[side * peers + peer] = chunk
-        stream_out[side] = packed[1, :, 0:piece].astype(jnp.bfloat16)
+    for row in range(batches):
+        for part in range(PARTS):
+            start, place = part * piece, row * PARTS + part
+            packed[0, pl.ds(place, 1), 0:piece] = normed[row : row + 1, start : start + piece]
+            packed[1, pl.ds(place, 1), 0:piece] = stream[row : row + 1, start : start + piece]
+        lane = iota((PARTS, LANES), 1)
+        names = jnp.where(lane == 0, ids[row, 0], jnp.where(lane == 1, ids[row, 1], 0))
+        packed[0, pl.ds(row * PARTS, PARTS), piece : piece + LANES] = names.astype(jnp.float32)
+    chunk = packed[0].astype(jnp.bfloat16)
+    for peer in range(peers):
+        send[peer] = chunk
+    stream_out[...] = packed[1, :, 0:piece].astype(jnp.bfloat16)
     for row in range(batches):
         lane = iota((1, logits.shape[1]), 1)
         own = logits[row : row + 1]
@@ -155,23 +152,26 @@
 def select_kernel(expert, received, chosen_out, places_out):
     count, width = received.shape
     piece = width - LANES
-    slots = CORES * 2 * CAP
+    slots = 2 * CAP
+    sides = 2
     here = expert[0].astype(jnp.float32)
     names = received[:, piece:].astype(jnp.float32)
     lane = iota(names.shape, 1)
     match = jnp.where((names == here) & (lane < 2), 1.0, 0.0)
     match = jnp.sum(match, axis=1, keepdims=True)
     a, b = iota((count, count), 0), iota((count, count), 1)
-    span = 8 * (count // (8 * CORES))
-    earlier = (a // span == b // span) & (a % 8 == b % 8) & (b < a)
+    span = 2 * PARTS
+    earlier = (a % span == b % span) & (b // span < a // span)
     rank = jnp.dot(
         jnp.where(earlier, 1.0, 0.0).astype(jnp.bfloat16),
         jnp.broadcast_to(match, (count, LANES)).astype(jnp.bfloat16),
         preferred_element_type=jnp.float32,
     )
     r, col = iota((count, LANES), 0), iota((count, LANES), 1)
-    part, batch, core = r % PARTS, (r % 8) // PARTS, r // span
-    target = part * slots + core * (2 * CAP) + batch * CAP + rank.astype(jnp.int32)
+    part, batch = r % PARTS, (r % span) // PARTS
+    wide = PARTS // sides
+    target = (part % wide) * (sides * slots) + (part // wide) * slots + batch * CAP
+    target = target + rank.astype(jnp.int32)
     places = jnp.where((col == target) & (match > 0.5), 1.0, 0.0).astype(jnp.bfloat16)
     places_out[...] = places
     chosen = lax.dot_general(
@@ -180,16 +180,17 @@
         (((0,), (0,)), ((), ())),
         preferred_element_type=jnp.float32,
     ).astype(jnp.bfloat16).astype(jnp.float32)
-    for part in range(PARTS):
+    count = sides * slots
+    for part in range(wide):
         chosen_out[:, part * piece : (part + 1) * piece] = chosen[
-            part * slots : (part + 1) * slots
+            part * count : (part + 1) * count
         ].astype(jnp.bfloat16)
 
 
-def fetch_kernel(after, gate_at, up_at, down_at, gate, up, down, ready, sems):
+def fetch_kernel(after, up_at, down_at, up, down, ready, sems):
     pieces = 4
     copies = []
-    for source, target in ((gate_at, gate), (up_at, up), (down_at, down)):
+    for source, target in ((up_at, up), (down_at, down)):
         rows = source.shape[0] // pieces
         for piece in range(pieces):
             at = pl.ds(piece * rows, rows)
@@ -210,37 +211,58 @@
         out[index * count : (index + 1) * count, :] = part[...]
 
 
-def near_kernel(core, rows, w_gate, w_up, gate_out, up_out):
-    half = rows.shape[1]
-    at = pl.ds(pl.multiple_of(core[0] * half, half), half)
-    gate_out[...] = jnp.dot(rows[...], w_gate[at], preferred_element_type=jnp.float32)
-    up_out[...] = jnp.dot(rows[...], w_up[at], preferred_element_type=jnp.float32)
-
-
-def far_kernel(core, rows, gate, up, w_gate, w_up, w_down, act_out, out):
-    half = rows.shape[1]
-    at = pl.ds(pl.multiple_of((1 - core[0]) * half, half), half)
-    total = gate[...] + jnp.dot(rows[...], w_gate[at], preferred_element_type=jnp.float32)
-    other = up[...] + jnp.dot(rows[...], w_up[at], preferred_element_type=jnp.float32)
-    act = (total * (1.0 / (1.0 + jnp.exp(-total))) * other).astype(jnp.bfloat16)
-    act_out[...] = act
-    out[...] = jnp.dot(act, w_down[:, at], preferred_element_type=jnp.float32).astype(out.dtype)
-
-
-def down_kernel(core, act, w_down, out):
+def whole_rows(rows, slots):
+    wide = rows[...].astype(jnp.float32)
+    count = wide.shape[0] // (2 * slots)
+    return [
+        jnp.concatenate(
+            [wide[(2 * i + side) * slots : (2 * i + side + 1) * slots] for i in range(count)], axis=0
+        ).astype(jnp.bfloat16)
+        for side in range(2)
+    ]
+
+
+def half_rows(whole, slots, out):
     half = out.shape[1]
-    at = pl.ds(pl.multiple_of(core[0] * half, half), half)
-    out[...] = jnp.dot(act[...], w_down[:, at], preferred_element_type=jnp.float32)
+    count = whole.shape[0] // slots
+    parts = []
+    for i in range(count):
+        for side in range(2):
+            parts.append(whole[i * slots : (i + 1) * slots, side * half : (side + 1) * half])
+    out[...] = jnp.concatenate(parts, axis=0).astype(out.dtype)
+
+
+def expert_kernel(mine, other, w_gate, w_up, w_down, act_out, out):
+    slots = 2 * CAP
+    half = mine.shape[1]
+    sides = [
+        jnp.concatenate(pair, axis=0)
+        for pair in zip(whole_rows(mine, slots), whole_rows(other, slots))
+    ]
+    gate, up = (
+        jnp.dot(sides[0], w[0:half], preferred_element_type=jnp.float32)
+        + jnp.dot(sides[1], w[half : 2 * half], preferred_element_type=jnp.float32)
+        for w in (w_gate, w_up)
+    )
+    act = (gate * (1.0 / (1.0 + jnp.exp(-gate))) * up).astype(jnp.bfloat16)
+    count = act.shape[0] // 2
+    act_out[...] = act[0:count]
+    half_rows(jnp.dot(act[count:], w_down[...], preferred_element_type=jnp.float32), slots, out)
+
+
+def down_kernel(act, w_down, out):
+    half_rows(jnp.dot(act[...], w_down[...], preferred_element_type=jnp.float32), 2 * CAP, out)
 
 
 def spread_kernel(places, own, first, second, third, send):
     slots, width = own.shape
-    piece = width // PARTS
+    piece = send.shape[1]
+    wide = width // piece
     total = own[...].astype(jnp.float32) + first[...].astype(jnp.float32)
     total = total + second[...].astype(jnp.float32) + third[...].astype(jnp.float32)
     stacked = jnp.concatenate(
-        [total[:, part * piece : (part + 1) * piece] for part in range(PARTS)]
-        + [jnp.zeros((LANES - PARTS * slots, piece), jnp.float32)],
+        [total[:, part * piece : (part + 1) * piece] for part in range(wide)]
+        + [jnp.zeros((LANES - wide * slots, piece), jnp.float32)],
         axis=0,
     ).astype(jnp.bfloat16)
     send[...] = jnp.dot(places[...], stacked, preferred_element_type=jnp.float32).astype(
@@ -249,21 +271,16 @@
 
 
 def combine_kernel(received, stream, gates, out, rows):
-    peers = received.shape[0] // CORES
-    piece = received.shape[2]
-    half = piece * PARTS
+    peers, _, piece = received.shape
     batches = out.shape[0]
     gate = gates[...]
-    for core in range(CORES):
-        total = jnp.zeros(received.shape[1:], jnp.float32)
-        for peer in range(peers):
-            total += received[core * peers + peer].astype(jnp.float32) * gate[:, peer : peer + 1]
-        total += stream[core].astype(jnp.float32)
-        for row in range(batches):
-            for part in range(PARTS):
-                start = core * half + part * piece
-                place = row * PARTS + part
-                rows[row : row + 1, start : start + piece] = total[place : place + 1]
+    total = stream[...].astype(jnp.float32)
+    for peer in range(peers):
+        total += received[peer].astype(jnp.float32) * gate[:, peer : peer + 1]
+    for row in range(batches):
+        for part in range(PARTS):
+            place = row * PARTS + part
+            rows[row : row + 1, part * piece : (part + 1) * piece] = total[place : place + 1]
     out[...] = rows[0:batches].astype(jnp.bfloat16)
 
 
@@ -277,10 +294,10 @@
     xs = lax.axis_size("x")
     peers = lax.axis_size("ep")
     half = features // CORES
-    piece = half // PARTS
-    slots = CORES * batches * CAP
+    piece = features // PARTS
+    pack = batches * PARTS
+    slots = 2 * batches * CAP
     expert = (lax.axis_index("ep") // 2).reshape(1)
-    core = lax.axis_index("core").reshape(1)
     f32, bf16 = jnp.float32, jnp.bfloat16
     hidden = w_gate.shape[2]
     params = pltpu.CompilerParams(vmem_limit_bytes=16 * 2**20)
@@ -298,11 +315,11 @@
         send, stream, gates = pl.pallas_call(
             attention_kernel,
             out_shape=(
-                jax.ShapeDtypeStruct((CORES * peers, 8, piece + LANES), bf16),
-                jax.ShapeDtypeStruct((CORES, 8, piece), bf16),
-                jax.ShapeDtypeStruct((8, LANES), f32),
+                jax.ShapeDtypeStruct((peers, pack, piece + LANES), bf16),
+                jax.ShapeDtypeStruct((pack, piece), bf16),
+                jax.ShapeDtypeStruct((pack, LANES), f32),
             ),
-            in_specs=[SMEM, SMEM] + [ANY] * 10,
+            in_specs=[SMEM] + [ANY] * 10,
             out_specs=(VMEM, VMEM, VMEM),
             scratch_shapes=[
                 pltpu.SMEM((batches,), jnp.int32),
@@ -317,7 +334,7 @@
                 pltpu.VMEM((batches, context, kv_width), bf16),
                 pltpu.VMEM((batches, 8 * KV_HEADS, kv_width), f32),
                 pltpu.VMEM((8, features), f32),
-                pltpu.VMEM((2, 8, piece + LANES), f32),
+                pltpu.VMEM((2, pack, piece + LANES), f32),
                 pltpu.SemaphoreType.DMA((2 * batches,)),
                 pltpu.SemaphoreType.DMA((8,)),
             ],
@@ -325,7 +342,6 @@
             name="attention",
         )(
             expert,
-            core,
             in_hbm(lengths.reshape(batches)),
             in_hbm(expert_ids.reshape(batches, 2)),
             in_hbm(query.reshape(batches, features)),
@@ -338,19 +354,19 @@
             in_hbm(router.T),
         )
     with jax.named_scope("rows_to_experts"):
-        received = lax.all_to_all(send, ("core", "ep"), 0, 0, tiled=True)
+        received = lax.all_to_all(send, "ep", 0, 0, tiled=True)
     with jax.named_scope("select"):
         chosen, places = pl.pallas_call(
             select_kernel,
             out_shape=(
                 jax.ShapeDtypeStruct((slots, half), bf16),
-                jax.ShapeDtypeStruct((CORES * peers * 8, LANES), bf16),
+                jax.ShapeDtypeStruct((peers * pack, LANES), bf16),
             ),
             in_specs=[SMEM, VMEM],
             out_specs=(VMEM, VMEM),
             compiler_params=params,
             name="select",
-        )(expert, received.reshape(CORES * peers * 8, piece + LANES))
+        )(expert, received.reshape(peers * pack, piece + LANES))
 
     def along(array, step):
         return lax.ppermute(array, "x", [(i, (i + step) % xs) for i in range(xs)])
@@ -359,19 +375,20 @@
         return lax.ppermute(array, "core", [(0, 1), (1, 0)])
 
     with jax.named_scope("rows_along_x"):
-        parts = [chosen] + [along(chosen, step) for step in range(1, xs)]
+        steps = (1, xs - 1) + tuple(range(2, xs - 1))
+        parts = [chosen] + [along(chosen, step) for step in steps]
     with jax.named_scope("weights"):
-        gate_here, up_here, down_here, ready = pl.pallas_call(
+        up_here, down_here, ready = pl.pallas_call(
             fetch_kernel,
-            out_shape=tuple(pltpu.VMEM(w.shape[1:], bf16) for w in (w_gate, w_up, w_down))
+            out_shape=tuple(pltpu.VMEM(w.shape[1:], bf16) for w in (w_up, w_down))
             + (jax.ShapeDtypeStruct((8, LANES), f32),),
-            in_specs=[VMEM] + [ANY] * 3,
-            out_specs=(VMEM,) * 4,
-            scratch_shapes=[pltpu.SemaphoreType.DMA((12,))],
+            in_specs=[VMEM] + [ANY] * 2,
+            out_specs=(VMEM,) * 3,
+            scratch_shapes=[pltpu.SemaphoreType.DMA((8,))],
             compiler_params=pltpu.CompilerParams(vmem_limit_bytes=2**20),
-            cost_estimate=cost(0, 6 * w_gate.size),
+            cost_estimate=cost(0, 4 * w_gate.size),
             name="weights",
-        )(places, in_hbm(w_gate[0]), in_hbm(w_up[0]), in_hbm(w_down[0]))
+        )(places, in_hbm(w_up[0]), in_hbm(w_down[0]))
     with jax.named_scope("join"):
         mine = pl.pallas_call(
             join_kernel,
@@ -383,52 +400,42 @@
         )(ready, *parts)
     with jax.named_scope("rows_between_cores"):
         other = swap(mine)
-    with jax.named_scope("near_half"):
-        gate, up = pl.pallas_call(
-            near_kernel,
-            out_shape=(jax.ShapeDtypeStruct((mine.shape[0], hidden), f32),) * 2,
-            in_specs=[SMEM, VMEM, VMEM, VMEM],
-            out_specs=(VMEM, VMEM),
-            compiler_params=params,
-            cost_estimate=cost(2 * mine.size * 2 * hidden, 2 * w_gate.size),
-            name="near_half",
-        )(core, mine, in_vmem(gate_here), in_vmem(up_here))
-    with jax.named_scope("far_half"):
+    weights_in = [in_vmem(w_gate[0]), in_vmem(up_here)]
+    rows_here = mine.shape[0] // 2
+    with jax.named_scope("experts"):
         act, other_sum = pl.pallas_call(
-            far_kernel,
+            expert_kernel,
             out_shape=(
-                jax.ShapeDtypeStruct((mine.shape[0], hidden), bf16),
+                jax.ShapeDtypeStruct((rows_here, hidden), bf16),
                 jax.ShapeDtypeStruct(mine.shape, bf16),
             ),
-            in_specs=[SMEM] + [VMEM] * 6,
+            in_specs=[VMEM] * 5,
             out_specs=(VMEM, VMEM),
             compiler_params=params,
-            cost_estimate=cost(2 * mine.size * 3 * hidden, 3 * w_gate.size),
-            name="far_half",
-        )(
-            core, other, gate, up,
-            in_vmem(gate_here), in_vmem(up_here), in_vmem(down_here),
-        )
+            cost_estimate=cost(10 * mine.size * hidden, 6 * w_gate.size),
+            name="experts",
+        )(mine, other, *weights_in, in_vmem(down_here))
     with jax.named_scope("sums_between_cores"):
         arrived = swap(other_sum)
-    with jax.named_scope("down"):
+    with jax.named_scope("own_down"):
         mine_sum = pl.pallas_call(
             down_kernel,
             out_shape=jax.ShapeDtypeStruct(mine.shape, f32),
-            in_specs=[SMEM] + [VMEM] * 2,
+            in_specs=[VMEM] * 2,
             out_specs=VMEM,
             compiler_params=params,
-            cost_estimate=cost(2 * mine.size * hidden, w_gate.size),
-            name="down",
-        )(core, act, in_vmem(down_here))
+            cost_estimate=cost(2 * mine.size * hidden, 2 * w_gate.size),
+            name="own_down",
+        )(act, in_vmem(down_here))
         total = (mine_sum + arrived.astype(f32)).astype(bf16)
     with jax.named_scope("sums_along_x"):
         total = total.reshape(xs, slots, half)
-        backs = [along(total[step], xs - step) for step in range(1, xs)]
+        backs = [along(total[1 + place], xs - step) for place, step in enumerate(steps)]
+        backs = [backs[1], backs[0]] + backs[2:]
     with jax.named_scope("spread"):
         send = pl.pallas_call(
             spread_kernel,
-            out_shape=jax.ShapeDtypeStruct((CORES * peers * 8, piece), bf16),
+            out_shape=jax.ShapeDtypeStruct((peers * pack, piece), bf16),
             in_specs=[VMEM] * (2 + len(backs)),
             out_specs=VMEM,
             compiler_params=params,
@@ -436,7 +443,7 @@
         )(places, total[0], *backs)
     with jax.named_scope("sums_to_rows"):
         received = lax.all_to_all(
-            send.reshape(CORES * peers, 8, piece), ("core", "ep"), 0, 0, tiled=True
+            send.reshape(peers, pack, piece), "ep", 0, 0, tiled=True
         )
     with jax.named_scope("combine"):
         out = pl.pallas_call(

time: 70.2 us -> 66.6 us (0.949)
  blocking collectives: 33.8 us -> 31.9 us
  waiting for transfers between devices: 10.8 us -> 9.09 us
  starting transfers between devices: 8.02 us -> 9.22 us
    ppermute x6, waiting for transfers between devices: 8.74 us -> 6.43 us  [along(): return lax.ppermute(array, 'x', [(i, (i + step) % xs) for i in range(xs)])]
    all_to_all x2, blocking collectives: 33.8 us -> 31.9 us  [the longest x1 18.6 us: shards(): received = lax.all_to_all(send, 'ep', 0, 0, tiled=True)]
    pallas_call x1, Pallas kernels: 6.52 us -> 4.84 us  [shards(): pl.pallas_call(fetch_kernel, out_shape=tuple((pltpu.VMEM(w.shape[1:], bf1...]
    ppermute x6, starting transfers between devices: 7.72 us -> 8.94 us  [along(): return lax.ppermute(array, 'x', [(i, (i + step) % xs) for i in range(xs)])]
    pallas_call x4 -> x3, Pallas kernels: 7.47 us -> 7.93 us  [the longest x1 4.32 us: shards(): pl.pallas_call(attention_kernel, out_shape=(jax.ShapeDtypeStruct((peers,...]
  transfers between devices with their start and end apart: 8 -> 8, of which waited for: 5 -> 4; matrix products, arithmetic and copies ran while one was open for 0% -> 0% of each run, Pallas kernels for 12% -> 9%
where the time goes in v3:
time: 66.6 us; the launch traced here: 65.8 us
  blocking collectives  31.9 us (48%)
  Pallas kernels  15.3 us (23%)
  starting transfers between devices  9.22 us (14%)
  waiting for transfers between devices  9.09 us (14%)
    all_to_all x1, blocking collectives, shards(): received = lax.all_to_all(send, 'ep', 0, 0, tiled=True)  18.6 us
    all_to_all x1, blocking collectives, shards(): lax.all_to_all(send.reshape(peers, pack, piece), 'ep', 0, 0, tiled=True)  13.3 us
    ppermute x6, starting transfers between devices, along(): return lax.ppermute(array, 'x', [(i, (i + step) % xs) for i in range(xs)])  8.94 us
    ppermute x6, waiting for transfers between devices, along(): return lax.ppermute(array, 'x', [(i, (i + step) % xs) for i in range(xs)])  6.43 us
    pallas_call x1, Pallas kernels, shards(): pl.pallas_call(fetch_kernel, out_shape=tuple((pltpu.VMEM(w.shape[1:], bf1...  4.84 us
    pallas_call x1, Pallas kernels, shards(): pl.pallas_call(attention_kernel, out_shape=(jax.ShapeDtypeStruct((peers,...  4.32 us
    pallas_call x1, Pallas kernels, shards(): pl.pallas_call(expert_kernel, out_shape=(jax.ShapeDtypeStruct((rows_here,...  3.32 us
    ppermute x2, waiting for transfers between devices, swap(): return lax.ppermute(array, 'core', [(0, 1), (1, 0)])  2.67 us
  transfers between devices with their start and end apart: 8, of which 4 were waited for; matrix products, arithmetic and copies ran while one was open for 0% of the time, Pallas kernels for 9%

profile of v3, /device:TPU:6, one launch (start us, length us, event | category | flops | bytes accessed | tf_op | source)
XLA Modules:
  0.0 65.8 jit_solution(11937927106435315624)
XLA Ops:
  0.0 4.3 %attention.1 = (bf16[16,16,896]{2,1,0:T(8,128)(2,1)S(1)}, bf16[16,768]{1,0:T(8,128)(2,1)S(1)}, f32[16,128]{1,0:T(8,128)S(1)}) custom-call(s32[1]{0:T(128)} %bitcast.expert, s32[2]{0:T(128)} %bitcast.33, s32[2,2]{1,0:T(2,128)} %bitcast.32, bf16[2,6144]{1,0:T(2,128)(2,1)} %bitcast.27, bf16[2,6144]{1,0:T(2,128)(2,1)} %bitcast.28, bf16[2,1024]{1,0:T(2,128)(2,1)} %bitcast.30, ...), custom_call_target="tpu_custom_call" | custom-call | tf_op jit(solution)/shard_map/attention/attention/pallas_call | solution.py:315
  4.3 18.6 %all_to_all.10 = bf16[16,16,896]{2,1,0:T(8,128)(2,1)S(1)} all-to-all(bf16[16,16,896]{2,1,0:T(8,128)(2,1)S(1)} %get-tuple-element.15), channel_id=1, replica_groups=mesh['x'=4,'core'=2,'ep'=16] {'ep'}, dimensions={0} | all-to-all | bytes 917504 | tf_op jit(solution)/shard_map/rows_to_experts/all_to_all | solution.py:357
  23.0 0.5 select.5
  23.5 1.5 %collective-permute-start.2 = (bf16[24,3072]{1,0:T(8,128)(2,1)S(1)}, bf16[24,3072]{1,0:T(8,128)(2,1)S(1)}, u32[]{:S(2)}, u32[]{:S(2)}) collective-permute-start(bf16[24,3072]{1,0:T(8,128)(2,1)S(1)} %get-tuple-element.18.refs_0_), channel_id=1, source_target_pairs={{0,64},{32,96},{64,0},{96,32},{1,65},{33,97},{65,1},{97,33},{2,66}... | collective-permute-start | bytes 442376 | tf_op jit(solution)/shard_map/rows_along_x/ppermute | solution.py:372
  25.0 0.0 collective-permute-start.1
  25.0 3.2 %collective-permute-start = (bf16[24,3072]{1,0:T(8,128)(2,1)S(1)}, bf16[24,3072]{1,0:T(8,128)(2,1)S(1)}, u32[]{:S(2)}, u32[]{:S(2)}) collective-permute-start(bf16[24,3072]{1,0:T(8,128)(2,1)S(1)} %get-tuple-element.18.refs_0_), channel_id=1, source_target_pairs={{0,32},{32,64},{64,96},{96,0},{1,33},{33,65},{65,97},{97,1},{2,34}... | collective-permute-start | bytes 442376 | tf_op jit(solution)/shard_map/rows_along_x/ppermute | solution.py:372
  28.2 0.0 slice-start
  28.2 0.0 slice-start.1
  28.2 4.8 %weights.1 = (bf16[6144,512]{1,0:T(8,128)(2,1)S(1)}, bf16[512,6144]{1,0:T(8,128)(2,1)S(1)}, f32[8,128]{1,0:T(8,128)S(1)}) custom-call(bf16[256,128]{1,0:T(8,128)(2,1)S(1)} %get-tuple-element.16.after.places, bf16[6144,512]{1,0:T(8,128)(2,1)} %bitcast.22, bf16[512,6144]{1,0:T(8,128)(2,1)} %bitcast.23), custom_call_target="tpu_custom_call" | custom-call | bytes 12582912 | tf_op jit(solution)/shard_map/weights/weights/pallas_call | solution.py:381
  33.1 0.0 collective-permute-done.2.refs_3_
  33.1 0.0 collective-permute-done.1.refs_2_
  33.1 0.0 collective-permute-done.refs_1_
  33.2 0.1 collective-permute-start.3
  33.3 2.0 %collective-permute-done.3.other = bf16[96,3072]{1,0:T(8,128)(2,1)S(1)} collective-permute-done((bf16[96,3072]{1,0:T(8,128)(2,1)S(1)}, bf16[96,3072]{1,0:T(8,128)(2,1)S(1)}, u32[]{:S(2)}, u32[]{:S(2)}) %collective-permute-start.3) | collective-permute-done | bytes 589856 | tf_op jit(solution)/shard_map/rows_between_cores/ppermute | solution.py:375
  35.2 0.0 slice-done
  35.2 0.0 slice-done.1
  35.2 3.3 %experts.1 = (bf16[48,512]{1,0:T(8,128)(2,1)S(1)}, bf16[96,3072]{1,0:T(8,128)(2,1)S(1)}) custom-call(bf16[96,3072]{1,0:T(8,128)(2,1)S(1)} %join.1.mine, bf16[96,3072]{1,0:T(8,128)(2,1)S(1)} %collective-permute-done.3.other, bf16[6144,512]{1,0:T(8,128)(2,1)S(1)} %bitcast.19, bf16[6144,512]{1,0:T(8,128)(2,1)S(1)} %get-tuple-element.19.w_up, ...), custom_call_target="tpu_custom_call" | custom-call | flops 1509949440 | bytes 18874368 | tf_op jit(solution)/shard_map/experts/experts/pallas_call | solution.py:406
  38.6 0.2 collective-permute-start.4
  38.8 1.2 %own_down.1 = f32[96,3072]{1,0:T(8,128)S(1)} custom-call(bf16[48,512]{1,0:T(8,128)(2,1)S(1)} %get-tuple-element.21.act, bf16[512,6144]{1,0:T(8,128)(2,1)S(1)} %get-tuple-element.20.w_down), custom_call_target="tpu_custom_call" | custom-call | flops 301989888 | bytes 6291456 | tf_op jit(solution)/shard_map/own_down/own_down/pallas_call | solution.py:421
  40.0 0.7 %collective-permute-done.4 = bf16[96,3072]{1,0:T(8,128)(2,1)S(1)} collective-permute-done((bf16[96,3072]{1,0:T(8,128)(2,1)S(1)}, bf16[96,3072]{1,0:T(8,128)(2,1)S(1)}, u32[]{:S(2)}, u32[]{:S(2)}) %collective-permute-start.4) | collective-permute-done | bytes 589856 | tf_op jit(solution)/shard_map/sums_between_cores/ppermute | solution.py:375
  40.7 0.1 add_convert_fusion
  40.8 1.0 %collective-permute-start.7 = (bf16[24,3072]{1,0:T(8,128)(2,1)S(1)}, bf16[24,3072]{1,0:T(8,128)(2,1)S(1)}, u32[]{:S(2)}, u32[]{:S(2)}) collective-permute-start(bf16[24,3072]{1,0:T(8,128)(2,1)S(1)} %get-tuple-element.25), channel_id=1, source_target_pairs={{0,64},{32,96},{64,0},{96,32},{1,65},{33,97},{65,1},{97,33},{2,66}... | collective-permute-start | bytes 442376 | tf_op jit(solution)/shard_map/sums_along_x/ppermute | solution.py:372
  41.8 1.4 %collective-permute-start.6 = (bf16[24,3072]{1,0:T(8,128)(2,1)S(1)}, bf16[24,3072]{1,0:T(8,128)(2,1)S(1)}, u32[]{:S(2)}, u32[]{:S(2)}) collective-permute-start(bf16[24,3072]{1,0:T(8,128)(2,1)S(1)} %get-tuple-element.26), channel_id=1, source_target_pairs={{0,96},{32,0},{64,32},{96,64},{1,97},{33,1},{65,33},{97,65},{2,98}... | collective-permute-start | bytes 442376 | tf_op jit(solution)/shard_map/sums_along_x/ppermute | solution.py:372
  43.2 1.8 %collective-permute-start.5 = (bf16[24,3072]{1,0:T(8,128)(2,1)S(1)}, bf16[24,3072]{1,0:T(8,128)(2,1)S(1)}, u32[]{:S(2)}, u32[]{:S(2)}) collective-permute-start(bf16[24,3072]{1,0:T(8,128)(2,1)S(1)} %get-tuple-element.27), channel_id=1, source_target_pairs={{0,32},{32,64},{64,96},{96,0},{1,33},{33,65},{65,97},{97,1},{2,34}... | collective-permute-start | bytes 442376 | tf_op jit(solution)/shard_map/sums_along_x/ppermute | solution.py:372
  45.0 4.1 %collective-permute-done.7.third = bf16[24,3072]{1,0:T(8,128)(2,1)S(1)} collective-permute-done((bf16[24,3072]{1,0:T(8,128)(2,1)S(1)}, bf16[24,3072]{1,0:T(8,128)(2,1)S(1)}, u32[]{:S(2)}, u32[]{:S(2)}) %collective-permute-start.7) | collective-permute-done | bytes 147488 | tf_op jit(solution)/shard_map/sums_along_x/ppermute | solution.py:372
  49.2 2.3 %collective-permute-done.6.second = bf16[24,3072]{1,0:T(8,128)(2,1)S(1)} collective-permute-done((bf16[24,3072]{1,0:T(8,128)(2,1)S(1)}, bf16[24,3072]{1,0:T(8,128)(2,1)S(1)}, u32[]{:S(2)}, u32[]{:S(2)}) %collective-permute-start.6) | collective-permute-done | bytes 147488 | tf_op jit(solution)/shard_map/sums_along_x/ppermute | solution.py:372
  51.5 0.0 collective-permute-done.5.first
  51.5 0.3 spread.1
  51.8 13.3 %all_to_all.11.received = bf16[16,16,768]{2,1,0:T(8,128)(2,1)S(1)} all-to-all(bf16[16,16,768]{2,1,0:T(8,128)(2,1)S(1)} %bitcast.21), channel_id=1, replica_groups=mesh['x'=4,'core'=2,'ep'=16] {'ep'}, dimensions={0} | all-to-all | bytes 786432 | tf_op jit(solution)/shard_map/sums_to_rows/all_to_all | solution.py:445
  65.1 0.8 %combine.1 = bf16[2,6144]{1,0:T(2,128)(2,1)} custom-call(bf16[16,16,768]{2,1,0:T(8,128)(2,1)S(1)} %all_to_all.11.received, bf16[16,768]{1,0:T(8,128)(2,1)S(1)} %get-tuple-element.23.stream, f32[16,128]{1,0:T(8,128)S(1)} %get-tuple-element.24.gates), custom_call_target="tpu_custom_call" | custom-call | tf_op jit(solution)/shard_map/combine/combine/pallas_call | solution.py:449
  (3 shorter events, 0.1 us)
Async XLA Ops:
  23.5 9.6 %collective-permute-start.2 = (bf16[24,3072]{1,0:T(8,128)(2,1)S(1)}, bf16[24,3072]{1,0:T(8,128)(2,1)S(1)}, u32[]{:S(2)}, u32[]{:S(2)}) collective-permute-start(bf16[24,3072]{1,0:T(8,128)(2,1)S(1)} %get-tuple-element.18.refs_0_), channel_id=1, source_target_pairs={{0,64},{32,96},{64,0},{96,32},{1,65},{33,97},{65,1},{97,33},{2,66}... | collective-permute-start | bytes 442376 | tf_op jit(solution)/shard_map/rows_along_x/ppermute | solution.py:372
  25.0 8.1 %collective-permute-start.1 = (bf16[24,3072]{1,0:T(8,128)(2,1)S(1)}, bf16[24,3072]{1,0:T(8,128)(2,1)S(1)}, u32[]{:S(2)}, u32[]{:S(2)}) collective-permute-start(bf16[24,3072]{1,0:T(8,128)(2,1)S(1)} %get-tuple-element.18.refs_0_), channel_id=1, source_target_pairs={{0,96},{32,0},{64,32},{96,64},{1,97},{33,1},{65,33},{97,65},{2,98}... | collective-permute-start | bytes 442376 | tf_op jit(solution)/shard_map/rows_along_x/ppermute | solution.py:372
  25.0 8.1 %collective-permute-start = (bf16[24,3072]{1,0:T(8,128)(2,1)S(1)}, bf16[24,3072]{1,0:T(8,128)(2,1)S(1)}, u32[]{:S(2)}, u32[]{:S(2)}) collective-permute-start(bf16[24,3072]{1,0:T(8,128)(2,1)S(1)} %get-tuple-element.18.refs_0_), channel_id=1, source_target_pairs={{0,32},{32,64},{64,96},{96,0},{1,33},{33,65},{65,97},{97,1},{2,34}... | collective-permute-start | bytes 442376 | tf_op jit(solution)/shard_map/rows_along_x/ppermute | solution.py:372
  28.2 7.0 %slice-start = ((s8[6291456]{0:T(1024)(128)(4,1)}), s8[4194304]{0:T(1024)(128)(4,1)S(1)}, s32[]{:S(2)}) async-start(s8[6291456]{0:T(1024)(128)(4,1)} %bitcast.17), calls=%async_computation.2 | async-start | bytes 8388608
  28.2 7.0 %slice-start.1 = ((s8[6291456]{0:T(1024)(128)(4,1)}), s8[2097152]{0:T(1024)(128)(4,1)S(1)}, s32[]{:S(2)}) async-start(s8[6291456]{0:T(1024)(128)(4,1)} %bitcast.17), calls=%async_computation.3 | async-start | bytes 4194304
  33.2 2.1 %collective-permute-start.3 = (bf16[96,3072]{1,0:T(8,128)(2,1)S(1)}, bf16[96,3072]{1,0:T(8,128)(2,1)S(1)}, u32[]{:S(2)}, u32[]{:S(2)}) collective-permute-start(bf16[96,3072]{1,0:T(8,128)(2,1)S(1)} %join.1.mine), channel_id=1, source_target_pairs={{0,16},{16,0},{1,17},{17,1},{2,18},{18,2},{3,19},{19,3},{4,20},{20... | collective-permute-start | bytes 1769480 | tf_op jit(solution)/shard_map/rows_between_cores/ppermute | solution.py:375
  38.6 2.1 %collective-permute-start.4 = (bf16[96,3072]{1,0:T(8,128)(2,1)S(1)}, bf16[96,3072]{1,0:T(8,128)(2,1)S(1)}, u32[]{:S(2)}, u32[]{:S(2)}) collective-permute-start(bf16[96,3072]{1,0:T(8,128)(2,1)S(1)} %get-tuple-element.22), channel_id=1, source_target_pairs={{0,16},{16,0},{1,17},{17,1},{2,18},{18,2},{3,19},{19,3},{4,20},{20... | collective-permute-start | bytes 1769480 | tf_op jit(solution)/shard_map/sums_between_cores/ppermute | solution.py:375
  40.8 8.3 %collective-permute-start.7 = (bf16[24,3072]{1,0:T(8,128)(2,1)S(1)}, bf16[24,3072]{1,0:T(8,128)(2,1)S(1)}, u32[]{:S(2)}, u32[]{:S(2)}) collective-permute-start(bf16[24,3072]{1,0:T(8,128)(2,1)S(1)} %get-tuple-element.25), channel_id=1, source_target_pairs={{0,64},{32,96},{64,0},{96,32},{1,65},{33,97},{65,1},{97,33},{2,66}... | collective-permute-start | bytes 442376 | tf_op jit(solution)/shard_map/sums_along_x/ppermute | solution.py:372
  41.8 9.7 %collective-permute-start.6 = (bf16[24,3072]{1,0:T(8,128)(2,1)S(1)}, bf16[24,3072]{1,0:T(8,128)(2,1)S(1)}, u32[]{:S(2)}, u32[]{:S(2)}) collective-permute-start(bf16[24,3072]{1,0:T(8,128)(2,1)S(1)} %get-tuple-element.26), channel_id=1, source_target_pairs={{0,96},{32,0},{64,32},{96,64},{1,97},{33,1},{65,33},{97,65},{2,98}... | collective-permute-start | bytes 442376 | tf_op jit(solution)/shard_map/sums_along_x/ppermute | solution.py:372
  43.2 8.2 %collective-permute-start.5 = (bf16[24,3072]{1,0:T(8,128)(2,1)S(1)}, bf16[24,3072]{1,0:T(8,128)(2,1)S(1)}, u32[]{:S(2)}, u32[]{:S(2)}) collective-permute-start(bf16[24,3072]{1,0:T(8,128)(2,1)S(1)} %get-tuple-element.27), channel_id=1, source_target_pairs={{0,32},{32,64},{64,96},{96,0},{1,33},{33,65},{65,97},{97,1},{2,34}... | collective-permute-start | bytes 442376 | tf_op jit(solution)/shard_map/sums_along_x/ppermute | solution.py:372

commit v4 on v3

--- a/solution.py
+++ b/solution.py
@@ -12,7 +12,7 @@
 CAP = 6
 CORES = 2
 LANES = 128
-PARTS = 8
+PARTS = 4
 EPSILON = 1e-05
 
 VMEM = pl.BlockSpec(memory_space=pltpu.VMEM)
@@ -28,7 +28,7 @@
     expert, lengths_at, ids_at, query_at, residual_at, new_key_at, new_value_at, keys, values, gain_at,
     router_at, send, stream_out, gates_out,
     lengths, ids, query, residual, new_key, new_value, gain, router,
-    key_buf, value_buf, spread, rows, packed, sems, small_sems,
+    key_buf, value_buf, spread, mixed, base, scale, chunk, sems, small_sems,
 ):
     batches, features = query.shape
     heads = features // HEAD
@@ -58,86 +58,96 @@
             )
         )
     ]
-    for copy in small[:3]:
+    for copy in [small[0]] + [pair[0] for pair in copies] + small[1:]:
         copy.start()
-    for copy in copies[0]:
-        copy.start()
-    for copy in small[3:]:
-        copy.start()
-    for pair in copies[1:]:
-        for copy in pair:
-            copy.start()
-    rows[...] = jnp.zeros_like(rows)
+    for pair in copies:
+        pair[1].start()
     spread[...] = jnp.zeros_like(spread)
-    for copy in small:
-        copy.wait()
+    small[0].wait()
     query_wide = query[...].astype(jnp.float32)
-    key_wide = new_key[...].astype(jnp.float32)
-    value_wide = new_value[...].astype(jnp.float32)
     for row in range(batches):
         for head in range(heads):
             block, place = head // group, head % group
             spread[row, pl.ds(8 * block + place, 1), pl.ds(HEAD * block, HEAD)] = query_wide[
                 row : row + 1, HEAD * head : HEAD * (head + 1)
             ]
-    for row in range(batches):
-        queries = spread[row]
-        own = jnp.sum(queries * key_wide[row : row + 1], axis=1, keepdims=True) * HEAD**-0.5
+    scores = []
+    for row in range(batches):
         copies[row][0].wait()
-        scores = (
+        scores.append(
             lax.dot_general(
-                queries.astype(jnp.bfloat16),
+                spread[row].astype(jnp.bfloat16),
                 key_buf[row],
                 (((1,), (1,)), ((), ())),
                 preferred_element_type=jnp.float32,
             )
-            * HEAD**-0.5
-        )
-        scores = jnp.where(iota(scores.shape, 1) < lengths[row], scores, -jnp.inf)
-        peak = jnp.maximum(jnp.max(scores, axis=1, keepdims=True), own)
-        terms = jnp.exp(scores - peak)
+        )
+    for copy in small[1:]:
+        copy.wait()
+    key_wide = new_key[...].astype(jnp.float32)
+    value_wide = new_value[...].astype(jnp.float32)
+    residual_wide = residual[...].astype(jnp.float32)
+    router_wide = router[...].astype(jnp.float32)
+    for row in range(batches):
+        for part in range(PARTS):
+            start, place = part * piece, row * PARTS + part
+            at = pl.ds(place, 1)
+            base[at, :] = residual_wide[row : row + 1, start : start + piece]
+            scale[at, :] = gain[:, start : start + piece]
+        lane = iota((PARTS, LANES), 1)
+        names = jnp.where(lane == 0, ids[row, 0], jnp.where(lane == 1, ids[row, 1], 0))
+        chunk[pl.ds(row * PARTS, PARTS), piece : piece + LANES] = names.astype(jnp.float32)
+    shares = []
+    for row in range(batches):
+        own = jnp.sum(spread[row] * key_wide[row : row + 1], axis=1, keepdims=True) * HEAD**-0.5
+        score = scores[row] * HEAD**-0.5
+        score = jnp.where(iota(score.shape, 1) < lengths[row], score, -jnp.inf)
+        peak = jnp.maximum(jnp.max(score, axis=1, keepdims=True), own)
+        terms = jnp.exp(score - peak)
         own_term = jnp.exp(own - peak)
         total = jnp.sum(terms, axis=1, keepdims=True) + own_term
         weights = (terms / total).astype(jnp.bfloat16)
         own_weight = (own_term / total).astype(jnp.bfloat16).astype(jnp.float32)
+        shares.append((weights, own_weight))
+    for row in range(batches):
+        weights, own_weight = shares[row]
         copies[row][1].wait()
         mixture = jnp.dot(weights, value_buf[row], preferred_element_type=jnp.float32)
         mixture = mixture + own_weight * value_wide[row : row + 1]
         for head in range(heads):
             block, place = head // group, head % group
-            rows[row : row + 1, HEAD * head : HEAD * (head + 1)] = mixture[
+            part, start = HEAD * head // piece, HEAD * head % piece
+            mixed[pl.ds(row * PARTS + part, 1), pl.ds(start, HEAD)] = mixture[
                 8 * block + place : 8 * block + place + 1, HEAD * block : HEAD * (block + 1)
             ]
-    attended = rows[0:batches].astype(jnp.bfloat16).astype(jnp.float32)
-    stream = (residual[...].astype(jnp.float32) + attended).astype(jnp.bfloat16)
+    attended = mixed[...].astype(jnp.bfloat16).astype(jnp.float32)
+    stream = (base[...] + attended).astype(jnp.bfloat16)
+    stream_out[...] = stream
     stream = stream.astype(jnp.float32)
-    mean_square = jnp.sum(stream * stream, axis=1, keepdims=True) * (1.0 / features)
-    normed = (stream * lax.rsqrt(mean_square + EPSILON) * gain[...]).astype(jnp.bfloat16)
+    squares = jnp.sum(stream * stream, axis=1, keepdims=True)
+    owner = iota(squares.shape, 0) // PARTS
+    mean_square = jnp.zeros_like(squares)
+    for row in range(batches):
+        total = jnp.sum(jnp.where(owner == row, squares, 0.0), axis=0, keepdims=True)
+        mean_square = jnp.where(owner == row, total * (1.0 / features), mean_square)
+    normed = (stream * lax.rsqrt(mean_square + EPSILON) * scale[...]).astype(jnp.bfloat16)
     normed = normed.astype(jnp.float32)
-    rows[0:batches] = normed
-    logits = lax.dot_general(
-        rows[...].astype(jnp.bfloat16),
-        router[...],
-        (((1,), (1,)), ((), ())),
-        preferred_element_type=jnp.float32,
-    )
-    for row in range(batches):
+    chunk[:, 0:piece] = normed
+    sent = chunk[...].astype(jnp.bfloat16)
+    for peer in range(peers):
+        send[peer] = sent
+    for row in range(batches):
+        logits = jnp.zeros((router.shape[0], 1), jnp.float32)
         for part in range(PARTS):
-            start, place = part * piece, row * PARTS + part
-            packed[0, pl.ds(place, 1), 0:piece] = normed[row : row + 1, start : start + piece]
-            packed[1, pl.ds(place, 1), 0:piece] = stream[row : row + 1, start : start + piece]
-        lane = iota((PARTS, LANES), 1)
-        names = jnp.where(lane == 0, ids[row, 0], jnp.where(lane == 1, ids[row, 1], 0))
-        packed[0, pl.ds(row * PARTS, PARTS), piece : piece + LANES] = names.astype(jnp.float32)
-    chunk = packed[0].astype(jnp.bfloat16)
-    for peer in range(peers):
-        send[peer] = chunk
-    stream_out[...] = packed[1, :, 0:piece].astype(jnp.bfloat16)
-    for row in range(batches):
-        lane = iota((1, logits.shape[1]), 1)
-        own = logits[row : row + 1]
-        first = jnp.sum(jnp.where(lane == ids[row, 0], own, 0.0), axis=1, keepdims=True)
-        second = jnp.sum(jnp.where(lane == ids[row, 1], own, 0.0), axis=1, keepdims=True)
+            place = row * PARTS + part
+            logits += jnp.sum(
+                router_wide[:, part * piece : (part + 1) * piece] * normed[place : place + 1],
+                axis=1,
+                keepdims=True,
+            )
+        name = iota(logits.shape, 0)
+        first = jnp.sum(jnp.where(name == ids[row, 0], logits, 0.0), axis=0, keepdims=True)
+        second = jnp.sum(jnp.where(name == ids[row, 1], logits, 0.0), axis=0, keepdims=True)
         larger = jnp.maximum(first, second)
         first, second = jnp.exp(first - larger), jnp.exp(second - larger)
         total = first + second
@@ -333,8 +343,10 @@
                 pltpu.VMEM((batches, context, kv_width), bf16),
                 pltpu.VMEM((batches, context, kv_width), bf16),
                 pltpu.VMEM((batches, 8 * KV_HEADS, kv_width), f32),
-                pltpu.VMEM((8, features), f32),
-                pltpu.VMEM((2, pack, piece + LANES), f32),
+                pltpu.VMEM((pack, piece), f32),
+                pltpu.VMEM((pack, piece), f32),
+                pltpu.VMEM((pack, piece), f32),
+                pltpu.VMEM((pack, piece + LANES), f32),
                 pltpu.SemaphoreType.DMA((2 * batches,)),
                 pltpu.SemaphoreType.DMA((8,)),
             ],

time: 66.6 us -> 65.4 us (0.982)
  Pallas kernels: 15.3 us -> 14.4 us
    pallas_call x1, Pallas kernels: 4.32 us -> 3.47 us  [shards(): pl.pallas_call(attention_kernel, out_shape=(jax.ShapeDtypeStruct((peers,...]
where the time goes in v4:
time: 65.4 us; the launch traced here: 64.6 us
  blocking collectives  31.5 us (48%)
  Pallas kernels  14.4 us (22%)
  starting transfers between devices  9.23 us (14%)
  waiting for transfers between devices  9.08 us (14%)
    all_to_all x1, blocking collectives, shards(): received = lax.all_to_all(send, 'ep', 0, 0, tiled=True)  18 us
    all_to_all x1, blocking collectives, shards(): lax.all_to_all(send.reshape(peers, pack, piece), 'ep', 0, 0, tiled=True)  13.5 us
    ppermute x6, starting transfers between devices, along(): return lax.ppermute(array, 'x', [(i, (i + step) % xs) for i in range(xs)])  8.94 us
    ppermute x6, waiting for transfers between devices, along(): return lax.ppermute(array, 'x', [(i, (i + step) % xs) for i in range(xs)])  6.42 us
    pallas_call x1, Pallas kernels, shards(): pl.pallas_call(fetch_kernel, out_shape=tuple((pltpu.VMEM(w.shape[1:], bf1...  4.84 us
    pallas_call x1, Pallas kernels, shards(): pl.pallas_call(attention_kernel, out_shape=(jax.ShapeDtypeStruct((peers,...  3.47 us
    pallas_call x1, Pallas kernels, shards(): pl.pallas_call(expert_kernel, out_shape=(jax.ShapeDtypeStruct((rows_here,...  3.32 us
    ppermute x2, waiting for transfers between devices, swap(): return lax.ppermute(array, 'core', [(0, 1), (1, 0)])  2.66 us
  transfers between devices with their start and end apart: 8, of which 4 were waited for; matrix products, arithmetic and copies ran while one was open for 0% of the time, Pallas kernels for 9%

profile of v4, /device:TPU:6, one launch (start us, length us, event | category | flops | bytes accessed | tf_op | source)
XLA Modules:
  0.0 64.6 jit_solution(18220199906508683198)
XLA Ops:
  0.0 3.5 %attention.1 = (bf16[16,8,1664]{2,1,0:T(8,128)(2,1)S(1)}, bf16[8,1536]{1,0:T(8,128)(2,1)S(1)}, f32[8,128]{1,0:T(8,128)S(1)}) custom-call(s32[1]{0:T(128)} %bitcast.expert, s32[2]{0:T(128)} %bitcast.33, s32[2,2]{1,0:T(2,128)} %bitcast.32, bf16[2,6144]{1,0:T(2,128)(2,1)} %bitcast.27, bf16[2,6144]{1,0:T(2,128)(2,1)} %bitcast.28, bf16[2,1024]{1,0:T(2,128)(2,1)} %bitcast.30, ...), custom_call_target="tpu_custom_call" | custom-call | tf_op jit(solution)/shard_map/attention/attention/pallas_call | solution.py:325
  3.5 18.0 %all_to_all.10 = bf16[16,8,1664]{2,1,0:T(8,128)(2,1)S(1)} all-to-all(bf16[16,8,1664]{2,1,0:T(8,128)(2,1)S(1)} %get-tuple-element.15), channel_id=1, replica_groups=mesh['x'=4,'core'=2,'ep'=16] {'ep'}, dimensions={0} | all-to-all | bytes 851968 | tf_op jit(solution)/shard_map/rows_to_experts/all_to_all | solution.py:369
  21.5 0.5 select.5
  22.0 1.5 %collective-permute-start.2 = (bf16[24,3072]{1,0:T(8,128)(2,1)S(1)}, bf16[24,3072]{1,0:T(8,128)(2,1)S(1)}, u32[]{:S(2)}, u32[]{:S(2)}) collective-permute-start(bf16[24,3072]{1,0:T(8,128)(2,1)S(1)} %get-tuple-element.18.refs_0_), channel_id=1, source_target_pairs={{0,64},{32,96},{64,0},{96,32},{1,65},{33,97},{65,1},{97,33},{2,66}... | collective-permute-start | bytes 442376 | tf_op jit(solution)/shard_map/rows_along_x/ppermute | solution.py:384
  23.5 0.0 collective-permute-start.1
  23.5 3.2 %collective-permute-start = (bf16[24,3072]{1,0:T(8,128)(2,1)S(1)}, bf16[24,3072]{1,0:T(8,128)(2,1)S(1)}, u32[]{:S(2)}, u32[]{:S(2)}) collective-permute-start(bf16[24,3072]{1,0:T(8,128)(2,1)S(1)} %get-tuple-element.18.refs_0_), channel_id=1, source_target_pairs={{0,32},{32,64},{64,96},{96,0},{1,33},{33,65},{65,97},{97,1},{2,34}... | collective-permute-start | bytes 442376 | tf_op jit(solution)/shard_map/rows_along_x/ppermute | solution.py:384
  26.7 0.0 slice-start
  26.7 0.0 slice-start.1
  26.7 4.8 %weights.1 = (bf16[6144,512]{1,0:T(8,128)(2,1)S(1)}, bf16[512,6144]{1,0:T(8,128)(2,1)S(1)}, f32[8,128]{1,0:T(8,128)S(1)}) custom-call(bf16[128,128]{1,0:T(8,128)(2,1)S(1)} %get-tuple-element.16.after.places, bf16[6144,512]{1,0:T(8,128)(2,1)} %bitcast.22, bf16[512,6144]{1,0:T(8,128)(2,1)} %bitcast.23), custom_call_target="tpu_custom_call" | custom-call | bytes 12582912 | tf_op jit(solution)/shard_map/weights/weights/pallas_call | solution.py:393
  31.6 0.0 collective-permute-done.2.refs_3_
  31.6 0.0 collective-permute-done.1.refs_2_
  31.6 0.0 collective-permute-done.refs_1_
  31.6 0.1 collective-permute-start.3
  31.7 2.0 %collective-permute-done.3.other = bf16[96,3072]{1,0:T(8,128)(2,1)S(1)} collective-permute-done((bf16[96,3072]{1,0:T(8,128)(2,1)S(1)}, bf16[96,3072]{1,0:T(8,128)(2,1)S(1)}, u32[]{:S(2)}, u32[]{:S(2)}) %collective-permute-start.3) | collective-permute-done | bytes 589856 | tf_op jit(solution)/shard_map/rows_between_cores/ppermute | solution.py:387
  33.7 0.0 slice-done
  33.7 0.0 slice-done.1
  33.7 3.3 %experts.1 = (bf16[48,512]{1,0:T(8,128)(2,1)S(1)}, bf16[96,3072]{1,0:T(8,128)(2,1)S(1)}) custom-call(bf16[96,3072]{1,0:T(8,128)(2,1)S(1)} %join.1.mine, bf16[96,3072]{1,0:T(8,128)(2,1)S(1)} %collective-permute-done.3.other, bf16[6144,512]{1,0:T(8,128)(2,1)S(1)} %bitcast.19, bf16[6144,512]{1,0:T(8,128)(2,1)S(1)} %get-tuple-element.19.w_up, ...), custom_call_target="tpu_custom_call" | custom-call | flops 1509949440 | bytes 18874368 | tf_op jit(solution)/shard_map/experts/experts/pallas_call | solution.py:418
  37.1 0.2 collective-permute-start.4
  37.3 1.2 %own_down.1 = f32[96,3072]{1,0:T(8,128)S(1)} custom-call(bf16[48,512]{1,0:T(8,128)(2,1)S(1)} %get-tuple-element.21.act, bf16[512,6144]{1,0:T(8,128)(2,1)S(1)} %get-tuple-element.20.w_down), custom_call_target="tpu_custom_call" | custom-call | flops 301989888 | bytes 6291456 | tf_op jit(solution)/shard_map/own_down/own_down/pallas_call | solution.py:433
  38.5 0.7 %collective-permute-done.4 = bf16[96,3072]{1,0:T(8,128)(2,1)S(1)} collective-permute-done((bf16[96,3072]{1,0:T(8,128)(2,1)S(1)}, bf16[96,3072]{1,0:T(8,128)(2,1)S(1)}, u32[]{:S(2)}, u32[]{:S(2)}) %collective-permute-start.4) | collective-permute-done | bytes 589856 | tf_op jit(solution)/shard_map/sums_between_cores/ppermute | solution.py:387
  39.1 0.1 add_convert_fusion
  39.3 1.0 %collective-permute-start.7 = (bf16[24,3072]{1,0:T(8,128)(2,1)S(1)}, bf16[24,3072]{1,0:T(8,128)(2,1)S(1)}, u32[]{:S(2)}, u32[]{:S(2)}) collective-permute-start(bf16[24,3072]{1,0:T(8,128)(2,1)S(1)} %get-tuple-element.25), channel_id=1, source_target_pairs={{0,64},{32,96},{64,0},{96,32},{1,65},{33,97},{65,1},{97,33},{2,66}... | collective-permute-start | bytes 442376 | tf_op jit(solution)/shard_map/sums_along_x/ppermute | solution.py:384
  40.3 1.4 %collective-permute-start.6 = (bf16[24,3072]{1,0:T(8,128)(2,1)S(1)}, bf16[24,3072]{1,0:T(8,128)(2,1)S(1)}, u32[]{:S(2)}, u32[]{:S(2)}) collective-permute-start(bf16[24,3072]{1,0:T(8,128)(2,1)S(1)} %get-tuple-element.26), channel_id=1, source_target_pairs={{0,96},{32,0},{64,32},{96,64},{1,97},{33,1},{65,33},{97,65},{2,98}... | collective-permute-start | bytes 442376 | tf_op jit(solution)/shard_map/sums_along_x/ppermute | solution.py:384
  41.7 1.8 %collective-permute-start.5 = (bf16[24,3072]{1,0:T(8,128)(2,1)S(1)}, bf16[24,3072]{1,0:T(8,128)(2,1)S(1)}, u32[]{:S(2)}, u32[]{:S(2)}) collective-permute-start(bf16[24,3072]{1,0:T(8,128)(2,1)S(1)} %get-tuple-element.27), channel_id=1, source_target_pairs={{0,32},{32,64},{64,96},{96,0},{1,33},{33,65},{65,97},{97,1},{2,34}... | collective-permute-start | bytes 442376 | tf_op jit(solution)/shard_map/sums_along_x/ppermute | solution.py:384
  43.6 4.1 %collective-permute-done.7.third = bf16[24,3072]{1,0:T(8,128)(2,1)S(1)} collective-permute-done((bf16[24,3072]{1,0:T(8,128)(2,1)S(1)}, bf16[24,3072]{1,0:T(8,128)(2,1)S(1)}, u32[]{:S(2)}, u32[]{:S(2)}) %collective-permute-start.7) | collective-permute-done | bytes 147488 | tf_op jit(solution)/shard_map/sums_along_x/ppermute | solution.py:384
  47.7 2.3 %collective-permute-done.6.second = bf16[24,3072]{1,0:T(8,128)(2,1)S(1)} collective-permute-done((bf16[24,3072]{1,0:T(8,128)(2,1)S(1)}, bf16[24,3072]{1,0:T(8,128)(2,1)S(1)}, u32[]{:S(2)}, u32[]{:S(2)}) %collective-permute-start.6) | collective-permute-done | bytes 147488 | tf_op jit(solution)/shard_map/sums_along_x/ppermute | solution.py:384
  50.0 0.0 collective-permute-done.5.first
  50.0 0.3 spread.1
  50.2 13.5 %all_to_all.11.received = bf16[16,8,1536]{2,1,0:T(8,128)(2,1)S(1)} all-to-all(bf16[16,8,1536]{2,1,0:T(8,128)(2,1)S(1)} %bitcast.21), channel_id=1, replica_groups=mesh['x'=4,'core'=2,'ep'=16] {'ep'}, dimensions={0} | all-to-all | bytes 786432 | tf_op jit(solution)/shard_map/sums_to_rows/all_to_all | solution.py:457
  63.8 0.8 %combine.1 = bf16[2,6144]{1,0:T(2,128)(2,1)} custom-call(bf16[16,8,1536]{2,1,0:T(8,128)(2,1)S(1)} %all_to_all.11.received, bf16[8,1536]{1,0:T(8,128)(2,1)S(1)} %get-tuple-element.23.stream, f32[8,128]{1,0:T(8,128)S(1)} %get-tuple-element.24.gates), custom_call_target="tpu_custom_call" | custom-call | tf_op jit(solution)/shard_map/combine/combine/pallas_call | solution.py:461
  (3 shorter events, 0.1 us)
Async XLA Ops:
  22.0 9.6 %collective-permute-start.2 = (bf16[24,3072]{1,0:T(8,128)(2,1)S(1)}, bf16[24,3072]{1,0:T(8,128)(2,1)S(1)}, u32[]{:S(2)}, u32[]{:S(2)}) collective-permute-start(bf16[24,3072]{1,0:T(8,128)(2,1)S(1)} %get-tuple-element.18.refs_0_), channel_id=1, source_target_pairs={{0,64},{32,96},{64,0},{96,32},{1,65},{33,97},{65,1},{97,33},{2,66}... | collective-permute-start | bytes 442376 | tf_op jit(solution)/shard_map/rows_along_x/ppermute | solution.py:384
  23.5 8.1 %collective-permute-start.1 = (bf16[24,3072]{1,0:T(8,128)(2,1)S(1)}, bf16[24,3072]{1,0:T(8,128)(2,1)S(1)}, u32[]{:S(2)}, u32[]{:S(2)}) collective-permute-start(bf16[24,3072]{1,0:T(8,128)(2,1)S(1)} %get-tuple-element.18.refs_0_), channel_id=1, source_target_pairs={{0,96},{32,0},{64,32},{96,64},{1,97},{33,1},{65,33},{97,65},{2,98}... | collective-permute-start | bytes 442376 | tf_op jit(solution)/shard_map/rows_along_x/ppermute | solution.py:384
  23.5 8.1 %collective-permute-start = (bf16[24,3072]{1,0:T(8,128)(2,1)S(1)}, bf16[24,3072]{1,0:T(8,128)(2,1)S(1)}, u32[]{:S(2)}, u32[]{:S(2)}) collective-permute-start(bf16[24,3072]{1,0:T(8,128)(2,1)S(1)} %get-tuple-element.18.refs_0_), channel_id=1, source_target_pairs={{0,32},{32,64},{64,96},{96,0},{1,33},{33,65},{65,97},{97,1},{2,34}... | collective-permute-start | bytes 442376 | tf_op jit(solution)/shard_map/rows_along_x/ppermute | solution.py:384
  26.7 7.0 %slice-start = ((s8[6291456]{0:T(1024)(128)(4,1)}), s8[4194304]{0:T(1024)(128)(4,1)S(1)}, s32[]{:S(2)}) async-start(s8[6291456]{0:T(1024)(128)(4,1)} %bitcast.17), calls=%async_computation.2 | async-start | bytes 8388608
  26.7 7.0 %slice-start.1 = ((s8[6291456]{0:T(1024)(128)(4,1)}), s8[2097152]{0:T(1024)(128)(4,1)S(1)}, s32[]{:S(2)}) async-start(s8[6291456]{0:T(1024)(128)(4,1)} %bitcast.17), calls=%async_computation.3 | async-start | bytes 4194304
  31.6 2.1 %collective-permute-start.3 = (bf16[96,3072]{1,0:T(8,128)(2,1)S(1)}, bf16[96,3072]{1,0:T(8,128)(2,1)S(1)}, u32[]{:S(2)}, u32[]{:S(2)}) collective-permute-start(bf16[96,3072]{1,0:T(8,128)(2,1)S(1)} %join.1.mine), channel_id=1, source_target_pairs={{0,16},{16,0},{1,17},{17,1},{2,18},{18,2},{3,19},{19,3},{4,20},{20... | collective-permute-start | bytes 1769480 | tf_op jit(solution)/shard_map/rows_between_cores/ppermute | solution.py:387
  37.1 2.1 %collective-permute-start.4 = (bf16[96,3072]{1,0:T(8,128)(2,1)S(1)}, bf16[96,3072]{1,0:T(8,128)(2,1)S(1)}, u32[]{:S(2)}, u32[]{:S(2)}) collective-permute-start(bf16[96,3072]{1,0:T(8,128)(2,1)S(1)} %get-tuple-element.22), channel_id=1, source_target_pairs={{0,16},{16,0},{1,17},{17,1},{2,18},{18,2},{3,19},{19,3},{4,20},{20... | collective-permute-start | bytes 1769480 | tf_op jit(solution)/shard_map/sums_between_cores/ppermute | solution.py:387
  39.3 8.3 %collective-permute-start.7 = (bf16[24,3072]{1,0:T(8,128)(2,1)S(1)}, bf16[24,3072]{1,0:T(8,128)(2,1)S(1)}, u32[]{:S(2)}, u32[]{:S(2)}) collective-permute-start(bf16[24,3072]{1,0:T(8,128)(2,1)S(1)} %get-tuple-element.25), channel_id=1, source_target_pairs={{0,64},{32,96},{64,0},{96,32},{1,65},{33,97},{65,1},{97,33},{2,66}... | collective-permute-start | bytes 442376 | tf_op jit(solution)/shard_map/sums_along_x/ppermute | solution.py:384
  40.3 9.6 %collective-permute-start.6 = (bf16[24,3072]{1,0:T(8,128)(2,1)S(1)}, bf16[24,3072]{1,0:T(8,128)(2,1)S(1)}, u32[]{:S(2)}, u32[]{:S(2)}) collective-permute-start(bf16[24,3072]{1,0:T(8,128)(2,1)S(1)} %get-tuple-element.26), channel_id=1, source_target_pairs={{0,96},{32,0},{64,32},{96,64},{1,97},{33,1},{65,33},{97,65},{2,98}... | collective-permute-start | bytes 442376 | tf_op jit(solution)/shard_map/sums_along_x/ppermute | solution.py:384
  41.7 8.2 %collective-permute-start.5 = (bf16[24,3072]{1,0:T(8,128)(2,1)S(1)}, bf16[24,3072]{1,0:T(8,128)(2,1)S(1)}, u32[]{:S(2)}, u32[]{:S(2)}) collective-permute-start(bf16[24,3072]{1,0:T(8,128)(2,1)S(1)} %get-tuple-element.27), channel_id=1, source_target_pairs={{0,32},{32,64},{64,96},{96,0},{1,33},{33,65},{65,97},{97,1},{2,34}... | collective-permute-start | bytes 442376 | tf_op jit(solution)/shard_map/sums_along_x/ppermute | solution.py:384

commit v5 on v4

--- a/solution.py
+++ b/solution.py
@@ -26,8 +26,8 @@
 
 def attention_kernel(
     expert, lengths_at, ids_at, query_at, residual_at, new_key_at, new_value_at, keys, values, gain_at,
-    router_at, send, stream_out, gates_out,
-    lengths, ids, query, residual, new_key, new_value, gain, router,
+    send, stream_out,
+    lengths, ids, query, residual, new_key, new_value, gain,
     key_buf, value_buf, spread, mixed, base, scale, chunk, sems, small_sems,
 ):
     batches, features = query.shape
@@ -52,7 +52,6 @@
                 (new_value_at, new_value),
                 (residual_at, residual),
                 (gain_at, gain),
-                (router_at, router),
                 (lengths_at, lengths),
                 (ids_at, ids),
             )
@@ -87,7 +86,6 @@
     key_wide = new_key[...].astype(jnp.float32)
     value_wide = new_value[...].astype(jnp.float32)
     residual_wide = residual[...].astype(jnp.float32)
-    router_wide = router[...].astype(jnp.float32)
     for row in range(batches):
         for part in range(PARTS):
             start, place = part * piece, row * PARTS + part
@@ -136,27 +134,6 @@
     sent = chunk[...].astype(jnp.bfloat16)
     for peer in range(peers):
         send[peer] = sent
-    for row in range(batches):
-        logits = jnp.zeros((router.shape[0], 1), jnp.float32)
-        for part in range(PARTS):
-            place = row * PARTS + part
-            logits += jnp.sum(
-                router_wide[:, part * piece : (part + 1) * piece] * normed[place : place + 1],
-                axis=1,
-                keepdims=True,
-            )
-        name = iota(logits.shape, 0)
-        first = jnp.sum(jnp.where(name == ids[row, 0], logits, 0.0), axis=0, keepdims=True)
-        second = jnp.sum(jnp.where(name == ids[row, 1], logits, 0.0), axis=0, keepdims=True)
-        larger = jnp.maximum(first, second)
-        first, second = jnp.exp(first - larger), jnp.exp(second - larger)
-        total = first + second
-        expert = iota((PARTS, LANES), 1) // 2
-        gates_out[pl.ds(row * PARTS, PARTS), :] = jnp.where(
-            expert == ids[row, 0],
-            first / total,
-            jnp.where(expert == ids[row, 1], second / total, 0.0),
-        )
 
 
 def select_kernel(expert, received, chosen_out, places_out):
@@ -197,7 +174,7 @@
         ].astype(jnp.bfloat16)
 
 
-def fetch_kernel(after, up_at, down_at, up, down, ready, sems):
+def fetch_kernel(after, sent, router, up_at, down_at, up, down, gates_out, sems):
     pieces = 4
     copies = []
     for source, target in ((up_at, up), (down_at, down)):
@@ -209,7 +186,32 @@
             )
     for copy in copies:
         copy.start()
-    ready[...] = jnp.zeros_like(ready)
+    piece = sent.shape[2] - LANES
+    normed = sent[0, :, 0:piece].astype(jnp.float32)
+    names = sent[0, :, piece:].astype(jnp.float32)
+    router_wide = router[...].astype(jnp.float32)
+    for row in range(normed.shape[0] // PARTS):
+        logits = jnp.zeros((router.shape[0], 1), jnp.float32)
+        for part in range(PARTS):
+            place = row * PARTS + part
+            logits += jnp.sum(
+                router_wide[:, part * piece : (part + 1) * piece] * normed[place : place + 1],
+                axis=1,
+                keepdims=True,
+            )
+        at = row * PARTS
+        expert = iota(logits.shape, 0).astype(jnp.float32)
+        ids = [names[at : at + 1, turn : turn + 1] for turn in range(2)]
+        first, second = (
+            jnp.sum(jnp.where(expert == name, logits, 0.0), axis=0, keepdims=True) for name in ids
+        )
+        larger = jnp.maximum(first, second)
+        first, second = jnp.exp(first - larger), jnp.exp(second - larger)
+        total = first + second
+        holder = (iota((PARTS, LANES), 1) // 2).astype(jnp.float32)
+        gates_out[pl.ds(at, PARTS), :] = jnp.where(
+            holder == ids[0], first / total, jnp.where(holder == ids[1], second / total, 0.0)
+        )
     for copy in copies:
         copy.wait()
 
@@ -322,15 +324,14 @@
         return pl.CostEstimate(flops=flops, bytes_accessed=moved, transcendentals=0)
 
     with jax.named_scope("attention"):
-        send, stream, gates = pl.pallas_call(
+        send, stream = pl.pallas_call(
             attention_kernel,
             out_shape=(
                 jax.ShapeDtypeStruct((peers, pack, piece + LANES), bf16),
                 jax.ShapeDtypeStruct((pack, piece), bf16),
-                jax.ShapeDtypeStruct((pack, LANES), f32),
             ),
-            in_specs=[SMEM] + [ANY] * 10,
-            out_specs=(VMEM, VMEM, VMEM),
+            in_specs=[SMEM] + [ANY] * 9,
+            out_specs=(VMEM, VMEM),
             scratch_shapes=[
                 pltpu.SMEM((batches,), jnp.int32),
                 pltpu.SMEM((batches, 2), jnp.int32),
@@ -339,7 +340,6 @@
                 pltpu.VMEM((batches, kv_width), bf16),
                 pltpu.VMEM((batches, kv_width), bf16),
                 pltpu.VMEM((1, features), f32),
-                pltpu.VMEM(router.shape[::-1], bf16),
                 pltpu.VMEM((batches, context, kv_width), bf16),
                 pltpu.VMEM((batches, context, kv_width), bf16),
                 pltpu.VMEM((batches, 8 * KV_HEADS, kv_width), f32),
@@ -363,7 +363,6 @@
             in_hbm(key_cache.reshape(batches, context, kv_width)),
             in_hbm(value_cache.reshape(batches, context, kv_width)),
             in_hbm(norm_gain.reshape(1, features)),
-            in_hbm(router.T),
         )
     with jax.named_scope("rows_to_experts"):
         received = lax.all_to_all(send, "ep", 0, 0, tiled=True)
@@ -387,20 +386,20 @@
         return lax.ppermute(array, "core", [(0, 1), (1, 0)])
 
     with jax.named_scope("rows_along_x"):
-        steps = (1, xs - 1) + tuple(range(2, xs - 1))
+        steps = tuple(range(2, xs - 1)) + (xs - 1, 1)
         parts = [chosen] + [along(chosen, step) for step in steps]
     with jax.named_scope("weights"):
-        up_here, down_here, ready = pl.pallas_call(
+        up_here, down_here, gates = pl.pallas_call(
             fetch_kernel,
             out_shape=tuple(pltpu.VMEM(w.shape[1:], bf16) for w in (w_up, w_down))
-            + (jax.ShapeDtypeStruct((8, LANES), f32),),
-            in_specs=[VMEM] + [ANY] * 2,
+            + (jax.ShapeDtypeStruct((pack, LANES), f32),),
+            in_specs=[VMEM] * 3 + [ANY] * 2,
             out_specs=(VMEM,) * 3,
             scratch_shapes=[pltpu.SemaphoreType.DMA((8,))],
             compiler_params=pltpu.CompilerParams(vmem_limit_bytes=2**20),
             cost_estimate=cost(0, 4 * w_gate.size),
             name="weights",
-        )(places, in_hbm(w_up[0]), in_hbm(w_down[0]))
+        )(places, send, router.T, in_hbm(w_up[0]), in_hbm(w_down[0]))
     with jax.named_scope("join"):
         mine = pl.pallas_call(
             join_kernel,
@@ -409,7 +408,7 @@
             out_specs=VMEM,
             compiler_params=params,
             name="join",
-        )(ready, *parts)
+        )(gates, *parts)
     with jax.named_scope("rows_between_cores"):
         other = swap(mine)
     weights_in = [in_vmem(w_gate[0]), in_vmem(up_here)]
@@ -443,7 +442,7 @@
     with jax.named_scope("sums_along_x"):
         total = total.reshape(xs, slots, half)
         backs = [along(total[1 + place], xs - step) for place, step in enumerate(steps)]
-        backs = [backs[1], backs[0]] + backs[2:]
+        backs = backs[:-2] + [backs[-1], backs[-2]]
     with jax.named_scope("spread"):
         send = pl.pallas_call(
             spread_kernel,

time: 65.4 us -> 64.2 us (0.982); the launches traced: 64.6 us -> 64.1 us
  waiting for transfers between devices: 9.08 us -> 10.9 us
  starting transfers between devices: 9.23 us -> 7.75 us
  blocking collectives: 31.5 us -> 30.8 us
    ppermute x6, waiting for transfers between devices: 6.42 us -> 8.23 us  [along(): return lax.ppermute(array, 'x', [(i, (i + step) % xs) for i in range(xs)])]
    ppermute x6, starting transfers between devices: 8.94 us -> 7.45 us  [along(): return lax.ppermute(array, 'x', [(i, (i + step) % xs) for i in range(xs)])]
    all_to_all x1, blocking collectives: 13.5 us -> 12.8 us  [shards(): lax.all_to_all(send.reshape(peers, pack, piece), 'ep', 0, 0, tiled=True)]
  transfers between devices with their start and end apart: 8 -> 8, of which waited for: 4 -> 5; matrix products, arithmetic and copies ran while one was open for 0% -> 0% of each run, Pallas kernels for 9% -> 10%
where the time goes in v5:
time: 64.2 us; the launch traced here: 64.1 us
  blocking collectives  30.8 us (48%)
  Pallas kernels  14.4 us (22%)
  waiting for transfers between devices  10.9 us (17%)
  starting transfers between devices  7.75 us (12%)
    all_to_all x1, blocking collectives, shards(): received = lax.all_to_all(send, 'ep', 0, 0, tiled=True)  18 us
    all_to_all x1, blocking collectives, shards(): lax.all_to_all(send.reshape(peers, pack, piece), 'ep', 0, 0, tiled=True)  12.8 us
    ppermute x6, waiting for transfers between devices, along(): return lax.ppermute(array, 'x', [(i, (i + step) % xs) for i in range(xs)])  8.23 us
    ppermute x6, starting transfers between devices, along(): return lax.ppermute(array, 'x', [(i, (i + step) % xs) for i in range(xs)])  7.45 us
    pallas_call x1, Pallas kernels, shards(): pl.pallas_call(fetch_kernel, out_shape=tuple((pltpu.VMEM(w.shape[1:], bf1...  4.92 us
    pallas_call x1, Pallas kernels, shards(): pl.pallas_call(attention_kernel, out_shape=(jax.ShapeDtypeStruct((peers,...  3.35 us
    pallas_call x1, Pallas kernels, shards(): pl.pallas_call(expert_kernel, out_shape=(jax.ShapeDtypeStruct((rows_here,...  3.31 us
    ppermute x2, waiting for transfers between devices, swap(): return lax.ppermute(array, 'core', [(0, 1), (1, 0)])  2.65 us
  transfers between devices with their start and end apart: 8, of which 5 were waited for; matrix products, arithmetic and copies ran while one was open for 0% of the time, Pallas kernels for 10%

profile of v5, /device:TPU:6, one launch (start us, length us, event | category | flops | bytes accessed | tf_op | source)
XLA Modules:
  0.0 64.1 jit_solution(9635681722739008836)
XLA Ops:
  0.0 0.0 copy-start
  0.0 3.3 %attention.1 = (bf16[16,8,1664]{2,1,0:T(8,128)(2,1)S(1)}, bf16[8,1536]{1,0:T(8,128)(2,1)S(1)}) custom-call(s32[1]{0:T(128)} %bitcast.expert, s32[2]{0:T(128)} %bitcast.33, s32[2,2]{1,0:T(2,128)} %bitcast.32, bf16[2,6144]{1,0:T(2,128)(2,1)} %bitcast.27, bf16[2,6144]{1,0:T(2,128)(2,1)} %bitcast.28, bf16[2,1024]{1,0:T(2,128)(2,1)} %bitcast.30, ...), custom_call_target="tpu_custom_call" | custom-call | tf_op jit(solution)/shard_map/attention/attention/pallas_call | solution.py:327
  3.4 18.0 %all_to_all.10 = bf16[16,8,1664]{2,1,0:T(8,128)(2,1)S(1)} all-to-all(bf16[16,8,1664]{2,1,0:T(8,128)(2,1)S(1)} %get-tuple-element.14.sent), channel_id=1, replica_groups=mesh['x'=4,'core'=2,'ep'=16] {'ep'}, dimensions={0} | all-to-all | bytes 851968 | tf_op jit(solution)/shard_map/rows_to_experts/all_to_all | solution.py:368
  21.4 0.5 select.5
  21.9 0.5 collective-permute-start.2
  22.4 1.5 %collective-permute-start.1 = (bf16[24,3072]{1,0:T(8,128)(2,1)S(1)}, bf16[24,3072]{1,0:T(8,128)(2,1)S(1)}, u32[]{:S(2)}, u32[]{:S(2)}) collective-permute-start(bf16[24,3072]{1,0:T(8,128)(2,1)S(1)} %get-tuple-element.17.refs_0_), channel_id=1, source_target_pairs={{0,96},{32,0},{64,32},{96,64},{1,97},{33,1},{65,33},{97,65},{2,98}... | collective-permute-start | bytes 442376 | tf_op jit(solution)/shard_map/rows_along_x/ppermute | solution.py:383
  24.0 1.4 %collective-permute-start = (bf16[24,3072]{1,0:T(8,128)(2,1)S(1)}, bf16[24,3072]{1,0:T(8,128)(2,1)S(1)}, u32[]{:S(2)}, u32[]{:S(2)}) collective-permute-start(bf16[24,3072]{1,0:T(8,128)(2,1)S(1)} %get-tuple-element.17.refs_0_), channel_id=1, source_target_pairs={{0,64},{32,96},{64,0},{96,32},{1,65},{33,97},{65,1},{97,33},{2,66}... | collective-permute-start | bytes 442376 | tf_op jit(solution)/shard_map/rows_along_x/ppermute | solution.py:383
  25.4 0.0 slice-start
  25.4 0.0 copy-done
  25.4 0.0 slice-start.1
  25.4 4.9 %weights.1 = (bf16[6144,512]{1,0:T(8,128)(2,1)S(1)}, bf16[512,6144]{1,0:T(8,128)(2,1)S(1)}, f32[8,128]{1,0:T(8,128)S(1)}) custom-call(bf16[128,128]{1,0:T(8,128)(2,1)S(1)} %get-tuple-element.15.after.places, bf16[16,8,1664]{2,1,0:T(8,128)(2,1)S(1)} %get-tuple-element.14.sent, bf16[8,6144]{1,0:T(8,128)(2,1)S(1)} %bitcast.22, bf16[6144,512]{1,0:T(8,128)(2,1)} %bitcast.23, ...), custom_call_target="tpu_custom_call" | custom-call | bytes 12582912 | tf_op jit(solution)/shard_map/weights/weights/pallas_call | solution.py:392
  30.3 0.0 collective-permute-done.2.refs_3_
  30.3 0.0 collective-permute-done.1.refs_2_
  30.3 0.3 collective-permute-done.refs_1_
  30.7 0.1 collective-permute-start.3
  30.7 2.0 %collective-permute-done.3.other = bf16[96,3072]{1,0:T(8,128)(2,1)S(1)} collective-permute-done((bf16[96,3072]{1,0:T(8,128)(2,1)S(1)}, bf16[96,3072]{1,0:T(8,128)(2,1)S(1)}, u32[]{:S(2)}, u32[]{:S(2)}) %collective-permute-start.3) | collective-permute-done | bytes 589856 | tf_op jit(solution)/shard_map/rows_between_cores/ppermute | solution.py:386
  32.7 0.0 slice-done
  32.7 0.0 slice-done.1
  32.7 3.3 %experts.1 = (bf16[48,512]{1,0:T(8,128)(2,1)S(1)}, bf16[96,3072]{1,0:T(8,128)(2,1)S(1)}) custom-call(bf16[96,3072]{1,0:T(8,128)(2,1)S(1)} %join.1.mine, bf16[96,3072]{1,0:T(8,128)(2,1)S(1)} %collective-permute-done.3.other, bf16[6144,512]{1,0:T(8,128)(2,1)S(1)} %bitcast.19, bf16[6144,512]{1,0:T(8,128)(2,1)S(1)} %get-tuple-element.18.w_up, ...), custom_call_target="tpu_custom_call" | custom-call | flops 1509949440 | bytes 18874368 | tf_op jit(solution)/shard_map/experts/experts/pallas_call | solution.py:417
  36.1 0.2 collective-permute-start.4
  36.3 1.2 %own_down.1 = f32[96,3072]{1,0:T(8,128)S(1)} custom-call(bf16[48,512]{1,0:T(8,128)(2,1)S(1)} %get-tuple-element.20.act, bf16[512,6144]{1,0:T(8,128)(2,1)S(1)} %get-tuple-element.19.w_down), custom_call_target="tpu_custom_call" | custom-call | flops 301989888 | bytes 6291456 | tf_op jit(solution)/shard_map/own_down/own_down/pallas_call | solution.py:432
  37.5 0.7 %collective-permute-done.4 = bf16[96,3072]{1,0:T(8,128)(2,1)S(1)} collective-permute-done((bf16[96,3072]{1,0:T(8,128)(2,1)S(1)}, bf16[96,3072]{1,0:T(8,128)(2,1)S(1)}, u32[]{:S(2)}, u32[]{:S(2)}) %collective-permute-start.4) | collective-permute-done | bytes 589856 | tf_op jit(solution)/shard_map/sums_between_cores/ppermute | solution.py:386
  38.1 0.1 add_convert_fusion
  38.3 1.9 %collective-permute-start.7 = (bf16[24,3072]{1,0:T(8,128)(2,1)S(1)}, bf16[24,3072]{1,0:T(8,128)(2,1)S(1)}, u32[]{:S(2)}, u32[]{:S(2)}) collective-permute-start(bf16[24,3072]{1,0:T(8,128)(2,1)S(1)} %get-tuple-element.23), channel_id=1, source_target_pairs={{0,32},{32,64},{64,96},{96,0},{1,33},{33,65},{65,97},{97,1},{2,34}... | collective-permute-start | bytes 442376 | tf_op jit(solution)/shard_map/sums_along_x/ppermute | solution.py:383
  40.2 0.2 collective-permute-start.6
  40.4 1.9 %collective-permute-start.5 = (bf16[24,3072]{1,0:T(8,128)(2,1)S(1)}, bf16[24,3072]{1,0:T(8,128)(2,1)S(1)}, u32[]{:S(2)}, u32[]{:S(2)}) collective-permute-start(bf16[24,3072]{1,0:T(8,128)(2,1)S(1)} %get-tuple-element.25), channel_id=1, source_target_pairs={{0,64},{32,96},{64,0},{96,32},{1,65},{33,97},{65,1},{97,33},{2,66}... | collective-permute-start | bytes 442376 | tf_op jit(solution)/shard_map/sums_along_x/ppermute | solution.py:383
  42.3 2.0 %collective-permute-done.7.third = bf16[24,3072]{1,0:T(8,128)(2,1)S(1)} collective-permute-done((bf16[24,3072]{1,0:T(8,128)(2,1)S(1)}, bf16[24,3072]{1,0:T(8,128)(2,1)S(1)}, u32[]{:S(2)}, u32[]{:S(2)}) %collective-permute-start.7) | collective-permute-done | bytes 147488 | tf_op jit(solution)/shard_map/sums_along_x/ppermute | solution.py:383
  44.3 5.9 %collective-permute-done.6.second = bf16[24,3072]{1,0:T(8,128)(2,1)S(1)} collective-permute-done((bf16[24,3072]{1,0:T(8,128)(2,1)S(1)}, bf16[24,3072]{1,0:T(8,128)(2,1)S(1)}, u32[]{:S(2)}, u32[]{:S(2)}) %collective-permute-start.6) | collective-permute-done | bytes 147488 | tf_op jit(solution)/shard_map/sums_along_x/ppermute | solution.py:383
  50.2 0.0 collective-permute-done.5.first
  50.2 0.3 spread.1
  50.5 12.8 %all_to_all.11.received = bf16[16,8,1536]{2,1,0:T(8,128)(2,1)S(1)} all-to-all(bf16[16,8,1536]{2,1,0:T(8,128)(2,1)S(1)} %bitcast.21), channel_id=1, replica_groups=mesh['x'=4,'core'=2,'ep'=16] {'ep'}, dimensions={0} | all-to-all | bytes 786432 | tf_op jit(solution)/shard_map/sums_to_rows/all_to_all | solution.py:456
  63.3 0.8 %combine.1 = bf16[2,6144]{1,0:T(2,128)(2,1)} custom-call(bf16[16,8,1536]{2,1,0:T(8,128)(2,1)S(1)} %all_to_all.11.received, bf16[8,1536]{1,0:T(8,128)(2,1)S(1)} %get-tuple-element.22.stream, f32[8,128]{1,0:T(8,128)S(1)} %get-tuple-element.16.ready.gates), custom_call_target="tpu_custom_call" | custom-call | tf_op jit(solution)/shard_map/combine/combine/pallas_call | solution.py:460
  (3 shorter events, 0.1 us)
Async XLA Ops:
  0.0 25.4 %copy-start = (bf16[6144,8]{0,1:T(8,128)(2,1)S(1)}, bf16[6144,8]{0,1:T(8,128)(2,1)}, u32[]{:S(2)}) copy-start(bf16[6144,8]{0,1:T(8,128)(2,1)} %param.22) | copy-start | bytes 294916
  21.9 8.4 %collective-permute-start.2 = (bf16[24,3072]{1,0:T(8,128)(2,1)S(1)}, bf16[24,3072]{1,0:T(8,128)(2,1)S(1)}, u32[]{:S(2)}, u32[]{:S(2)}) collective-permute-start(bf16[24,3072]{1,0:T(8,128)(2,1)S(1)} %get-tuple-element.17.refs_0_), channel_id=1, source_target_pairs={{0,32},{32,64},{64,96},{96,0},{1,33},{33,65},{65,97},{97,1},{2,34}... | collective-permute-start | bytes 442376 | tf_op jit(solution)/shard_map/rows_along_x/ppermute | solution.py:383
  22.4 7.9 %collective-permute-start.1 = (bf16[24,3072]{1,0:T(8,128)(2,1)S(1)}, bf16[24,3072]{1,0:T(8,128)(2,1)S(1)}, u32[]{:S(2)}, u32[]{:S(2)}) collective-permute-start(bf16[24,3072]{1,0:T(8,128)(2,1)S(1)} %get-tuple-element.17.refs_0_), channel_id=1, source_target_pairs={{0,96},{32,0},{64,32},{96,64},{1,97},{33,1},{65,33},{97,65},{2,98}... | collective-permute-start | bytes 442376 | tf_op jit(solution)/shard_map/rows_along_x/ppermute | solution.py:383
  24.0 6.6 %collective-permute-start = (bf16[24,3072]{1,0:T(8,128)(2,1)S(1)}, bf16[24,3072]{1,0:T(8,128)(2,1)S(1)}, u32[]{:S(2)}, u32[]{:S(2)}) collective-permute-start(bf16[24,3072]{1,0:T(8,128)(2,1)S(1)} %get-tuple-element.17.refs_0_), channel_id=1, source_target_pairs={{0,64},{32,96},{64,0},{96,32},{1,65},{33,97},{65,1},{97,33},{2,66}... | collective-permute-start | bytes 442376 | tf_op jit(solution)/shard_map/rows_along_x/ppermute | solution.py:383
  25.4 7.4 %slice-start = ((s8[6291456]{0:T(1024)(128)(4,1)}), s8[4194304]{0:T(1024)(128)(4,1)S(1)}, s32[]{:S(2)}) async-start(s8[6291456]{0:T(1024)(128)(4,1)} %bitcast.17), calls=%async_computation.2 | async-start | bytes 8388608
  25.4 7.4 %slice-start.1 = ((s8[6291456]{0:T(1024)(128)(4,1)}), s8[2097152]{0:T(1024)(128)(4,1)S(1)}, s32[]{:S(2)}) async-start(s8[6291456]{0:T(1024)(128)(4,1)} %bitcast.17), calls=%async_computation.3 | async-start | bytes 4194304
  30.7 2.1 %collective-permute-start.3 = (bf16[96,3072]{1,0:T(8,128)(2,1)S(1)}, bf16[96,3072]{1,0:T(8,128)(2,1)S(1)}, u32[]{:S(2)}, u32[]{:S(2)}) collective-permute-start(bf16[96,3072]{1,0:T(8,128)(2,1)S(1)} %join.1.mine), channel_id=1, source_target_pairs={{0,16},{16,0},{1,17},{17,1},{2,18},{18,2},{3,19},{19,3},{4,20},{20... | collective-permute-start | bytes 1769480 | tf_op jit(solution)/shard_map/rows_between_cores/ppermute | solution.py:386
  36.1 2.1 %collective-permute-start.4 = (bf16[96,3072]{1,0:T(8,128)(2,1)S(1)}, bf16[96,3072]{1,0:T(8,128)(2,1)S(1)}, u32[]{:S(2)}, u32[]{:S(2)}) collective-permute-start(bf16[96,3072]{1,0:T(8,128)(2,1)S(1)} %get-tuple-element.21), channel_id=1, source_target_pairs={{0,16},{16,0},{1,17},{17,1},{2,18},{18,2},{3,19},{19,3},{4,20},{20... | collective-permute-start | bytes 1769480 | tf_op jit(solution)/shard_map/sums_between_cores/ppermute | solution.py:386
  38.3 6.0 %collective-permute-start.7 = (bf16[24,3072]{1,0:T(8,128)(2,1)S(1)}, bf16[24,3072]{1,0:T(8,128)(2,1)S(1)}, u32[]{:S(2)}, u32[]{:S(2)}) collective-permute-start(bf16[24,3072]{1,0:T(8,128)(2,1)S(1)} %get-tuple-element.23), channel_id=1, source_target_pairs={{0,32},{32,64},{64,96},{96,0},{1,33},{33,65},{65,97},{97,1},{2,34}... | collective-permute-start | bytes 442376 | tf_op jit(solution)/shard_map/sums_along_x/ppermute | solution.py:383
  40.2 10.0 %collective-permute-start.6 = (bf16[24,3072]{1,0:T(8,128)(2,1)S(1)}, bf16[24,3072]{1,0:T(8,128)(2,1)S(1)}, u32[]{:S(2)}, u32[]{:S(2)}) collective-permute-start(bf16[24,3072]{1,0:T(8,128)(2,1)S(1)} %get-tuple-element.24), channel_id=1, source_target_pairs={{0,96},{32,0},{64,32},{96,64},{1,97},{33,1},{65,33},{97,65},{2,98}... | collective-permute-start | bytes 442376 | tf_op jit(solution)/shard_map/sums_along_x/ppermute | solution.py:383
  40.4 9.8 %collective-permute-start.5 = (bf16[24,3072]{1,0:T(8,128)(2,1)S(1)}, bf16[24,3072]{1,0:T(8,128)(2,1)S(1)}, u32[]{:S(2)}, u32[]{:S(2)}) collective-permute-start(bf16[24,3072]{1,0:T(8,128)(2,1)S(1)} %get-tuple-element.25), channel_id=1, source_target_pairs={{0,64},{32,96},{64,0},{96,32},{1,65},{33,97},{65,1},{97,33},{2,66}... | collective-permute-start | bytes 442376 | tf_op jit(solution)/shard_map/sums_along_x/ppermute | solution.py:383

commit v6 on v5

--- a/solution.py
+++ b/solution.py
@@ -74,11 +74,18 @@
     for row in range(batches):
         copies[row][0].wait()
         scores.append(
-            lax.dot_general(
-                spread[row].astype(jnp.bfloat16),
-                key_buf[row],
-                (((1,), (1,)), ((), ())),
-                preferred_element_type=jnp.float32,
+            jnp.concatenate(
+                [
+                    lax.dot_general(
+                        spread[row, 8 * block : 8 * block + 8, lanes].astype(jnp.bfloat16),
+                        key_buf[row, :, lanes],
+                        (((1,), (1,)), ((), ())),
+                        preferred_element_type=jnp.float32,
+                    )
+                    for block in range(KV_HEADS)
+                    for lanes in (slice(HEAD * block, HEAD * (block + 1)),)
+                ],
+                axis=0,
             )
         )
     for copy in small[1:]:
@@ -104,20 +111,24 @@
         terms = jnp.exp(score - peak)
         own_term = jnp.exp(own - peak)
         total = jnp.sum(terms, axis=1, keepdims=True) + own_term
-        weights = (terms / total).astype(jnp.bfloat16)
+        weights = (terms / total).astype(jnp.bfloat16).astype(jnp.float32)
         own_weight = (own_term / total).astype(jnp.bfloat16).astype(jnp.float32)
         shares.append((weights, own_weight))
     for row in range(batches):
         weights, own_weight = shares[row]
         copies[row][1].wait()
-        mixture = jnp.dot(weights, value_buf[row], preferred_element_type=jnp.float32)
-        mixture = mixture + own_weight * value_wide[row : row + 1]
-        for head in range(heads):
-            block, place = head // group, head % group
-            part, start = HEAD * head // piece, HEAD * head % piece
-            mixed[pl.ds(row * PARTS + part, 1), pl.ds(start, HEAD)] = mixture[
-                8 * block + place : 8 * block + place + 1, HEAD * block : HEAD * (block + 1)
-            ]
+        for block in range(KV_HEADS):
+            at, lanes = slice(8 * block, 8 * block + 8), slice(HEAD * block, HEAD * (block + 1))
+            mixture = jnp.dot(
+                weights[at].astype(jnp.bfloat16),
+                value_buf[row, :, lanes],
+                preferred_element_type=jnp.float32,
+            )
+            mixture = mixture + own_weight[at] * value_wide[row : row + 1, lanes]
+            for place in range(group):
+                head = block * group + place
+                part, start = HEAD * head // piece, HEAD * head % piece
+                mixed[pl.ds(row * PARTS + part, 1), pl.ds(start, HEAD)] = mixture[place : place + 1]
     attended = mixed[...].astype(jnp.bfloat16).astype(jnp.float32)
     stream = (base[...] + attended).astype(jnp.bfloat16)
     stream_out[...] = stream
@@ -251,11 +262,15 @@
         jnp.concatenate(pair, axis=0)
         for pair in zip(whole_rows(mine, slots), whole_rows(other, slots))
     ]
-    gate, up = (
-        jnp.dot(sides[0], w[0:half], preferred_element_type=jnp.float32)
-        + jnp.dot(sides[1], w[half : 2 * half], preferred_element_type=jnp.float32)
-        for w in (w_gate, w_up)
-    )
+    gate = jnp.zeros((sides[0].shape[0], w_gate.shape[1]), jnp.float32)
+    up = gate
+    step = 512
+    for side in range(2):
+        for start in range(0, half, step):
+            x = sides[side][:, start : start + step]
+            at = side * half + start
+            gate += jnp.dot(x, w_gate[at : at + step], preferred_element_type=jnp.float32)
+            up += jnp.dot(x, w_up[at : at + step], preferred_element_type=jnp.float32)
     act = (gate * (1.0 / (1.0 + jnp.exp(-gate))) * up).astype(jnp.bfloat16)
     count = act.shape[0] // 2
     act_out[...] = act[0:count]

time: 64.2 us -> 64.1 us (level)
  no operation moved by 1% of the time
where the time goes in v6:
time: 64.1 us; the launch traced here: 63.9 us
  blocking collectives  30.8 us (48%)
  Pallas kernels  14.2 us (22%)
  waiting for transfers between devices  10.9 us (17%)
  starting transfers between devices  7.73 us (12%)
    all_to_all x1, blocking collectives, shards(): received = lax.all_to_all(send, 'ep', 0, 0, tiled=True)  18 us
    all_to_all x1, blocking collectives, shards(): lax.all_to_all(send.reshape(peers, pack, piece), 'ep', 0, 0, tiled=True)  12.8 us
    ppermute x6, waiting for transfers between devices, along(): return lax.ppermute(array, 'x', [(i, (i + step) % xs) for i in range(xs)])  8.23 us
    ppermute x6, starting transfers between devices, along(): return lax.ppermute(array, 'x', [(i, (i + step) % xs) for i in range(xs)])  7.43 us
    pallas_call x1, Pallas kernels, shards(): pl.pallas_call(fetch_kernel, out_shape=tuple((pltpu.VMEM(w.shape[1:], bf1...  4.92 us
    pallas_call x1, Pallas kernels, shards(): pl.pallas_call(expert_kernel, out_shape=(jax.ShapeDtypeStruct((rows_here,...  3.32 us
    pallas_call x1, Pallas kernels, shards(): pl.pallas_call(attention_kernel, out_shape=(jax.ShapeDtypeStruct((peers,...  3.22 us
    ppermute x2, waiting for transfers between devices, swap(): return lax.ppermute(array, 'core', [(0, 1), (1, 0)])  2.66 us
  transfers between devices with their start and end apart: 8, of which 5 were waited for; matrix products, arithmetic and copies ran while one was open for 0% of the time, Pallas kernels for 10%

profile of v6, /device:TPU:6, one launch (start us, length us, event | category | flops | bytes accessed | tf_op | source)
XLA Modules:
  0.0 63.9 jit_solution(10284176686296401413)
XLA Ops:
  0.0 0.0 copy-start
  0.0 3.2 %attention.1 = (bf16[16,8,1664]{2,1,0:T(8,128)(2,1)S(1)}, bf16[8,1536]{1,0:T(8,128)(2,1)S(1)}) custom-call(s32[1]{0:T(128)} %bitcast.expert, s32[2]{0:T(128)} %bitcast.33, s32[2,2]{1,0:T(2,128)} %bitcast.32, bf16[2,6144]{1,0:T(2,128)(2,1)} %bitcast.27, bf16[2,6144]{1,0:T(2,128)(2,1)} %bitcast.28, bf16[2,1024]{1,0:T(2,128)(2,1)} %bitcast.30, ...), custom_call_target="tpu_custom_call" | custom-call | tf_op jit(solution)/shard_map/attention/attention/pallas_call | solution.py:342
  3.2 18.0 %all_to_all.10 = bf16[16,8,1664]{2,1,0:T(8,128)(2,1)S(1)} all-to-all(bf16[16,8,1664]{2,1,0:T(8,128)(2,1)S(1)} %get-tuple-element.14.sent), channel_id=1, replica_groups=mesh['x'=4,'core'=2,'ep'=16] {'ep'}, dimensions={0} | all-to-all | bytes 851968 | tf_op jit(solution)/shard_map/rows_to_experts/all_to_all | solution.py:383
  21.2 0.5 select.5
  21.7 0.5 collective-permute-start.2
  22.3 1.6 %collective-permute-start.1 = (bf16[24,3072]{1,0:T(8,128)(2,1)S(1)}, bf16[24,3072]{1,0:T(8,128)(2,1)S(1)}, u32[]{:S(2)}, u32[]{:S(2)}) collective-permute-start(bf16[24,3072]{1,0:T(8,128)(2,1)S(1)} %get-tuple-element.17.refs_0_), channel_id=1, source_target_pairs={{0,96},{32,0},{64,32},{96,64},{1,97},{33,1},{65,33},{97,65},{2,98}... | collective-permute-start | bytes 442376 | tf_op jit(solution)/shard_map/rows_along_x/ppermute | solution.py:398
  23.8 1.4 %collective-permute-start = (bf16[24,3072]{1,0:T(8,128)(2,1)S(1)}, bf16[24,3072]{1,0:T(8,128)(2,1)S(1)}, u32[]{:S(2)}, u32[]{:S(2)}) collective-permute-start(bf16[24,3072]{1,0:T(8,128)(2,1)S(1)} %get-tuple-element.17.refs_0_), channel_id=1, source_target_pairs={{0,64},{32,96},{64,0},{96,32},{1,65},{33,97},{65,1},{97,33},{2,66}... | collective-permute-start | bytes 442376 | tf_op jit(solution)/shard_map/rows_along_x/ppermute | solution.py:398
  25.2 0.0 slice-start
  25.2 0.0 copy-done
  25.2 0.0 slice-start.1
  25.2 4.9 %weights.1 = (bf16[6144,512]{1,0:T(8,128)(2,1)S(1)}, bf16[512,6144]{1,0:T(8,128)(2,1)S(1)}, f32[8,128]{1,0:T(8,128)S(1)}) custom-call(bf16[128,128]{1,0:T(8,128)(2,1)S(1)} %get-tuple-element.15.after.places, bf16[16,8,1664]{2,1,0:T(8,128)(2,1)S(1)} %get-tuple-element.14.sent, bf16[8,6144]{1,0:T(8,128)(2,1)S(1)} %bitcast.22, bf16[6144,512]{1,0:T(8,128)(2,1)} %bitcast.23, ...), custom_call_target="tpu_custom_call" | custom-call | bytes 12582912 | tf_op jit(solution)/shard_map/weights/weights/pallas_call | solution.py:407
  30.2 0.0 collective-permute-done.2.refs_3_
  30.2 0.0 collective-permute-done.1.refs_2_
  30.2 0.3 collective-permute-done.refs_1_
  30.5 0.1 collective-permute-start.3
  30.6 2.0 %collective-permute-done.3.other = bf16[96,3072]{1,0:T(8,128)(2,1)S(1)} collective-permute-done((bf16[96,3072]{1,0:T(8,128)(2,1)S(1)}, bf16[96,3072]{1,0:T(8,128)(2,1)S(1)}, u32[]{:S(2)}, u32[]{:S(2)}) %collective-permute-start.3) | collective-permute-done | bytes 589856 | tf_op jit(solution)/shard_map/rows_between_cores/ppermute | solution.py:401
  32.6 0.0 slice-done
  32.6 0.0 slice-done.1
  32.6 3.3 %experts.1 = (bf16[48,512]{1,0:T(8,128)(2,1)S(1)}, bf16[96,3072]{1,0:T(8,128)(2,1)S(1)}) custom-call(bf16[96,3072]{1,0:T(8,128)(2,1)S(1)} %join.1.mine, bf16[96,3072]{1,0:T(8,128)(2,1)S(1)} %collective-permute-done.3.other, bf16[6144,512]{1,0:T(8,128)(2,1)S(1)} %bitcast.19, bf16[6144,512]{1,0:T(8,128)(2,1)S(1)} %get-tuple-element.18.w_up, ...), custom_call_target="tpu_custom_call" | custom-call | flops 1509949440 | bytes 18874368 | tf_op jit(solution)/shard_map/experts/experts/pallas_call | solution.py:432
  35.9 0.2 collective-permute-start.4
  36.2 1.2 %own_down.1 = f32[96,3072]{1,0:T(8,128)S(1)} custom-call(bf16[48,512]{1,0:T(8,128)(2,1)S(1)} %get-tuple-element.20.act, bf16[512,6144]{1,0:T(8,128)(2,1)S(1)} %get-tuple-element.19.w_down), custom_call_target="tpu_custom_call" | custom-call | flops 301989888 | bytes 6291456 | tf_op jit(solution)/shard_map/own_down/own_down/pallas_call | solution.py:447
  37.4 0.7 %collective-permute-done.4 = bf16[96,3072]{1,0:T(8,128)(2,1)S(1)} collective-permute-done((bf16[96,3072]{1,0:T(8,128)(2,1)S(1)}, bf16[96,3072]{1,0:T(8,128)(2,1)S(1)}, u32[]{:S(2)}, u32[]{:S(2)}) %collective-permute-start.4) | collective-permute-done | bytes 589856 | tf_op jit(solution)/shard_map/sums_between_cores/ppermute | solution.py:401
  38.0 0.1 add_convert_fusion
  38.2 1.9 %collective-permute-start.7 = (bf16[24,3072]{1,0:T(8,128)(2,1)S(1)}, bf16[24,3072]{1,0:T(8,128)(2,1)S(1)}, u32[]{:S(2)}, u32[]{:S(2)}) collective-permute-start(bf16[24,3072]{1,0:T(8,128)(2,1)S(1)} %get-tuple-element.23), channel_id=1, source_target_pairs={{0,32},{32,64},{64,96},{96,0},{1,33},{33,65},{65,97},{97,1},{2,34}... | collective-permute-start | bytes 442376 | tf_op jit(solution)/shard_map/sums_along_x/ppermute | solution.py:398
  40.1 0.2 collective-permute-start.6
  40.3 1.8 %collective-permute-start.5 = (bf16[24,3072]{1,0:T(8,128)(2,1)S(1)}, bf16[24,3072]{1,0:T(8,128)(2,1)S(1)}, u32[]{:S(2)}, u32[]{:S(2)}) collective-permute-start(bf16[24,3072]{1,0:T(8,128)(2,1)S(1)} %get-tuple-element.25), channel_id=1, source_target_pairs={{0,64},{32,96},{64,0},{96,32},{1,65},{33,97},{65,1},{97,33},{2,66}... | collective-permute-start | bytes 442376 | tf_op jit(solution)/shard_map/sums_along_x/ppermute | solution.py:398
  42.2 2.0 %collective-permute-done.7.third = bf16[24,3072]{1,0:T(8,128)(2,1)S(1)} collective-permute-done((bf16[24,3072]{1,0:T(8,128)(2,1)S(1)}, bf16[24,3072]{1,0:T(8,128)(2,1)S(1)}, u32[]{:S(2)}, u32[]{:S(2)}) %collective-permute-start.7) | collective-permute-done | bytes 147488 | tf_op jit(solution)/shard_map/sums_along_x/ppermute | solution.py:398
  44.2 5.9 %collective-permute-done.6.second = bf16[24,3072]{1,0:T(8,128)(2,1)S(1)} collective-permute-done((bf16[24,3072]{1,0:T(8,128)(2,1)S(1)}, bf16[24,3072]{1,0:T(8,128)(2,1)S(1)}, u32[]{:S(2)}, u32[]{:S(2)}) %collective-permute-start.6) | collective-permute-done | bytes 147488 | tf_op jit(solution)/shard_map/sums_along_x/ppermute | solution.py:398
  50.1 0.0 collective-permute-done.5.first
  50.1 0.3 spread.1
  50.4 12.8 %all_to_all.11.received = bf16[16,8,1536]{2,1,0:T(8,128)(2,1)S(1)} all-to-all(bf16[16,8,1536]{2,1,0:T(8,128)(2,1)S(1)} %bitcast.21), channel_id=1, replica_groups=mesh['x'=4,'core'=2,'ep'=16] {'ep'}, dimensions={0} | all-to-all | bytes 786432 | tf_op jit(solution)/shard_map/sums_to_rows/all_to_all | solution.py:471
  63.2 0.8 %combine.1 = bf16[2,6144]{1,0:T(2,128)(2,1)} custom-call(bf16[16,8,1536]{2,1,0:T(8,128)(2,1)S(1)} %all_to_all.11.received, bf16[8,1536]{1,0:T(8,128)(2,1)S(1)} %get-tuple-element.22.stream, f32[8,128]{1,0:T(8,128)S(1)} %get-tuple-element.16.ready.gates), custom_call_target="tpu_custom_call" | custom-call | tf_op jit(solution)/shard_map/combine/combine/pallas_call | solution.py:475
  (3 shorter events, 0.1 us)
Async XLA Ops:
  0.0 25.2 %copy-start = (bf16[6144,8]{0,1:T(8,128)(2,1)S(1)}, bf16[6144,8]{0,1:T(8,128)(2,1)}, u32[]{:S(2)}) copy-start(bf16[6144,8]{0,1:T(8,128)(2,1)} %param.22) | copy-start | bytes 294916
  21.7 8.4 %collective-permute-start.2 = (bf16[24,3072]{1,0:T(8,128)(2,1)S(1)}, bf16[24,3072]{1,0:T(8,128)(2,1)S(1)}, u32[]{:S(2)}, u32[]{:S(2)}) collective-permute-start(bf16[24,3072]{1,0:T(8,128)(2,1)S(1)} %get-tuple-element.17.refs_0_), channel_id=1, source_target_pairs={{0,32},{32,64},{64,96},{96,0},{1,33},{33,65},{65,97},{97,1},{2,34}... | collective-permute-start | bytes 442376 | tf_op jit(solution)/shard_map/rows_along_x/ppermute | solution.py:398
  22.3 7.9 %collective-permute-start.1 = (bf16[24,3072]{1,0:T(8,128)(2,1)S(1)}, bf16[24,3072]{1,0:T(8,128)(2,1)S(1)}, u32[]{:S(2)}, u32[]{:S(2)}) collective-permute-start(bf16[24,3072]{1,0:T(8,128)(2,1)S(1)} %get-tuple-element.17.refs_0_), channel_id=1, source_target_pairs={{0,96},{32,0},{64,32},{96,64},{1,97},{33,1},{65,33},{97,65},{2,98}... | collective-permute-start | bytes 442376 | tf_op jit(solution)/shard_map/rows_along_x/ppermute | solution.py:398
  23.8 6.6 %collective-permute-start = (bf16[24,3072]{1,0:T(8,128)(2,1)S(1)}, bf16[24,3072]{1,0:T(8,128)(2,1)S(1)}, u32[]{:S(2)}, u32[]{:S(2)}) collective-permute-start(bf16[24,3072]{1,0:T(8,128)(2,1)S(1)} %get-tuple-element.17.refs_0_), channel_id=1, source_target_pairs={{0,64},{32,96},{64,0},{96,32},{1,65},{33,97},{65,1},{97,33},{2,66}... | collective-permute-start | bytes 442376 | tf_op jit(solution)/shard_map/rows_along_x/ppermute | solution.py:398
  25.2 7.4 %slice-start = ((s8[6291456]{0:T(1024)(128)(4,1)}), s8[4194304]{0:T(1024)(128)(4,1)S(1)}, s32[]{:S(2)}) async-start(s8[6291456]{0:T(1024)(128)(4,1)} %bitcast.17), calls=%async_computation.2 | async-start | bytes 8388608
  25.2 7.4 %slice-start.1 = ((s8[6291456]{0:T(1024)(128)(4,1)}), s8[2097152]{0:T(1024)(128)(4,1)S(1)}, s32[]{:S(2)}) async-start(s8[6291456]{0:T(1024)(128)(4,1)} %bitcast.17), calls=%async_computation.3 | async-start | bytes 4194304
  30.5 2.1 %collective-permute-start.3 = (bf16[96,3072]{1,0:T(8,128)(2,1)S(1)}, bf16[96,3072]{1,0:T(8,128)(2,1)S(1)}, u32[]{:S(2)}, u32[]{:S(2)}) collective-permute-start(bf16[96,3072]{1,0:T(8,128)(2,1)S(1)} %join.1.mine), channel_id=1, source_target_pairs={{0,16},{16,0},{1,17},{17,1},{2,18},{18,2},{3,19},{19,3},{4,20},{20... | collective-permute-start | bytes 1769480 | tf_op jit(solution)/shard_map/rows_between_cores/ppermute | solution.py:401
  35.9 2.1 %collective-permute-start.4 = (bf16[96,3072]{1,0:T(8,128)(2,1)S(1)}, bf16[96,3072]{1,0:T(8,128)(2,1)S(1)}, u32[]{:S(2)}, u32[]{:S(2)}) collective-permute-start(bf16[96,3072]{1,0:T(8,128)(2,1)S(1)} %get-tuple-element.21), channel_id=1, source_target_pairs={{0,16},{16,0},{1,17},{17,1},{2,18},{18,2},{3,19},{19,3},{4,20},{20... | collective-permute-start | bytes 1769480 | tf_op jit(solution)/shard_map/sums_between_cores/ppermute | solution.py:401
  38.2 6.0 %collective-permute-start.7 = (bf16[24,3072]{1,0:T(8,128)(2,1)S(1)}, bf16[24,3072]{1,0:T(8,128)(2,1)S(1)}, u32[]{:S(2)}, u32[]{:S(2)}) collective-permute-start(bf16[24,3072]{1,0:T(8,128)(2,1)S(1)} %get-tuple-element.23), channel_id=1, source_target_pairs={{0,32},{32,64},{64,96},{96,0},{1,33},{33,65},{65,97},{97,1},{2,34}... | collective-permute-start | bytes 442376 | tf_op jit(solution)/shard_map/sums_along_x/ppermute | solution.py:398
  40.1 10.0 %collective-permute-start.6 = (bf16[24,3072]{1,0:T(8,128)(2,1)S(1)}, bf16[24,3072]{1,0:T(8,128)(2,1)S(1)}, u32[]{:S(2)}, u32[]{:S(2)}) collective-permute-start(bf16[24,3072]{1,0:T(8,128)(2,1)S(1)} %get-tuple-element.24), channel_id=1, source_target_pairs={{0,96},{32,0},{64,32},{96,64},{1,97},{33,1},{65,33},{97,65},{2,98}... | collective-permute-start | bytes 442376 | tf_op jit(solution)/shard_map/sums_along_x/ppermute | solution.py:398
  40.3 9.8 %collective-permute-start.5 = (bf16[24,3072]{1,0:T(8,128)(2,1)S(1)}, bf16[24,3072]{1,0:T(8,128)(2,1)S(1)}, u32[]{:S(2)}, u32[]{:S(2)}) collective-permute-start(bf16[24,3072]{1,0:T(8,128)(2,1)S(1)} %get-tuple-element.25), channel_id=1, source_target_pairs={{0,64},{32,96},{64,0},{96,32},{1,65},{33,97},{65,1},{97,33},{2,66}... | collective-permute-start | bytes 442376 | tf_op jit(solution)/shard_map/sums_along_x/ppermute | solution.py:398

commit v7 on v6

--- a/solution.py
+++ b/solution.py
@@ -57,10 +57,10 @@
             )
         )
     ]
-    for copy in [small[0]] + [pair[0] for pair in copies] + small[1:]:
+    for copy in [small[0]] + [pair[0] for pair in copies] + [pair[1] for pair in copies]:
         copy.start()
-    for pair in copies:
-        pair[1].start()
+    for copy in small[1:]:
+        copy.start()
     spread[...] = jnp.zeros_like(spread)
     small[0].wait()
     query_wide = query[...].astype(jnp.float32)

time: 64.1 us -> 64.1 us (level)
  no operation moved by 1% of the time
where the time goes in v7:
time: 64.1 us; the launch traced here: 63.9 us
  blocking collectives  30.8 us (48%)
  Pallas kernels  14.2 us (22%)
  waiting for transfers between devices  10.9 us (17%)
  starting transfers between devices  7.73 us (12%)
    all_to_all x1, blocking collectives, shards(): received = lax.all_to_all(send, 'ep', 0, 0, tiled=True)  18 us
    all_to_all x1, blocking collectives, shards(): lax.all_to_all(send.reshape(peers, pack, piece), 'ep', 0, 0, tiled=True)  12.8 us
    ppermute x6, waiting for transfers between devices, along(): return lax.ppermute(array, 'x', [(i, (i + step) % xs) for i in range(xs)])  8.23 us
    ppermute x6, starting transfers between devices, along(): return lax.ppermute(array, 'x', [(i, (i + step) % xs) for i in range(xs)])  7.43 us
    pallas_call x1, Pallas kernels, shards(): pl.pallas_call(fetch_kernel, out_shape=tuple((pltpu.VMEM(w.shape[1:], bf1...  4.92 us
    pallas_call x1, Pallas kernels, shards(): pl.pallas_call(expert_kernel, out_shape=(jax.ShapeDtypeStruct((rows_here,...  3.32 us
    pallas_call x1, Pallas kernels, shards(): pl.pallas_call(attention_kernel, out_shape=(jax.ShapeDtypeStruct((peers,...  3.22 us
    ppermute x2, waiting for transfers between devices, swap(): return lax.ppermute(array, 'core', [(0, 1), (1, 0)])  2.66 us
  transfers between devices with their start and end apart: 8, of which 5 were waited for; matrix products, arithmetic and copies ran while one was open for 0% of the time, Pallas kernels for 10%

profile of v7, /device:TPU:6, one launch (start us, length us, event | category | flops | bytes accessed | tf_op | source)
XLA Modules:
  0.0 63.9 jit_solution(9148320357093564338)
XLA Ops:
  0.0 0.0 copy-start
  0.0 3.2 %attention.1 = (bf16[16,8,1664]{2,1,0:T(8,128)(2,1)S(1)}, bf16[8,1536]{1,0:T(8,128)(2,1)S(1)}) custom-call(s32[1]{0:T(128)} %bitcast.expert, s32[2]{0:T(128)} %bitcast.33, s32[2,2]{1,0:T(2,128)} %bitcast.32, bf16[2,6144]{1,0:T(2,128)(2,1)} %bitcast.27, bf16[2,6144]{1,0:T(2,128)(2,1)} %bitcast.28, bf16[2,1024]{1,0:T(2,128)(2,1)} %bitcast.30, ...), custom_call_target="tpu_custom_call" | custom-call | tf_op jit(solution)/shard_map/attention/attention/pallas_call | solution.py:342
  3.2 18.0 %all_to_all.10 = bf16[16,8,1664]{2,1,0:T(8,128)(2,1)S(1)} all-to-all(bf16[16,8,1664]{2,1,0:T(8,128)(2,1)S(1)} %get-tuple-element.14.sent), channel_id=1, replica_groups=mesh['x'=4,'core'=2,'ep'=16] {'ep'}, dimensions={0} | all-to-all | bytes 851968 | tf_op jit(solution)/shard_map/rows_to_experts/all_to_all | solution.py:383
  21.2 0.5 select.5
  21.7 0.5 collective-permute-start.2
  22.3 1.6 %collective-permute-start.1 = (bf16[24,3072]{1,0:T(8,128)(2,1)S(1)}, bf16[24,3072]{1,0:T(8,128)(2,1)S(1)}, u32[]{:S(2)}, u32[]{:S(2)}) collective-permute-start(bf16[24,3072]{1,0:T(8,128)(2,1)S(1)} %get-tuple-element.17.refs_0_), channel_id=1, source_target_pairs={{0,96},{32,0},{64,32},{96,64},{1,97},{33,1},{65,33},{97,65},{2,98}... | collective-permute-start | bytes 442376 | tf_op jit(solution)/shard_map/rows_along_x/ppermute | solution.py:398
  23.8 1.4 %collective-permute-start = (bf16[24,3072]{1,0:T(8,128)(2,1)S(1)}, bf16[24,3072]{1,0:T(8,128)(2,1)S(1)}, u32[]{:S(2)}, u32[]{:S(2)}) collective-permute-start(bf16[24,3072]{1,0:T(8,128)(2,1)S(1)} %get-tuple-element.17.refs_0_), channel_id=1, source_target_pairs={{0,64},{32,96},{64,0},{96,32},{1,65},{33,97},{65,1},{97,33},{2,66}... | collective-permute-start | bytes 442376 | tf_op jit(solution)/shard_map/rows_along_x/ppermute | solution.py:398
  25.2 0.0 slice-start
  25.2 0.0 copy-done
  25.2 0.0 slice-start.1
  25.2 4.9 %weights.1 = (bf16[6144,512]{1,0:T(8,128)(2,1)S(1)}, bf16[512,6144]{1,0:T(8,128)(2,1)S(1)}, f32[8,128]{1,0:T(8,128)S(1)}) custom-call(bf16[128,128]{1,0:T(8,128)(2,1)S(1)} %get-tuple-element.15.after.places, bf16[16,8,1664]{2,1,0:T(8,128)(2,1)S(1)} %get-tuple-element.14.sent, bf16[8,6144]{1,0:T(8,128)(2,1)S(1)} %bitcast.22, bf16[6144,512]{1,0:T(8,128)(2,1)} %bitcast.23, ...), custom_call_target="tpu_custom_call" | custom-call | bytes 12582912 | tf_op jit(solution)/shard_map/weights/weights/pallas_call | solution.py:407
  30.2 0.0 collective-permute-done.2.refs_3_
  30.2 0.0 collective-permute-done.1.refs_2_
  30.2 0.3 collective-permute-done.refs_1_
  30.5 0.1 collective-permute-start.3
  30.6 2.0 %collective-permute-done.3.other = bf16[96,3072]{1,0:T(8,128)(2,1)S(1)} collective-permute-done((bf16[96,3072]{1,0:T(8,128)(2,1)S(1)}, bf16[96,3072]{1,0:T(8,128)(2,1)S(1)}, u32[]{:S(2)}, u32[]{:S(2)}) %collective-permute-start.3) | collective-permute-done | bytes 589856 | tf_op jit(solution)/shard_map/rows_between_cores/ppermute | solution.py:401
  32.6 0.0 slice-done
  32.6 0.0 slice-done.1
  32.6 3.3 %experts.1 = (bf16[48,512]{1,0:T(8,128)(2,1)S(1)}, bf16[96,3072]{1,0:T(8,128)(2,1)S(1)}) custom-call(bf16[96,3072]{1,0:T(8,128)(2,1)S(1)} %join.1.mine, bf16[96,3072]{1,0:T(8,128)(2,1)S(1)} %collective-permute-done.3.other, bf16[6144,512]{1,0:T(8,128)(2,1)S(1)} %bitcast.19, bf16[6144,512]{1,0:T(8,128)(2,1)S(1)} %get-tuple-element.18.w_up, ...), custom_call_target="tpu_custom_call" | custom-call | flops 1509949440 | bytes 18874368 | tf_op jit(solution)/shard_map/experts/experts/pallas_call | solution.py:432
  35.9 0.2 collective-permute-start.4
  36.2 1.2 %own_down.1 = f32[96,3072]{1,0:T(8,128)S(1)} custom-call(bf16[48,512]{1,0:T(8,128)(2,1)S(1)} %get-tuple-element.20.act, bf16[512,6144]{1,0:T(8,128)(2,1)S(1)} %get-tuple-element.19.w_down), custom_call_target="tpu_custom_call" | custom-call | flops 301989888 | bytes 6291456 | tf_op jit(solution)/shard_map/own_down/own_down/pallas_call | solution.py:447
  37.4 0.7 %collective-permute-done.4 = bf16[96,3072]{1,0:T(8,128)(2,1)S(1)} collective-permute-done((bf16[96,3072]{1,0:T(8,128)(2,1)S(1)}, bf16[96,3072]{1,0:T(8,128)(2,1)S(1)}, u32[]{:S(2)}, u32[]{:S(2)}) %collective-permute-start.4) | collective-permute-done | bytes 589856 | tf_op jit(solution)/shard_map/sums_between_cores/ppermute | solution.py:401
  38.0 0.1 add_convert_fusion
  38.2 1.9 %collective-permute-start.7 = (bf16[24,3072]{1,0:T(8,128)(2,1)S(1)}, bf16[24,3072]{1,0:T(8,128)(2,1)S(1)}, u32[]{:S(2)}, u32[]{:S(2)}) collective-permute-start(bf16[24,3072]{1,0:T(8,128)(2,1)S(1)} %get-tuple-element.23), channel_id=1, source_target_pairs={{0,32},{32,64},{64,96},{96,0},{1,33},{33,65},{65,97},{97,1},{2,34}... | collective-permute-start | bytes 442376 | tf_op jit(solution)/shard_map/sums_along_x/ppermute | solution.py:398
  40.1 0.2 collective-permute-start.6
  40.3 1.8 %collective-permute-start.5 = (bf16[24,3072]{1,0:T(8,128)(2,1)S(1)}, bf16[24,3072]{1,0:T(8,128)(2,1)S(1)}, u32[]{:S(2)}, u32[]{:S(2)}) collective-permute-start(bf16[24,3072]{1,0:T(8,128)(2,1)S(1)} %get-tuple-element.25), channel_id=1, source_target_pairs={{0,64},{32,96},{64,0},{96,32},{1,65},{33,97},{65,1},{97,33},{2,66}... | collective-permute-start | bytes 442376 | tf_op jit(solution)/shard_map/sums_along_x/ppermute | solution.py:398
  42.2 2.0 %collective-permute-done.7.third = bf16[24,3072]{1,0:T(8,128)(2,1)S(1)} collective-permute-done((bf16[24,3072]{1,0:T(8,128)(2,1)S(1)}, bf16[24,3072]{1,0:T(8,128)(2,1)S(1)}, u32[]{:S(2)}, u32[]{:S(2)}) %collective-permute-start.7) | collective-permute-done | bytes 147488 | tf_op jit(solution)/shard_map/sums_along_x/ppermute | solution.py:398
  44.2 5.9 %collective-permute-done.6.second = bf16[24,3072]{1,0:T(8,128)(2,1)S(1)} collective-permute-done((bf16[24,3072]{1,0:T(8,128)(2,1)S(1)}, bf16[24,3072]{1,0:T(8,128)(2,1)S(1)}, u32[]{:S(2)}, u32[]{:S(2)}) %collective-permute-start.6) | collective-permute-done | bytes 147488 | tf_op jit(solution)/shard_map/sums_along_x/ppermute | solution.py:398
  50.1 0.0 collective-permute-done.5.first
  50.1 0.3 spread.1
  50.4 12.8 %all_to_all.11.received = bf16[16,8,1536]{2,1,0:T(8,128)(2,1)S(1)} all-to-all(bf16[16,8,1536]{2,1,0:T(8,128)(2,1)S(1)} %bitcast.21), channel_id=1, replica_groups=mesh['x'=4,'core'=2,'ep'=16] {'ep'}, dimensions={0} | all-to-all | bytes 786432 | tf_op jit(solution)/shard_map/sums_to_rows/all_to_all | solution.py:471
  63.2 0.8 %combine.1 = bf16[2,6144]{1,0:T(2,128)(2,1)} custom-call(bf16[16,8,1536]{2,1,0:T(8,128)(2,1)S(1)} %all_to_all.11.received, bf16[8,1536]{1,0:T(8,128)(2,1)S(1)} %get-tuple-element.22.stream, f32[8,128]{1,0:T(8,128)S(1)} %get-tuple-element.16.ready.gates), custom_call_target="tpu_custom_call" | custom-call | tf_op jit(solution)/shard_map/combine/combine/pallas_call | solution.py:475
  (3 shorter events, 0.1 us)
Async XLA Ops:
  0.0 25.2 %copy-start = (bf16[6144,8]{0,1:T(8,128)(2,1)S(1)}, bf16[6144,8]{0,1:T(8,128)(2,1)}, u32[]{:S(2)}) copy-start(bf16[6144,8]{0,1:T(8,128)(2,1)} %param.22) | copy-start | bytes 294916
  21.7 8.4 %collective-permute-start.2 = (bf16[24,3072]{1,0:T(8,128)(2,1)S(1)}, bf16[24,3072]{1,0:T(8,128)(2,1)S(1)}, u32[]{:S(2)}, u32[]{:S(2)}) collective-permute-start(bf16[24,3072]{1,0:T(8,128)(2,1)S(1)} %get-tuple-element.17.refs_0_), channel_id=1, source_target_pairs={{0,32},{32,64},{64,96},{96,0},{1,33},{33,65},{65,97},{97,1},{2,34}... | collective-permute-start | bytes 442376 | tf_op jit(solution)/shard_map/rows_along_x/ppermute | solution.py:398
  22.3 7.9 %collective-permute-start.1 = (bf16[24,3072]{1,0:T(8,128)(2,1)S(1)}, bf16[24,3072]{1,0:T(8,128)(2,1)S(1)}, u32[]{:S(2)}, u32[]{:S(2)}) collective-permute-start(bf16[24,3072]{1,0:T(8,128)(2,1)S(1)} %get-tuple-element.17.refs_0_), channel_id=1, source_target_pairs={{0,96},{32,0},{64,32},{96,64},{1,97},{33,1},{65,33},{97,65},{2,98}... | collective-permute-start | bytes 442376 | tf_op jit(solution)/shard_map/rows_along_x/ppermute | solution.py:398
  23.8 6.6 %collective-permute-start = (bf16[24,3072]{1,0:T(8,128)(2,1)S(1)}, bf16[24,3072]{1,0:T(8,128)(2,1)S(1)}, u32[]{:S(2)}, u32[]{:S(2)}) collective-permute-start(bf16[24,3072]{1,0:T(8,128)(2,1)S(1)} %get-tuple-element.17.refs_0_), channel_id=1, source_target_pairs={{0,64},{32,96},{64,0},{96,32},{1,65},{33,97},{65,1},{97,33},{2,66}... | collective-permute-start | bytes 442376 | tf_op jit(solution)/shard_map/rows_along_x/ppermute | solution.py:398
  25.2 7.4 %slice-start = ((s8[6291456]{0:T(1024)(128)(4,1)}), s8[4194304]{0:T(1024)(128)(4,1)S(1)}, s32[]{:S(2)}) async-start(s8[6291456]{0:T(1024)(128)(4,1)} %bitcast.17), calls=%async_computation.2 | async-start | bytes 8388608
  25.2 7.4 %slice-start.1 = ((s8[6291456]{0:T(1024)(128)(4,1)}), s8[2097152]{0:T(1024)(128)(4,1)S(1)}, s32[]{:S(2)}) async-start(s8[6291456]{0:T(1024)(128)(4,1)} %bitcast.17), calls=%async_computation.3 | async-start | bytes 4194304
  30.5 2.1 %collective-permute-start.3 = (bf16[96,3072]{1,0:T(8,128)(2,1)S(1)}, bf16[96,3072]{1,0:T(8,128)(2,1)S(1)}, u32[]{:S(2)}, u32[]{:S(2)}) collective-permute-start(bf16[96,3072]{1,0:T(8,128)(2,1)S(1)} %join.1.mine), channel_id=1, source_target_pairs={{0,16},{16,0},{1,17},{17,1},{2,18},{18,2},{3,19},{19,3},{4,20},{20... | collective-permute-start | bytes 1769480 | tf_op jit(solution)/shard_map/rows_between_cores/ppermute | solution.py:401
  35.9 2.1 %collective-permute-start.4 = (bf16[96,3072]{1,0:T(8,128)(2,1)S(1)}, bf16[96,3072]{1,0:T(8,128)(2,1)S(1)}, u32[]{:S(2)}, u32[]{:S(2)}) collective-permute-start(bf16[96,3072]{1,0:T(8,128)(2,1)S(1)} %get-tuple-element.21), channel_id=1, source_target_pairs={{0,16},{16,0},{1,17},{17,1},{2,18},{18,2},{3,19},{19,3},{4,20},{20... | collective-permute-start | bytes 1769480 | tf_op jit(solution)/shard_map/sums_between_cores/ppermute | solution.py:401
  38.2 6.0 %collective-permute-start.7 = (bf16[24,3072]{1,0:T(8,128)(2,1)S(1)}, bf16[24,3072]{1,0:T(8,128)(2,1)S(1)}, u32[]{:S(2)}, u32[]{:S(2)}) collective-permute-start(bf16[24,3072]{1,0:T(8,128)(2,1)S(1)} %get-tuple-element.23), channel_id=1, source_target_pairs={{0,32},{32,64},{64,96},{96,0},{1,33},{33,65},{65,97},{97,1},{2,34}... | collective-permute-start | bytes 442376 | tf_op jit(solution)/shard_map/sums_along_x/ppermute | solution.py:398
  40.1 10.0 %collective-permute-start.6 = (bf16[24,3072]{1,0:T(8,128)(2,1)S(1)}, bf16[24,3072]{1,0:T(8,128)(2,1)S(1)}, u32[]{:S(2)}, u32[]{:S(2)}) collective-permute-start(bf16[24,3072]{1,0:T(8,128)(2,1)S(1)} %get-tuple-element.24), channel_id=1, source_target_pairs={{0,96},{32,0},{64,32},{96,64},{1,97},{33,1},{65,33},{97,65},{2,98}... | collective-permute-start | bytes 442376 | tf_op jit(solution)/shard_map/sums_along_x/ppermute | solution.py:398
  40.3 9.8 %collective-permute-start.5 = (bf16[24,3072]{1,0:T(8,128)(2,1)S(1)}, bf16[24,3072]{1,0:T(8,128)(2,1)S(1)}, u32[]{:S(2)}, u32[]{:S(2)}) collective-permute-start(bf16[24,3072]{1,0:T(8,128)(2,1)S(1)} %get-tuple-element.25), channel_id=1, source_target_pairs={{0,64},{32,96},{64,0},{96,32},{1,65},{33,97},{65,1},{97,33},{2,66}... | collective-permute-start | bytes 442376 | tf_op jit(solution)/shard_map/sums_along_x/ppermute | solution.py:398
